TPU v7x, 32 devices: a whole 2x2x4 slice. The times are simulated.
32 devices in a mesh: seq: 8 (over z, x), tp: 4 (over y, core).
Axes of the slice: x: 2, y: 2, z: 4, core: 2. Of those that a mesh axis runs over, the one named last changes fastest.
Arguments:
- queries: bfloat16 [2048, 4096], P('seq', 'tp'), may hold values from -6 to 6
- keys: bfloat16 [2048, 4096], P('seq', 'tp'), may hold values from -6 to 6
- values: bfloat16 [2048, 4096], P('seq', 'tp'), may hold values from -12 to 12
- seeds: bfloat16 [32, 256], P('tp'), may hold values from -6 to 6
- gain: float32 [4096], P('tp'), may hold values from 0.1 to 1.9
Outputs:
- attended: bfloat16 [2048, 4096], P('seq', 'tp')
All inputs are finite; a program needn't handle non-finite values.
Results may differ from a plain program's by a relative error of at most 0.009.
Values sent between devices are 32-bit elements; how exact they have to be, the bound alone decides.
No kernel may reach another device: no remote copies, remote signals or barrier semaphores. Data moves between devices by JAX's collectives and lax.ppermute only.
A program may use at most 192 MiB of HBM per device.

v0:
```python
import jax
import jax.numpy as jnp
from jax import lax
from jax.sharding import PartitionSpec as P


def prefix(value, axis, join, neutral):
    count, mine = (lax.axis_size(axis), lax.axis_index(axis))
    pieces = jax.tree.map(lambda part: lax.all_gather(part, axis), value)
    subtotal = jax.tree.map(
        lambda part, zero: jnp.full_like(part, 0) + jnp.asarray(zero, part.dtype), value, neutral
    )

    def step(position, subtotal):
        longer = join(subtotal, jax.tree.map(lambda part: part[position], pieces))
        return jax.tree.map(lambda new, old: jnp.where(position < mine, new, old), longer, subtotal)

    return lax.fori_loop(0, count - 1, step, subtotal)


def circulant_table(seeds, width):
    heads_here = seeds.shape[0]
    total = seeds.shape[1]
    groups = total // width
    blocks = seeds.reshape(heads_here, groups, width)
    repeated = jnp.tile(blocks, (1, 1, 2 * width - 1))
    square = repeated.reshape(heads_here, groups, width, 2 * width - 1)[:, :, :, :width]
    return jnp.transpose(square, (0, 2, 1, 3)).reshape(heads_here, width, total)


def feature_map(rows, table, heads_here, width):
    count = rows.shape[0]
    x = rows.reshape(count, heads_here, width)
    mixed = jnp.einsum("thj,hjm->thm", x, table, preferred_element_type=jnp.float32) * width ** (
        -0.25
    )
    return (jax.nn.elu(mixed) + 1.0).astype(jnp.bfloat16)


def add_pair(earlier, later):
    return (earlier[0] + later[0], earlier[1] + later[1])


def per_device(queries, keys, values, seeds, gain):
    high = lax.Precision.HIGHEST
    tok = queries.shape[0]
    heads_here = seeds.shape[0]
    feats = seeds.shape[1]
    width = queries.shape[1] // heads_here
    block = min(512, tok)
    count = tok // block
    table = circulant_table(seeds, width)
    causal = jnp.tril(jnp.ones((block, block), dtype=bool))

    def advance(carry, inputs):
        state, totals = carry
        q_rows, k_rows, v_rows = inputs
        fq = feature_map(q_rows, table, heads_here, width)
        fk = feature_map(k_rows, table, heads_here, width)
        vals = v_rows.reshape(block, heads_here, width)
        scores = jnp.einsum("bhm,chm->hbc", fq, fk, preferred_element_type=jnp.float32)
        scores = jnp.where(causal[None], scores, 0.0)
        wscores = scores.astype(jnp.bfloat16)
        num = jnp.einsum("hbc,che->bhe", wscores, vals, preferred_element_type=jnp.float32)
        fq_wide = fq.astype(jnp.float32)
        num = num + jnp.einsum("bhm,hme->bhe", fq_wide, state, precision=high)
        den = jnp.sum(scores, axis=2).T + jnp.einsum("bhm,hm->bh", fq_wide, totals, precision=high)
        state = state + jnp.einsum("chm,che->hme", fk, vals, preferred_element_type=jnp.float32)
        totals = totals + jnp.sum(fk.astype(jnp.float32), axis=0)
        return ((state, totals), (num, den, fq))

    start = (
        jnp.zeros((heads_here, feats, width), jnp.float32),
        jnp.zeros((heads_here, feats), jnp.float32),
    )
    (local_state, local_totals), (num, den, fq) = lax.scan(
        advance,
        start,
        (
            queries.reshape(count, block, -1),
            keys.reshape(count, block, -1),
            values.reshape(count, block, -1),
        ),
    )
    num = num.reshape(tok, heads_here, width)
    den = den.reshape(tok, heads_here)
    fq = fq.reshape(tok, heads_here, feats)
    prior_state, prior_totals = prefix(
        (local_state, local_totals),
        "seq",
        add_pair,
        (jnp.zeros_like(local_state), jnp.zeros_like(local_totals)),
    )
    fq_wide = fq.astype(jnp.float32)
    num = num + jnp.einsum("thm,hme->the", fq_wide, prior_state, precision=high)
    den = den + jnp.einsum("thm,hm->th", fq_wide, prior_totals, precision=high)
    heads = num / den[:, :, None]
    squares = jnp.sum(heads * heads, axis=(1, 2))
    overall = lax.psum(squares, "tp")
    entries = heads_here * width * lax.axis_size("tp")
    factor = lax.rsqrt(overall / entries + 1e-06)
    normed = heads.reshape(tok, heads_here * width) * factor[:, None] * gain[None, :]
    return normed.astype(jnp.bfloat16)


def solution(mesh):
    placed = (P("seq", "tp"), P("seq", "tp"), P("seq", "tp"), P("tp", None), P("tp"))
    return jax.shard_map(
        per_device, mesh=mesh, in_specs=placed, out_specs=P("seq", "tp"), check_vma=False
    )
```

profile of v0, /device:TPU:0, one launch (start us, length us, event | category | flops | bytes accessed | tf_op | source)
XLA Modules:
  0.0 172.9 jit_solution(12537090255754344960)
XLA Ops:
  6.5 0.0 copy-start
  6.5 0.0 all-gather.4.cloned.1.call-start
  6.5 0.7 copy.25
  7.3 0.1 tile.10
  7.4 3.2 %tile.11 = bf16[8,2,128,255]{3,2,1,0:T(8,128)(2,1)S(1)} reshape(bf16[8,2,255,128]{3,2,1,0:T(8,128)(2,1)S(1)} %tile.10) | data formatting | bytes 2088960 | tf_op jit(solution)/shard_map/tile | solution.py:26
  10.6 0.0 copy-done
  10.7 0.0 copy-start.4
  10.7 0.0 copy-start.1
  10.7 1.3 convert_reduce_fusion
  12.0 0.1 copy-done.1
  12.1 1.5 fusion.18
  13.6 0.0 all-gather.4.cloned.1.call-update
  13.7 32.7 %all-gather.1 = f32[64,256]{1,0:T(8,128)S(1)} all-gather(f32[8,256]{1,0:T(8,128)S(1)} %get-tuple-element.183), channel_id=3, replica_groups=mesh['seq'=8,'tp'=4] {'seq'}, dimensions={0}, use_global_device_ids=true | all-gather | bytes 73728 | tf_op jit(solution)/shard_map/all_gather | solution.py:9
  46.5 2.5 %fusion.2 = bf16[256,8,256]{2,0,1:T(8,128)(2,1)S(1)} fusion(bf16[256,1024]{1,0:T(8,128)(2,1)} %param.7, bf16[8,2,128,255]{3,2,1,0:T(8,128)(2,1)} %copy-done.4), kind=kOutput, calls=%fused_computation.8 | convolution fusion | flops 137363456 | bytes 2097152 | tf_op jit(solution)/shard_map/while/body/eval_jaxpr/thj,hjm->thm/dot_general | solution.py:34
  48.9 0.9 fusion.28
  49.8 0.5 select_reduce_fusion
  50.3 0.4 convolution_bitcast_fusion.2
  50.7 2.1 %fusion.8 = f32[256,8,128]{0,2,1:T(8,128)} fusion(f32[256,8,128]{0,2,1:T(8,128)S(1)} %convolution_bitcast_fusion.2, bf16[256,8,256]{2,0,1:T(8,128)(2,1)S(1)} %fusion.2), kind=kOutput, calls=%fused_computation.19 | convolution fusion | flops 805568512 | bytes 3145728 | tf_op jit(solution)/shard_map/while/body/eval_jaxpr/bhm,hme->bhe/dot_general | solution.py:66
  52.8 89.0 %all-gather.4.cloned.1.call-done = f32[64,256,128]{2,1,0:T(8,128)} async-done(((f32[8,256,128]{2,1,0:T(8,128)}), f32[64,256,128]{2,1,0:T(8,128)}) %all-gather.4.cloned.1.call-update) | async-done | bytes 8388624 | tf_op jit(solution)/shard_map/all_gather | solution.py:9
  141.8 11.4 %while.10 = (s32[]{:T(128)}, f32[8,256,128]{2,1,0:T(8,128)S(1)}, f32[8,256]{1,0:T(8,128)S(1)}, s32[]{:T(128)}, f32[8,8,256,128]{3,2,1,0:T(8,128)}, /*index=5*/f32[8,8,256]{2,1,0:T(8,128)S(1)}, s32[]{:T(128)}, s32[]{:T(128)}) while((s32[]{:T(128)}, f32[8,256,128]{2,1,0:T(8,128)S(1)}, f32[8,256]{1,0:T(8,128)S(1)}, s32[]{:T(128)}, ...), condition=%wide.region_2.3_spmd.clone, body=%wide.region_1.2_spmd.clone.sunk | while | flops 792580 | bytes 3170419 | solution.py:18
  141.8 1.6 add_select_fusion.4
  143.5 1.6 add_select_fusion.4
  145.1 1.6 add_select_fusion.4
  146.7 1.6 add_select_fusion.4
  148.4 1.6 add_select_fusion.4
  150.0 1.6 add_select_fusion.4
  151.6 1.6 add_select_fusion.4
  153.2 0.9 fusion.26
  154.2 3.2 %multiply_reduce_fusion = (f32[256]{0:T(256)S(1)}, f32[256,8,128]{0,2,1:T(8,128)}) fusion(f32[256,8]{0,1:T(8,128)S(1)} %fusion.25, f32[256,8,128]{0,2,1:T(8,128)} %fusion.8, f32[8,256,128]{2,1,0:T(8,128)S(1)} %get-tuple-element.148, bf16[256,8,256]{2,0,1:T(8,128)(2,1)S(1)} %fusion.2), kind=kOutput, calls=%fused_computation.22 | convolution fusion | flops 806354688 | bytes 4203520 | tf_op jit(solution)/shard_map/thm,hme->the/dot_general | solution.py:95
  157.4 1.6 copy.34
  158.9 6.2 %psum.7 = f32[256]{0:T(256)S(1)} all-reduce(f32[256]{0:T(256)S(1)} %get-tuple-element.187), channel_id=1, replica_groups=mesh['seq'=8,'tp'=4] {'tp'}, use_global_device_ids=true, to_apply=%region_5.6 | all-reduce | flops 256 | bytes 2048 | tf_op jit(solution)/shard_map/psum | solution.py:99
  165.1 1.0 multiply_convert_fusion
  (19 shorter events, 0.1 us)
Async XLA Ops:
  6.5 4.1 %copy-start = (bf16[256,1024]{1,0:T(8,128)(2,1)S(1)}, bf16[256,1024]{1,0:T(8,128)(2,1)}, u32[]{:S(2)}) copy-start(bf16[256,1024]{1,0:T(8,128)(2,1)} %param.8) | copy-start | bytes 1572868
  6.5 135.3 %all-gather.4.cloned.1.call-start = ((), (), s32[]{:S(2)}) async-start(), calls=%async_computation | async-start | bytes 9437184 | tf_op jit(solution)/shard_map/all_gather | solution.py:9
  10.7 1.3 copy-start.4
  10.7 1.4 copy-start.1
  12.0 1.7 copy-start.2
  46.4 3.4 %copy-start.3 = (bf16[256,8,256]{2,0,1:T(8,128)(2,1)S(1)}, bf16[256,8,256]{2,0,1:T(8,128)(2,1)}, u32[]{:S(2)}) copy-start(bf16[256,8,256]{2,0,1:T(8,128)(2,1)} %copy-done.2) | copy-start | bytes 3145732
  157.4 7.8 %copy-start.5 = (f32[1024]{0:T(1024)S(1)}, f32[1024]{0:T(1024)}, u32[]{:S(2)}) copy-start(f32[1024]{0:T(1024)} %param.11) | copy-start | bytes 12292
Sparse Core Ops, SparseCore 0:
  13.8 128.0 all-gather.3
where the time goes:
time: 173 us
  waiting for transfers between devices  89 us (51%)
  blocking collectives  38.9 us (22%)
  between operations  13.5 us (8%)
  matrix products  13.3 us (8%)
  other arithmetic  12.2 us (7%)
  local copies, waits for them, and re-layouts  5.81 us (3%)
    all_gather x1, waiting for transfers between devices, prefix(): pieces = jax.tree.map(lambda part: lax.all_gather(part, axis), value)  89 us
    all_gather x1, blocking collectives, prefix(): pieces = jax.tree.map(lambda part: lax.all_gather(part, axis), value)  32.7 us
    select_n x14, other arithmetic, step(): jnp.where(position < mine, new, old)  11.2 us
    psum x1, blocking collectives, per_device(): overall = lax.psum(squares, 'tp')  6.17 us
    another operation x3, local copies, waits for them, and re-layouts, circulant_table(): repeated = jnp.tile(blocks, (1, 1, 2 * width - 1))  4.1 us
    dot_general x2, matrix products, feature_map(): jnp.einsum('thj,hjm->thm', x, table, preferred_element_type=jnp.float32)  3.71 us
  transfers between devices with their start and end apart: 1, of which 1 were waited for; matrix products, arithmetic and copies ran while one was open for 4% of the time, Pallas kernels for 0%

commit v1 on v0

v1 whole, which is shorter than its diff:
```python
import functools

import jax
import jax.numpy as jnp
from jax import lax
from jax.experimental import pallas as pl
from jax.experimental.pallas import tpu as pltpu
from jax.sharding import PartitionSpec as P

WIDTH = 128
NT = (((1,), (1,)), ((), ()))
TN = (((0,), (0,)), ((), ()))
VMEM = pl.BlockSpec(memory_space=pltpu.VMEM)
SMEM = pl.BlockSpec(memory_space=pltpu.SMEM)
PARAMS = pltpu.CompilerParams(vmem_limit_bytes=24 * 2**20)


def rotated(seeds_ref, first):
    heads = seeds_ref.shape[0]
    seeds = seeds_ref[...].astype(jnp.float32)
    return pltpu.roll(seeds, lax.rem(heads - first, heads), 0)


def table_of(seeds, i, group):
    row = seeds[i : i + 1, group * WIDTH : (group + 1) * WIDTH]
    square = jnp.broadcast_to(row, (WIDTH, WIDTH))
    return pltpu.roll(square, 0, 1, stride=1, stride_axis=0).astype(jnp.bfloat16)


def phi(x, table):
    mixed = jnp.dot(x, table, preferred_element_type=jnp.float32) * WIDTH ** (-0.25)
    return (jnp.exp(jnp.minimum(mixed, 0.0)) + jnp.maximum(mixed, 0.0)).astype(jnp.bfloat16)


def features(x, seeds, i):
    groups = seeds.shape[1] // WIDTH
    return jnp.concatenate([phi(x, table_of(seeds, i, g)) for g in range(groups)], axis=1)


def columns(head):
    return pl.ds(pl.multiple_of(head * WIDTH, WIDTH), WIDTH)


def state_kernel(half, first_ref, seeds_ref, k_ref, v_ref, *outs):
    first = first_ref[0]
    seeds = rotated(seeds_ref, first)
    for i in range(half):
        head = first + i
        fk = features(k_ref[:, columns(head)], seeds, i)
        vals = v_ref[:, columns(head)]
        outs[i][0:WIDTH, :] = lax.dot_general(vals, fk, TN, preferred_element_type=jnp.float32)
        outs[0][WIDTH + i : WIDTH + i + 1, :] = jnp.sum(
            fk.astype(jnp.float32), axis=0, keepdims=True
        )


def local_kernel(first_ref, seeds_ref, q_ref, k_ref, v_ref, num_ref, den_ref, fq_ref):
    seeds = rotated(seeds_ref, first_ref[0])
    heads = seeds_ref.shape[0]
    feats = seeds_ref.shape[1]
    tok = q_ref.shape[0]
    rows = lax.broadcasted_iota(jnp.int32, (tok, tok), 0)
    causal = lax.broadcasted_iota(jnp.int32, (tok, tok), 1) <= rows
    for i in range(heads):
        head = lax.rem(first_ref[0] + i, heads)
        fk = features(k_ref[:, columns(head)], seeds, i)
        fq = features(q_ref[:, columns(head)], seeds, i)
        fq_ref[:, i * feats : (i + 1) * feats] = fq
        scores = lax.dot_general(fq, fk, NT, preferred_element_type=jnp.float32)
        scores = jnp.where(causal, scores, 0.0)
        num_ref[:, i * WIDTH : (i + 1) * WIDTH] = jnp.dot(
            scores.astype(jnp.bfloat16),
            v_ref[:, columns(head)],
            preferred_element_type=jnp.float32,
        )
        den_ref[:, i * WIDTH : (i + 1) * WIDTH] = jnp.broadcast_to(
            jnp.sum(scores, axis=1, keepdims=True), (tok, WIDTH)
        )


def join_kernel(half, offset, fq_ref, num_ref, den_ref, *refs):
    states, (heads_ref, squares_ref) = refs[:half], refs[half:]
    feats = states[0].shape[1]
    tok = fq_ref.shape[0]
    squares = jnp.zeros((tok, WIDTH), jnp.float32)
    for i in range(half):
        at = offset + i
        total = states[0][WIDTH + i : WIDTH + i + 1, :]
        wide = jnp.concatenate(
            [states[i][0:WIDTH, :], jnp.broadcast_to(total, (WIDTH, feats))], axis=0
        )
        upper = wide.astype(jnp.bfloat16)
        lower = (wide - upper.astype(jnp.float32)).astype(jnp.bfloat16)
        fq = fq_ref[:, at * feats : (at + 1) * feats]
        both = lax.dot_general(fq, upper, NT, preferred_element_type=jnp.float32)
        both = both + lax.dot_general(fq, lower, NT, preferred_element_type=jnp.float32)
        num = num_ref[:, at * WIDTH : (at + 1) * WIDTH] + both[:, :WIDTH]
        den = den_ref[:, at * WIDTH : (at + 1) * WIDTH] + both[:, WIDTH:]
        head = num / den
        heads_ref[:, i * WIDTH : (i + 1) * WIDTH] = head
        squares = squares + head * head
    rows = jnp.broadcast_to(jnp.sum(squares, axis=1, keepdims=True), (tok, WIDTH))
    squares_ref[...] = rows.T[0:8, :]


def norm_kernel(half, entries, first_ref, gain_ref, own_ref, other_ref, *refs):
    squares, out_ref = refs[:-1], refs[-1]
    tok = own_ref.shape[0]
    overall = functools.reduce(lambda a, b: a + b, [ref[...] for ref in squares])
    factor = lax.rsqrt(overall / entries + 1e-06)
    wide = jnp.broadcast_to(factor[0:1, :], (WIDTH, tok)).T
    for part, source in enumerate((own_ref, other_ref)):
        for i in range(half):
            head = lax.rem(first_ref[0] + part * half + i, 2 * half)
            at = columns(head)
            out_ref[:, at] = (
                source[:, i * WIDTH : (i + 1) * WIDTH] * wide * gain_ref[:, at]
            ).astype(jnp.bfloat16)


def call(kernel, outs, ins, scalars, flops):
    moved = sum(x.size * x.dtype.itemsize for x in ins)
    moved += sum(x.size * jnp.dtype(x.dtype).itemsize for x in jax.tree.leaves(outs))
    return pl.pallas_call(
        kernel,
        out_shape=outs,
        in_specs=[SMEM] * scalars + [VMEM] * (len(ins) - scalars),
        out_specs=jax.tree.map(lambda _: VMEM, outs),
        compiler_params=PARAMS,
        cost_estimate=pl.CostEstimate(flops=flops, bytes_accessed=moved, transcendentals=0),
    )(*ins)


def per_device(queries, keys, values, seeds, gain):
    f32 = jnp.float32
    tok = queries.shape[0]
    heads, feats = seeds.shape
    half = heads // 2
    count = lax.axis_size("seq")
    pairs = count // 2
    mine = lax.axis_index("seq")
    side = lax.rem(mine, 2)
    own_first = (side * half).reshape(1)
    other_first = ((1 - side) * half).reshape(1)
    shape = lambda *dims, dtype=f32: jax.ShapeDtypeStruct(dims, dtype)

    state_shapes = [shape(WIDTH + (8 if i == 0 else 0), feats) for i in range(half)]
    states = lambda first: call(
        functools.partial(state_kernel, half),
        state_shapes,
        (first, seeds, keys, values),
        1,
        half * tok * feats * WIDTH * 4,
    )
    theirs = states(other_first)
    ours = states(own_first)

    swap = [(i, i ^ 1) for i in range(count)]
    hops = [[(2 * p, 2 * p + 2), (2 * p + 1, 2 * p + 3)] for p in range(pairs - 1)]
    incoming = [lax.ppermute(part, "seq", swap) for part in theirs]
    totals = [a + b for a, b in zip(ours, incoming)]
    num, den, fq = call(
        local_kernel,
        [shape(tok, heads * WIDTH), shape(tok, heads * WIDTH), shape(tok, heads * feats, dtype=jnp.bfloat16)],
        (own_first, seeds, queries, keys, values),
        1,
        heads * tok * (feats * WIDTH * 4 + tok * (feats + WIDTH) * 2),
    )
    own_prior, passed = [], []
    for i in range(half):
        prior = jnp.zeros_like(totals[i])
        arrived = prior
        for hop in hops:
            arrived = lax.ppermute(arrived + totals[i], "seq", hop)
            prior = prior + arrived
        passed.append(lax.ppermute(prior + jnp.where(side == 0, ours[i], 0.0), "seq", swap))
        own_prior.append(prior + jnp.where(side == 0, 0.0, incoming[i]))
    join = lambda offset, prior: call(
        functools.partial(join_kernel, half, offset),
        [shape(tok, half * WIDTH), shape(8, tok)],
        (fq, num, den, *prior),
        0,
        half * tok * feats * WIDTH * 8,
    )
    own_heads, own_squares = join(0, own_prior)
    other_heads, other_squares = join(half, passed)
    squares = own_squares + other_squares
    across = lax.axis_size("tp")
    gathered = [squares] + [
        lax.ppermute(squares, "tp", [(i, (i + k) % across) for i in range(across)])
        for k in range(1, across)
    ]
    return call(
        functools.partial(norm_kernel, half, heads * WIDTH * across),
        shape(tok, heads * WIDTH, dtype=jnp.bfloat16),
        (own_first, gain.reshape(1, -1), own_heads, other_heads, *gathered),
        1,
        tok * heads * WIDTH * 3,
    )


def solution(mesh):
    placed = (P("seq", "tp"), P("seq", "tp"), P("seq", "tp"), P("tp", None), P("tp"))
    return jax.shard_map(
        per_device, mesh=mesh, in_specs=placed, out_specs=P("seq", "tp"), check_vma=False
    )
```

time: 173 us -> 59 us (0.34)
  the two profiles are of different devices: /device:TPU:0 before, /device:TPU:16 now
where the time goes in v1:
time: 59 us; the launch traced here: 58.5 us
  starting transfers between devices  23.9 us (41%)
  waiting for transfers between devices  18 us (31%)
  Pallas kernels  7.82 us (13%)
  other arithmetic  5.76 us (10%)
  local copies, waits for them, and re-layouts  2.78 us (5%)
    ppermute x12, starting transfers between devices, per_device(): arrived = lax.ppermute(arrived + totals[i], 'seq', hop)  13.6 us
    pallas_call x6, Pallas kernels, call(): pl.pallas_call(kernel, out_shape=outs, in_specs=[SMEM] * scalars + [VMEM]...  7.82 us
    ppermute x4, waiting for transfers between devices, per_device(): incoming = [lax.ppermute(part, 'seq', swap) for part in theirs]  7.27 us
    ppermute x12, waiting for transfers between devices, per_device(): arrived = lax.ppermute(arrived + totals[i], 'seq', hop)  4.44 us
    ppermute x4, starting transfers between devices, per_device(): lax.ppermute(prior + jnp.where(side == 0, ours[i], 0.0), 'seq', swap)  4.33 us
    ppermute x4, starting transfers between devices, per_device(): incoming = [lax.ppermute(part, 'seq', swap) for part in theirs]  4.12 us
    add x8, other arithmetic, per_device(): arrived = lax.ppermute(arrived + totals[i], 'seq', hop)  3.67 us
    ppermute x4, waiting for transfers between devices, per_device(): lax.ppermute(prior + jnp.where(side == 0, ours[i], 0.0), 'seq', swap)  3.42 us
  transfers between devices with their start and end apart: 23, of which 9 were waited for; matrix products, arithmetic and copies ran while one was open for 10% of the time, Pallas kernels for 9%

profile of v1, /device:TPU:16, one launch (start us, length us, event | category | flops | bytes accessed | tf_op | source)
XLA Modules:
  0.0 58.5 jit_solution(15290117781160423757)
XLA Ops:
  0.0 0.7 %copy-done.4 = bf16[8,256]{1,0:T(8,128)(2,1)S(1)} copy-done((bf16[8,256]{1,0:T(8,128)(2,1)S(1)}, bf16[8,256]{1,0:T(8,128)(2,1)}, u32[]{:S(2)}) %copy-start.4) | copy-done | bytes 4120
  0.7 1.0 %copy-done = bf16[256,1024]{1,0:T(8,128)(2,1)S(1)} copy-done((bf16[256,1024]{1,0:T(8,128)(2,1)S(1)}, bf16[256,1024]{1,0:T(8,128)(2,1)}, u32[]{:S(2)}) %copy-start) | copy-done | bytes 524312
  1.7 1.0 %copy-done.2 = bf16[256,1024]{1,0:T(8,128)(2,1)S(1)} copy-done((bf16[256,1024]{1,0:T(8,128)(2,1)S(1)}, bf16[256,1024]{1,0:T(8,128)(2,1)}, u32[]{:S(2)}) %copy-start.2) | copy-done | bytes 524312
  2.8 1.1 %shard_map.57 = (f32[136,256]{1,0:T(8,128)S(1)}, f32[128,256]{1,0:T(8,128)S(1)}, f32[128,256]{1,0:T(8,128)S(1)}, f32[128,256]{1,0:T(8,128)S(1)}) custom-call(s32[1]{0:T(128)} %bitcast.2.first_ref, bf16[8,256]{1,0:T(8,128)(2,1)S(1)} %copy-done.4, bf16[256,1024]{1,0:T(8,128)(2,1)S(1)} %copy-done, bf16[256,1024]{1,0:T(8,128)(2,1)S(1)} %copy-done.2), custom_call_target="tpu_custom_call" | custom-call | flops 134217728 | bytes 1585156 | tf_op jit(solution)/shard_map/pallas_call | solution.py:124
  3.9 1.6 %collective-permute-start.12 = (f32[128,256]{1,0:T(8,128)S(1)}, f32[128,256]{1,0:T(8,128)S(1)}, u32[]{:S(2)}, u32[]{:S(2)}) collective-permute-start(f32[128,256]{1,0:T(8,128)S(1)} %get-tuple-element.30), channel_id=1, source_target_pairs={{0,4},{4,0},{8,12},{12,8},{16,20},{20,16},{24,28},{28,24},{1,5},{5... | collective-permute-start | bytes 393224 | tf_op jit(solution)/shard_map/ppermute | solution.py:160
  6.0 1.5 %collective-permute-start.4 = (f32[128,256]{1,0:T(8,128)S(1)}, f32[128,256]{1,0:T(8,128)S(1)}, u32[]{:S(2)}, u32[]{:S(2)}) collective-permute-start(f32[128,256]{1,0:T(8,128)S(1)} %get-tuple-element.26), channel_id=1, source_target_pairs={{0,4},{4,0},{8,12},{12,8},{16,20},{20,16},{24,28},{28,24},{1,5},{5... | collective-permute-start | bytes 393224 | tf_op jit(solution)/shard_map/ppermute | solution.py:160
  8.0 1.1 %shard_map.56 = (f32[136,256]{1,0:T(8,128)S(1)}, f32[128,256]{1,0:T(8,128)S(1)}, f32[128,256]{1,0:T(8,128)S(1)}, f32[128,256]{1,0:T(8,128)S(1)}) custom-call(s32[1]{0:T(128)} %bitcast.first_ref, bf16[8,256]{1,0:T(8,128)(2,1)S(1)} %copy-done.4, bf16[256,1024]{1,0:T(8,128)(2,1)S(1)} %copy-done.1, bf16[256,1024]{1,0:T(8,128)(2,1)S(1)} %copy-done.3), custom_call_target="tpu_custom_call" | custom-call | flops 134217728 | bytes 1585156 | tf_op jit(solution)/shard_map/pallas_call | solution.py:124
  9.1 1.2 %collective-permute-done.12 = f32[128,256]{1,0:T(8,128)S(1)} collective-permute-done((f32[128,256]{1,0:T(8,128)S(1)}, f32[128,256]{1,0:T(8,128)S(1)}, u32[]{:S(2)}, u32[]{:S(2)}) %collective-permute-start.12) | collective-permute-done | bytes 131104 | tf_op jit(solution)/shard_map/ppermute | solution.py:160
  11.0 2.3 %collective-permute-done = f32[136,256]{1,0:T(8,128)S(1)} collective-permute-done((f32[136,256]{1,0:T(8,128)S(1)}, f32[136,256]{1,0:T(8,128)S(1)}, u32[]{:S(2)}, u32[]{:S(2)}) %collective-permute-start) | collective-permute-done | bytes 139296 | tf_op jit(solution)/shard_map/ppermute | solution.py:160
  14.0 3.8 %collective-permute-done.8 = f32[128,256]{1,0:T(8,128)S(1)} collective-permute-done((f32[128,256]{1,0:T(8,128)S(1)}, f32[128,256]{1,0:T(8,128)S(1)}, u32[]{:S(2)}, u32[]{:S(2)}) %collective-permute-start.8) | collective-permute-done | bytes 131104 | tf_op jit(solution)/shard_map/ppermute | solution.py:160
  19.2 1.3 %collective-permute-start.14 = (f32[128,256]{1,0:T(8,128)S(1)}, f32[128,256]{1,0:T(8,128)S(1)}, u32[]{:S(2)}, u32[]{:S(2)}) collective-permute-start(f32[128,256]{1,0:T(8,128)S(1)} %add.106), channel_id=1, source_target_pairs={{8,16},{12,20},{9,17},{13,21},{10,18},{14,22},{11,19},{15,23}} | collective-permute-start | bytes 393224 | tf_op jit(solution)/shard_map/ppermute | solution.py:174
  20.5 0.7 %add.88 = f32[136,256]{1,0:T(8,128)} add(f32[136,256]{1,0:T(8,128)S(1)} %collective-permute-done.1, f32[136,256]{1,0:T(8,128)S(1)} %add.87) | non-fusion elementwise | flops 34816 | bytes 417792 | tf_op jit(solution)/shard_map/add | solution.py:174
  21.2 1.3 %collective-permute-start.2 = (f32[136,256]{1,0:T(8,128)}, f32[136,256]{1,0:T(8,128)S(1)}, u32[]{:S(2)}, u32[]{:S(2)}) collective-permute-start(f32[136,256]{1,0:T(8,128)} %add.88), channel_id=1, source_target_pairs={{8,16},{12,20},{9,17},{13,21},{10,18},{14,22},{11,19},{15,23}} | collective-permute-start | bytes 417800 | tf_op jit(solution)/shard_map/ppermute | solution.py:174
  23.2 1.3 %collective-permute-start.10 = (f32[128,256]{1,0:T(8,128)}, f32[128,256]{1,0:T(8,128)}, u32[]{:S(2)}, u32[]{:S(2)}) collective-permute-start(f32[128,256]{1,0:T(8,128)} %add.100), channel_id=1, source_target_pairs={{8,16},{12,20},{9,17},{13,21},{10,18},{14,22},{11,19},{15,23}} | collective-permute-start | bytes 393224 | tf_op jit(solution)/shard_map/ppermute | solution.py:174
  25.2 1.3 %collective-permute-start.6 = (f32[128,256]{1,0:T(8,128)}, f32[128,256]{1,0:T(8,128)S(1)}, u32[]{:S(2)}, u32[]{:S(2)}) collective-permute-start(f32[128,256]{1,0:T(8,128)} %add.94), channel_id=1, source_target_pairs={{8,16},{12,20},{9,17},{13,21},{10,18},{14,22},{11,19},{15,23}} | collective-permute-start | bytes 393224 | tf_op jit(solution)/shard_map/ppermute | solution.py:174
  26.4 0.9 %collective-permute-done.14 = f32[128,256]{1,0:T(8,128)S(1)} collective-permute-done((f32[128,256]{1,0:T(8,128)S(1)}, f32[128,256]{1,0:T(8,128)S(1)}, u32[]{:S(2)}, u32[]{:S(2)}) %collective-permute-start.14) | collective-permute-done | bytes 131104 | tf_op jit(solution)/shard_map/ppermute | solution.py:174
  28.0 1.9 %collective-permute-start.15 = (f32[128,256]{1,0:T(8,128)}, f32[128,256]{1,0:T(8,128)}, u32[]{:S(2)}, u32[]{:S(2)}) collective-permute-start(f32[128,256]{1,0:T(8,128)} %add.108), channel_id=1, source_target_pairs={{16,24},{20,28},{17,25},{21,29},{18,26},{22,30},{19,27},{23,31}} | collective-permute-start | bytes 393224 | tf_op jit(solution)/shard_map/ppermute | solution.py:174
  29.9 3.3 %collective-permute-done.10 = f32[128,256]{1,0:T(8,128)} collective-permute-done((f32[128,256]{1,0:T(8,128)}, f32[128,256]{1,0:T(8,128)}, u32[]{:S(2)}, u32[]{:S(2)}) %collective-permute-start.10) | collective-permute-done | bytes 131104 | tf_op jit(solution)/shard_map/ppermute | solution.py:174
  33.2 0.9 %add.102 = f32[128,256]{1,0:T(8,128)S(1)} add(f32[128,256]{1,0:T(8,128)} %collective-permute-done.10, f32[128,256]{1,0:T(8,128)S(1)} %add.99) | non-fusion elementwise | flops 32768 | bytes 393216 | tf_op jit(solution)/shard_map/add | solution.py:174
  34.1 1.3 %collective-permute-start.11 = (f32[128,256]{1,0:T(8,128)S(1)}, f32[128,256]{1,0:T(8,128)S(1)}, u32[]{:S(2)}, u32[]{:S(2)}) collective-permute-start(f32[128,256]{1,0:T(8,128)S(1)} %add.102), channel_id=1, source_target_pairs={{16,24},{20,28},{17,25},{21,29},{18,26},{22,30},{19,27},{23,31}} | collective-permute-start | bytes 393224 | tf_op jit(solution)/shard_map/ppermute | solution.py:174
  35.5 1.3 %collective-permute-start.7 = (f32[128,256]{1,0:T(8,128)S(1)}, f32[128,256]{1,0:T(8,128)S(1)}, u32[]{:S(2)}, u32[]{:S(2)}) collective-permute-start(f32[128,256]{1,0:T(8,128)S(1)} %add.96), channel_id=1, source_target_pairs={{16,24},{20,28},{17,25},{21,29},{18,26},{22,30},{19,27},{23,31}} | collective-permute-start | bytes 393224 | tf_op jit(solution)/shard_map/ppermute | solution.py:174
  36.8 1.3 %collective-permute-start.3 = (f32[136,256]{1,0:T(8,128)S(1)}, f32[136,256]{1,0:T(8,128)S(1)}, u32[]{:S(2)}, u32[]{:S(2)}) collective-permute-start(f32[136,256]{1,0:T(8,128)S(1)} %add.90), channel_id=1, source_target_pairs={{16,24},{20,28},{17,25},{21,29},{18,26},{22,30},{19,27},{23,31}} | collective-permute-start | bytes 417800 | tf_op jit(solution)/shard_map/ppermute | solution.py:174
  38.1 1.0 %select_add_fusion.2 = (f32[128,256]{1,0:T(8,128)S(1)}, f32[128,256]{1,0:T(8,128)S(1)}) fusion(f32[128,256]{1,0:T(8,128)S(1)} %get-tuple-element.29, pred[]{:T(512)S(6)} %eq.2, f32[128,256]{1,0:T(8,128)} %collective-permute-done.15, f32[128,256]{1,0:T(8,128)S(1)} %collective-permute-done.13, f32[128,256]{1,0:T(8,128)S(1)} %collective-permute-done.14, ...), kind=kLoop, calls=%fused_computation.3 | loop fusion | flops 196608 | bytes 917505 | tf_op jit(solution)/shard_map/add | solution.py:176
  39.1 1.6 %collective-permute-start.19 = (f32[128,256]{1,0:T(8,128)S(1)}, f32[128,256]{1,0:T(8,128)S(1)}, u32[]{:S(2)}, u32[]{:S(2)}) collective-permute-start(f32[128,256]{1,0:T(8,128)S(1)} %get-tuple-element.37), channel_id=1, source_target_pairs={{0,4},{4,0},{8,12},{12,8},{16,20},{20,16},{24,28},{28,24},{1,5},{5... | collective-permute-start | bytes 393224 | tf_op jit(solution)/shard_map/ppermute | solution.py:176
  40.7 1.0 %select_add_fusion.3 = (f32[128,256]{1,0:T(8,128)S(1)}, f32[128,256]{1,0:T(8,128)S(1)}) fusion(f32[128,256]{1,0:T(8,128)S(1)} %get-tuple-element.27, pred[]{:T(512)S(6)} %eq.2, f32[128,256]{1,0:T(8,128)S(1)} %collective-permute-done.11, f32[128,256]{1,0:T(8,128)S(1)} %collective-permute-done.9, f32[128,256]{1,0:T(8,128)} %collective-permute-done.10, ...), kind=kLoop, calls=%fused_computation.4 | loop fusion | flops 196608 | bytes 917505 | tf_op jit(solution)/shard_map/add | solution.py:176
  42.6 1.6 %collective-permute-start.16 = (f32[136,256]{1,0:T(8,128)S(1)}, f32[136,256]{1,0:T(8,128)S(1)}, u32[]{:S(2)}, u32[]{:S(2)}) collective-permute-start(f32[136,256]{1,0:T(8,128)S(1)} %get-tuple-element.35), channel_id=1, source_target_pairs={{0,4},{4,0},{8,12},{12,8},{16,20},{20,16},{24,28},{28,24},{1,5},{5... | collective-permute-start | bytes 417800 | tf_op jit(solution)/shard_map/ppermute | solution.py:176
  44.8 3.3 %shard_map.55 = (f32[256,1024]{1,0:T(8,128)S(1)}, f32[256,1024]{1,0:T(8,128)S(1)}, bf16[256,2048]{1,0:T(8,128)(2,1)S(1)}) custom-call(s32[1]{0:T(128)} %bitcast.first_ref, bf16[8,256]{1,0:T(8,128)(2,1)S(1)} %copy-done.4, bf16[256,1024]{1,0:T(8,128)(2,1)S(1)} %copy-done.6, bf16[256,1024]{1,0:T(8,128)(2,1)S(1)} %copy-done.1, bf16[256,1024]{1,0:T(8,128)(2,1)S(1)} %copy-done.3), custom_call_target="tpu_custom_call" | custom-call | flops 671088640 | bytes 4722692 | tf_op jit(solution)/shard_map/pallas_call | solution.py:124
  48.7 3.4 %collective-permute-done.17.refs_1_ = f32[128,256]{1,0:T(8,128)S(1)} collective-permute-done((f32[128,256]{1,0:T(8,128)S(1)}, f32[128,256]{1,0:T(8,128)S(1)}, u32[]{:S(2)}, u32[]{:S(2)}) %collective-permute-start.17) | collective-permute-done | bytes 131104 | tf_op jit(solution)/shard_map/ppermute | solution.py:176
  52.8 1.6 %collective-permute-start.21 = (f32[8,256]{1,0:T(8,128)S(1)}, f32[8,256]{1,0:T(8,128)S(1)}, u32[]{:S(2)}, u32[]{:S(2)}) collective-permute-start(f32[8,256]{1,0:T(8,128)S(1)} %add.115.refs_0_), channel_id=1, source_target_pairs={{0,2},{1,3},{2,0},{3,1},{4,6},{5,7},{6,4},{7,5},{8,10},{9,11},{10,... | collective-permute-start | bytes 24584 | tf_op jit(solution)/shard_map/ppermute | solution.py:190
  54.6 2.0 %collective-permute-done.21.refs_2_ = f32[8,256]{1,0:T(8,128)S(1)} collective-permute-done((f32[8,256]{1,0:T(8,128)S(1)}, f32[8,256]{1,0:T(8,128)S(1)}, u32[]{:S(2)}, u32[]{:S(2)}) %collective-permute-start.21) | collective-permute-done | bytes 8224 | tf_op jit(solution)/shard_map/ppermute | solution.py:190
  56.5 0.9 %collective-permute-done.20.refs_1_ = f32[8,256]{1,0:T(8,128)S(1)} collective-permute-done((f32[8,256]{1,0:T(8,128)S(1)}, f32[8,256]{1,0:T(8,128)S(1)}, u32[]{:S(2)}, u32[]{:S(2)}) %collective-permute-start.20) | collective-permute-done | bytes 8224 | tf_op jit(solution)/shard_map/ppermute | solution.py:190
  57.5 1.1 %shard_map.60 = bf16[256,1024]{1,0:T(8,128)(2,1)} custom-call(s32[1]{0:T(128)} %bitcast.first_ref, f32[1,1024]{1,0:T(1,128)S(1)} %bitcast.3, f32[256,512]{1,0:T(8,128)S(1)} %get-tuple-element.31.own_ref, f32[256,512]{1,0:T(8,128)S(1)} %get-tuple-element.32.other_ref, f32[8,256]{1,0:T(8,128)S(1)} %add.115.refs_0_, ...), custom_call_target="tpu_custom_call" | custom-call | flops 786432 | bytes 1609732 | tf_op jit(solution)/shard_map/pallas_call | solution.py:124
  (51 shorter events, 8.9 us)
Async XLA Ops:
  0.0 0.7 %copy-start.4 = (bf16[8,256]{1,0:T(8,128)(2,1)S(1)}, bf16[8,256]{1,0:T(8,128)(2,1)}, u32[]{:S(2)}) copy-start(bf16[8,256]{1,0:T(8,128)(2,1)} %seeds_ref.5) | copy-start | bytes 12292
  0.7 1.0 %copy-start = (bf16[256,1024]{1,0:T(8,128)(2,1)S(1)}, bf16[256,1024]{1,0:T(8,128)(2,1)}, u32[]{:S(2)}) copy-start(bf16[256,1024]{1,0:T(8,128)(2,1)} %k_ref.5) | copy-start | bytes 1572868
  1.7 1.0 %copy-start.2 = (bf16[256,1024]{1,0:T(8,128)(2,1)S(1)}, bf16[256,1024]{1,0:T(8,128)(2,1)}, u32[]{:S(2)}) copy-start(bf16[256,1024]{1,0:T(8,128)(2,1)} %v_ref.5) | copy-start | bytes 1572868
  2.8 5.2 %copy-start.1 = (bf16[256,1024]{1,0:T(8,128)(2,1)S(1)}, bf16[256,1024]{1,0:T(8,128)(2,1)}, u32[]{:S(2)}) copy-start(bf16[256,1024]{1,0:T(8,128)(2,1)} %k_ref.5) | copy-start | bytes 1572868
  2.8 5.2 %copy-start.3 = (bf16[256,1024]{1,0:T(8,128)(2,1)S(1)}, bf16[256,1024]{1,0:T(8,128)(2,1)}, u32[]{:S(2)}) copy-start(bf16[256,1024]{1,0:T(8,128)(2,1)} %v_ref.5) | copy-start | bytes 1572868
  3.9 6.4 %collective-permute-start.12 = (f32[128,256]{1,0:T(8,128)S(1)}, f32[128,256]{1,0:T(8,128)S(1)}, u32[]{:S(2)}, u32[]{:S(2)}) collective-permute-start(f32[128,256]{1,0:T(8,128)S(1)} %get-tuple-element.30), channel_id=1, source_target_pairs={{0,4},{4,0},{8,12},{12,8},{16,20},{20,16},{24,28},{28,24},{1,5},{5... | collective-permute-start | bytes 393224 | tf_op jit(solution)/shard_map/ppermute | solution.py:160
  5.4 7.9 %collective-permute-start = (f32[136,256]{1,0:T(8,128)S(1)}, f32[136,256]{1,0:T(8,128)S(1)}, u32[]{:S(2)}, u32[]{:S(2)}) collective-permute-start(f32[136,256]{1,0:T(8,128)S(1)} %get-tuple-element.24), channel_id=1, source_target_pairs={{0,4},{4,0},{8,12},{12,8},{16,20},{20,16},{24,28},{28,24},{1,5},{5... | collective-permute-start | bytes 417800 | tf_op jit(solution)/shard_map/ppermute | solution.py:160
  6.0 12.5 %collective-permute-start.4 = (f32[128,256]{1,0:T(8,128)S(1)}, f32[128,256]{1,0:T(8,128)S(1)}, u32[]{:S(2)}, u32[]{:S(2)}) collective-permute-start(f32[128,256]{1,0:T(8,128)S(1)} %get-tuple-element.26), channel_id=1, source_target_pairs={{0,4},{4,0},{8,12},{12,8},{16,20},{20,16},{24,28},{28,24},{1,5},{5... | collective-permute-start | bytes 393224 | tf_op jit(solution)/shard_map/ppermute | solution.py:160
  7.5 10.3 %collective-permute-start.8 = (f32[128,256]{1,0:T(8,128)S(1)}, f32[128,256]{1,0:T(8,128)S(1)}, u32[]{:S(2)}, u32[]{:S(2)}) collective-permute-start(f32[128,256]{1,0:T(8,128)S(1)} %get-tuple-element.28), channel_id=1, source_target_pairs={{0,4},{4,0},{8,12},{12,8},{16,20},{20,16},{24,28},{28,24},{1,5},{5... | collective-permute-start | bytes 393224 | tf_op jit(solution)/shard_map/ppermute | solution.py:160
  10.4 8.8 %collective-permute-start.13 = (f32[128,256]{1,0:T(8,128)S(1)}, f32[128,256]{1,0:T(8,128)S(1)}, u32[]{:S(2)}, u32[]{:S(2)}) collective-permute-start(f32[128,256]{1,0:T(8,128)S(1)} %add.105), channel_id=1, source_target_pairs={{0,8},{4,12},{1,9},{5,13},{2,10},{6,14},{3,11},{7,15}} | collective-permute-start | bytes 393224 | tf_op jit(solution)/shard_map/ppermute | solution.py:174
  13.3 7.2 %collective-permute-start.1 = (f32[136,256]{1,0:T(8,128)S(1)}, f32[136,256]{1,0:T(8,128)S(1)}, u32[]{:S(2)}, u32[]{:S(2)}) collective-permute-start(f32[136,256]{1,0:T(8,128)S(1)} %add.87), channel_id=1, source_target_pairs={{0,8},{4,12},{1,9},{5,13},{2,10},{6,14},{3,11},{7,15}} | collective-permute-start | bytes 417800 | tf_op jit(solution)/shard_map/ppermute | solution.py:174
  17.8 4.7 %collective-permute-start.9 = (f32[128,256]{1,0:T(8,128)S(1)}, f32[128,256]{1,0:T(8,128)S(1)}, u32[]{:S(2)}, u32[]{:S(2)}) collective-permute-start(f32[128,256]{1,0:T(8,128)S(1)} %add.99), channel_id=1, source_target_pairs={{0,8},{4,12},{1,9},{5,13},{2,10},{6,14},{3,11},{7,15}} | collective-permute-start | bytes 393224 | tf_op jit(solution)/shard_map/ppermute | solution.py:174
  18.5 6.0 %collective-permute-start.5 = (f32[128,256]{1,0:T(8,128)S(1)}, f32[128,256]{1,0:T(8,128)S(1)}, u32[]{:S(2)}, u32[]{:S(2)}) collective-permute-start(f32[128,256]{1,0:T(8,128)S(1)} %add.93), channel_id=1, source_target_pairs={{0,8},{4,12},{1,9},{5,13},{2,10},{6,14},{3,11},{7,15}} | collective-permute-start | bytes 393224 | tf_op jit(solution)/shard_map/ppermute | solution.py:174
  19.2 8.1 %collective-permute-start.14 = (f32[128,256]{1,0:T(8,128)S(1)}, f32[128,256]{1,0:T(8,128)S(1)}, u32[]{:S(2)}, u32[]{:S(2)}) collective-permute-start(f32[128,256]{1,0:T(8,128)S(1)} %add.106), channel_id=1, source_target_pairs={{8,16},{12,20},{9,17},{13,21},{10,18},{14,22},{11,19},{15,23}} | collective-permute-start | bytes 393224 | tf_op jit(solution)/shard_map/ppermute | solution.py:174
  21.2 15.6 %collective-permute-start.2 = (f32[136,256]{1,0:T(8,128)}, f32[136,256]{1,0:T(8,128)S(1)}, u32[]{:S(2)}, u32[]{:S(2)}) collective-permute-start(f32[136,256]{1,0:T(8,128)} %add.88), channel_id=1, source_target_pairs={{8,16},{12,20},{9,17},{13,21},{10,18},{14,22},{11,19},{15,23}} | collective-permute-start | bytes 417800 | tf_op jit(solution)/shard_map/ppermute | solution.py:174
  23.2 10.0 %collective-permute-start.10 = (f32[128,256]{1,0:T(8,128)}, f32[128,256]{1,0:T(8,128)}, u32[]{:S(2)}, u32[]{:S(2)}) collective-permute-start(f32[128,256]{1,0:T(8,128)} %add.100), channel_id=1, source_target_pairs={{8,16},{12,20},{9,17},{13,21},{10,18},{14,22},{11,19},{15,23}} | collective-permute-start | bytes 393224 | tf_op jit(solution)/shard_map/ppermute | solution.py:174
  25.2 10.3 %collective-permute-start.6 = (f32[128,256]{1,0:T(8,128)}, f32[128,256]{1,0:T(8,128)S(1)}, u32[]{:S(2)}, u32[]{:S(2)}) collective-permute-start(f32[128,256]{1,0:T(8,128)} %add.94), channel_id=1, source_target_pairs={{8,16},{12,20},{9,17},{13,21},{10,18},{14,22},{11,19},{15,23}} | collective-permute-start | bytes 393224 | tf_op jit(solution)/shard_map/ppermute | solution.py:174
  28.0 10.2 %collective-permute-start.15 = (f32[128,256]{1,0:T(8,128)}, f32[128,256]{1,0:T(8,128)}, u32[]{:S(2)}, u32[]{:S(2)}) collective-permute-start(f32[128,256]{1,0:T(8,128)} %add.108), channel_id=1, source_target_pairs={{16,24},{20,28},{17,25},{21,29},{18,26},{22,30},{19,27},{23,31}} | collective-permute-start | bytes 393224 | tf_op jit(solution)/shard_map/ppermute | solution.py:174
  34.1 6.5 %collective-permute-start.11 = (f32[128,256]{1,0:T(8,128)S(1)}, f32[128,256]{1,0:T(8,128)S(1)}, u32[]{:S(2)}, u32[]{:S(2)}) collective-permute-start(f32[128,256]{1,0:T(8,128)S(1)} %add.102), channel_id=1, source_target_pairs={{16,24},{20,28},{17,25},{21,29},{18,26},{22,30},{19,27},{23,31}} | collective-permute-start | bytes 393224 | tf_op jit(solution)/shard_map/ppermute | solution.py:174
  35.5 8.6 %collective-permute-start.7 = (f32[128,256]{1,0:T(8,128)S(1)}, f32[128,256]{1,0:T(8,128)S(1)}, u32[]{:S(2)}, u32[]{:S(2)}) collective-permute-start(f32[128,256]{1,0:T(8,128)S(1)} %add.96), channel_id=1, source_target_pairs={{16,24},{20,28},{17,25},{21,29},{18,26},{22,30},{19,27},{23,31}} | collective-permute-start | bytes 393224 | tf_op jit(solution)/shard_map/ppermute | solution.py:174
  36.8 5.7 %collective-permute-start.3 = (f32[136,256]{1,0:T(8,128)S(1)}, f32[136,256]{1,0:T(8,128)S(1)}, u32[]{:S(2)}, u32[]{:S(2)}) collective-permute-start(f32[136,256]{1,0:T(8,128)S(1)} %add.90), channel_id=1, source_target_pairs={{16,24},{20,28},{17,25},{21,29},{18,26},{22,30},{19,27},{23,31}} | collective-permute-start | bytes 417800 | tf_op jit(solution)/shard_map/ppermute | solution.py:174
  39.1 9.6 %collective-permute-start.19 = (f32[128,256]{1,0:T(8,128)S(1)}, f32[128,256]{1,0:T(8,128)S(1)}, u32[]{:S(2)}, u32[]{:S(2)}) collective-permute-start(f32[128,256]{1,0:T(8,128)S(1)} %get-tuple-element.37), channel_id=1, source_target_pairs={{0,4},{4,0},{8,12},{12,8},{16,20},{20,16},{24,28},{28,24},{1,5},{5... | collective-permute-start | bytes 393224 | tf_op jit(solution)/shard_map/ppermute | solution.py:176
  41.6 7.1 %collective-permute-start.18 = (f32[128,256]{1,0:T(8,128)S(1)}, f32[128,256]{1,0:T(8,128)S(1)}, u32[]{:S(2)}, u32[]{:S(2)}) collective-permute-start(f32[128,256]{1,0:T(8,128)S(1)} %get-tuple-element.39), channel_id=1, source_target_pairs={{0,4},{4,0},{8,12},{12,8},{16,20},{20,16},{24,28},{28,24},{1,5},{5... | collective-permute-start | bytes 393224 | tf_op jit(solution)/shard_map/ppermute | solution.py:176
  42.5 2.2 %copy-start.6 = (bf16[256,1024]{1,0:T(8,128)(2,1)S(1)}, bf16[256,1024]{1,0:T(8,128)(2,1)}, u32[]{:S(2)}) copy-start(bf16[256,1024]{1,0:T(8,128)(2,1)} %q_ref.1) | copy-start | bytes 1572868
  42.6 9.6 %collective-permute-start.16 = (f32[136,256]{1,0:T(8,128)S(1)}, f32[136,256]{1,0:T(8,128)S(1)}, u32[]{:S(2)}, u32[]{:S(2)}) collective-permute-start(f32[136,256]{1,0:T(8,128)S(1)} %get-tuple-element.35), channel_id=1, source_target_pairs={{0,4},{4,0},{8,12},{12,8},{16,20},{20,16},{24,28},{28,24},{1,5},{5... | collective-permute-start | bytes 417800 | tf_op jit(solution)/shard_map/ppermute | solution.py:176
  44.2 8.0 %collective-permute-start.17 = (f32[128,256]{1,0:T(8,128)S(1)}, f32[128,256]{1,0:T(8,128)S(1)}, u32[]{:S(2)}, u32[]{:S(2)}) collective-permute-start(f32[128,256]{1,0:T(8,128)S(1)} %get-tuple-element.41), channel_id=1, source_target_pairs={{0,4},{4,0},{8,12},{12,8},{16,20},{20,16},{24,28},{28,24},{1,5},{5... | collective-permute-start | bytes 393224 | tf_op jit(solution)/shard_map/ppermute | solution.py:176
  52.7 4.7 %copy-start.5 = (f32[1024]{0:T(1024)S(1)}, f32[1024]{0:T(1024)}, u32[]{:S(2)}) copy-start(f32[1024]{0:T(1024)} %param.9) | copy-start | bytes 12292
  52.7 1.8 %collective-permute-start.22 = (f32[8,256]{1,0:T(8,128)S(1)}, f32[8,256]{1,0:T(8,128)S(1)}, u32[]{:S(2)}, u32[]{:S(2)}) collective-permute-start(f32[8,256]{1,0:T(8,128)S(1)} %add.115.refs_0_), channel_id=1, source_target_pairs={{0,3},{1,0},{2,1},{3,2},{4,7},{5,4},{6,5},{7,6},{8,11},{9,8},{10,9... | collective-permute-start | bytes 24584 | tf_op jit(solution)/shard_map/ppermute | solution.py:190
  52.8 3.7 %collective-permute-start.21 = (f32[8,256]{1,0:T(8,128)S(1)}, f32[8,256]{1,0:T(8,128)S(1)}, u32[]{:S(2)}, u32[]{:S(2)}) collective-permute-start(f32[8,256]{1,0:T(8,128)S(1)} %add.115.refs_0_), channel_id=1, source_target_pairs={{0,2},{1,3},{2,0},{3,1},{4,6},{5,7},{6,4},{7,5},{8,10},{9,11},{10,... | collective-permute-start | bytes 24584 | tf_op jit(solution)/shard_map/ppermute | solution.py:190
  54.4 3.1 %collective-permute-start.20 = (f32[8,256]{1,0:T(8,128)S(1)}, f32[8,256]{1,0:T(8,128)S(1)}, u32[]{:S(2)}, u32[]{:S(2)}) collective-permute-start(f32[8,256]{1,0:T(8,128)S(1)} %add.115.refs_0_), channel_id=1, source_target_pairs={{0,1},{1,2},{2,3},{3,0},{4,5},{5,6},{6,7},{7,4},{8,9},{9,10},{10,1... | collective-permute-start | bytes 24584 | tf_op jit(solution)/shard_map/ppermute | solution.py:190

commit v2 on v1

v2 whole, which is shorter than its diff:
```python
import functools

import jax
import jax.numpy as jnp
from jax import lax
from jax.experimental import pallas as pl
from jax.experimental.pallas import tpu as pltpu
from jax.sharding import PartitionSpec as P

WIDTH = 128
NT = (((1,), (1,)), ((), ()))
TN = (((0,), (0,)), ((), ()))
VMEM = pl.BlockSpec(memory_space=pltpu.VMEM)
HBM = pl.BlockSpec(memory_space=pltpu.HBM)
ANY = pl.BlockSpec(memory_space=pl.ANY)
SMEM = pl.BlockSpec(memory_space=pltpu.SMEM)
MIB = 2**20


def rotated(seeds_ref, first):
    heads = seeds_ref.shape[0]
    seeds = seeds_ref[...].astype(jnp.float32)
    return pltpu.roll(seeds, lax.rem(heads - first, heads), 0)


def table_of(seeds, i, group):
    row = seeds[i : i + 1, group * WIDTH : (group + 1) * WIDTH]
    square = jnp.broadcast_to(row, (WIDTH, WIDTH))
    return pltpu.roll(square, 0, 1, stride=1, stride_axis=0).astype(jnp.bfloat16)


def phi(x, table):
    mixed = jnp.dot(x, table, preferred_element_type=jnp.float32) * WIDTH ** (-0.25)
    return (jnp.exp(jnp.minimum(mixed, 0.0)) + jnp.maximum(mixed, 0.0)).astype(jnp.bfloat16)


def features(x, seeds, i):
    groups = seeds.shape[1] // WIDTH
    return jnp.concatenate([phi(x, table_of(seeds, i, g)) for g in range(groups)], axis=1)


def columns(head):
    return pl.ds(pl.multiple_of(head * WIDTH, WIDTH), WIDTH)


def state_kernel(half, first_ref, seeds_hbm, k_hbm, v_hbm, *refs):
    outs, (seeds_ref, k_ref, v_ref, sems) = refs[:half], refs[half:]
    first = first_ref[0]
    span = pl.ds(pl.multiple_of(first * WIDTH, WIDTH), half * WIDTH)
    copies = [
        pltpu.make_async_copy(seeds_hbm, seeds_ref, sems.at[0]),
        pltpu.make_async_copy(k_hbm.at[:, span], k_ref, sems.at[1]),
        pltpu.make_async_copy(v_hbm.at[:, span], v_ref, sems.at[2]),
    ]
    for copy in copies:
        copy.start()
    copies[0].wait()
    seeds = rotated(seeds_ref, first)
    outs[0][WIDTH:, :] = jnp.zeros((outs[0].shape[0] - WIDTH, outs[0].shape[1]), jnp.float32)
    copies[1].wait()
    copies[2].wait()
    for i in range(half):
        at = slice(i * WIDTH, (i + 1) * WIDTH)
        fk = features(k_ref[:, at], seeds, i)
        outs[i][0:WIDTH, :] = lax.dot_general(
            v_ref[:, at], fk, TN, preferred_element_type=jnp.float32
        )
        outs[0][WIDTH + i : WIDTH + i + 1, :] = jnp.sum(
            fk.astype(jnp.float32), axis=0, keepdims=True
        )


def local_kernel(places, first_ref, seeds_ref, q_ref, k_ref, v_ref, *outs):
    seeds = rotated(seeds_ref, first_ref[0])
    heads = seeds_ref.shape[0]
    tok = q_ref.shape[0]
    rows = lax.broadcasted_iota(jnp.int32, (tok, tok), 0)
    causal = lax.broadcasted_iota(jnp.int32, (tok, tok), 1) <= rows
    for n, i in enumerate(places):
        num_ref, den_ref, fq_ref = outs[3 * n : 3 * n + 3]
        head = lax.rem(first_ref[0] + i, heads)
        fk = features(k_ref[:, columns(head)], seeds, i)
        fq = features(q_ref[:, columns(head)], seeds, i)
        fq_ref[...] = fq
        scores = lax.dot_general(fq, fk, NT, preferred_element_type=jnp.float32)
        scores = jnp.where(causal, scores, 0.0)
        num_ref[...] = jnp.dot(
            scores.astype(jnp.bfloat16),
            v_ref[:, columns(head)],
            preferred_element_type=jnp.float32,
        )
        den_ref[...] = jnp.broadcast_to(jnp.sum(scores, axis=1, keepdims=True), (tok, WIDTH))


def join_kernel(i, *refs):
    ins, (own_ref, other_ref, squares_ref) = refs[:-3], refs[-3:]
    squares = jnp.zeros(own_ref.shape, jnp.float32)
    for n, out_ref in enumerate((own_ref, other_ref)):
        num_ref, den_ref, fq_ref, state_ref, totals_ref = ins[5 * n : 5 * n + 5]
        total = totals_ref[WIDTH + i : WIDTH + i + 1, :]
        wide = jnp.concatenate(
            [state_ref[0:WIDTH, :], jnp.broadcast_to(total, (WIDTH, total.shape[1]))], axis=0
        )
        upper = wide.astype(jnp.bfloat16)
        lower = (wide - upper.astype(jnp.float32)).astype(jnp.bfloat16)
        fq = fq_ref[...]
        both = lax.dot_general(fq, upper, NT, preferred_element_type=jnp.float32)
        both = both + lax.dot_general(fq, lower, NT, preferred_element_type=jnp.float32)
        head = (num_ref[...] + both[:, :WIDTH]) / (den_ref[...] + both[:, WIDTH:])
        out_ref[...] = head
        squares = squares + head * head
    rows = jnp.broadcast_to(jnp.sum(squares, axis=1, keepdims=True), squares.shape)
    squares_ref[...] = rows.T[0:8, :]
    if len(ins) > 10:
        squares_ref[...] += ins[10][...]


def norm_kernel(half, entries, first_ref, gain_ref, *refs):
    heads, squares, out_ref = refs[: 2 * half], refs[2 * half : -1], refs[-1]
    tok = out_ref.shape[0]
    overall = functools.reduce(lambda a, b: a + b, [ref[...] for ref in squares])
    factor = lax.rsqrt(overall / entries + 1e-06)
    wide = jnp.broadcast_to(factor[0:1, :], (WIDTH, tok)).T
    for i, source in enumerate(heads):
        at = columns(lax.rem(first_ref[0] + i, 2 * half))
        out_ref[:, at] = (source[...] * wide * gain_ref[:, at]).astype(jnp.bfloat16)


def first_kernel(flag_ref, _, ours_ref, incoming_ref, totals_ref, extra_ref):
    totals_ref[...] = ours_ref[...] + incoming_ref[...]
    extra_ref[...] = jnp.where(flag_ref[0] == 0, ours_ref[...], incoming_ref[...])


def hop_kernel(flag_ref, _, arrived_ref, totals_ref, *refs):
    sent_ref, prior_ref = refs[-2:]
    sent_ref[...] = arrived_ref[...] + totals_ref[...]
    prior_ref[...] = arrived_ref[...] + (refs[0][...] if len(refs) > 2 else 0.0)


def last_kernel(flag_ref, _, arrived_ref, extra_ref, *refs):
    passed_ref, own_ref = refs[-2:]
    prior = arrived_ref[...] + (refs[0][...] if len(refs) > 2 else 0.0)
    more = prior + extra_ref[...]
    passed_ref[...] = jnp.where(flag_ref[0] == 0, more, prior)
    own_ref[...] = jnp.where(flag_ref[0] == 0, prior, more)


def call(kernel, outs, ins, scalars, flops, scratch=(), place=VMEM, limit=16 * MIB, unused=0):
    moved = sum(x.size * x.dtype.itemsize for x in ins)
    moved += sum(x.size * jnp.dtype(x.dtype).itemsize for x in jax.tree.leaves(outs))
    return pl.pallas_call(
        kernel,
        out_shape=outs,
        in_specs=[SMEM] * scalars + [ANY] * unused + [place] * (len(ins) - scalars - unused),
        out_specs=jax.tree.map(lambda _: VMEM, outs),
        scratch_shapes=list(scratch),
        compiler_params=pltpu.CompilerParams(vmem_limit_bytes=limit),
        cost_estimate=pl.CostEstimate(flops=flops, bytes_accessed=moved, transcendentals=0),
    )(*ins)


def per_device(queries, keys, values, seeds, gain):
    f32 = jnp.float32
    tok = queries.shape[0]
    heads, feats = seeds.shape
    half = heads // 2
    count = lax.axis_size("seq")
    pairs = count // 2
    mine = lax.axis_index("seq")
    side = lax.rem(mine, 2)
    own_first = (side * half).reshape(1)
    other_first = ((1 - side) * half).reshape(1)
    shape = lambda *dims, dtype=f32: jax.ShapeDtypeStruct(dims, dtype)

    state_shapes = [shape(WIDTH + (8 if i == 0 else 0), feats) for i in range(half)]
    part = pltpu.VMEM((tok, half * WIDTH), keys.dtype)
    states = lambda first, limit: call(
        functools.partial(state_kernel, half),
        state_shapes,
        (first, seeds, keys, values),
        1,
        half * tok * feats * WIDTH * 4,
        [pltpu.VMEM((heads, feats), seeds.dtype), part, part, pltpu.SemaphoreType.DMA((3,))],
        HBM,
        limit,
    )
    theirs = states(other_first, 60 * MIB)
    ours = states(own_first, 40 * MIB)

    swap = [(i, i ^ 1) for i in range(count)]
    hops = [[(2 * p, 2 * p + 2), (2 * p + 1, 2 * p + 3)] for p in range(pairs - 1)]
    incoming = [lax.ppermute(part, "seq", swap) for part in theirs]
    totals, extra, prior = [None] * half, [None] * half, [None] * half
    arrived, own_prior, passed = [None] * half, [None] * half, [None] * half
    flag = side.reshape(1)
    last = flag
    for slot in range(half + len(hops)):
        for stage in range(len(hops) + 1):
            i = slot - stage
            if not 0 <= i < half:
                continue
            like = jax.ShapeDtypeStruct(ours[i].shape, f32)
            glue = lambda kernel, *ins: call(kernel, [like, like], (flag, last, *ins), 1, 10**9, unused=1)
            if stage == 0:
                totals[i], extra[i] = glue(first_kernel, ours[i], incoming[i])
                sent = totals[i]
            elif stage < len(hops):
                sent, prior[i] = glue(hop_kernel, arrived[i], totals[i], *([prior[i]] if stage > 1 else []))
            else:
                sent, own_prior[i] = glue(last_kernel, arrived[i], extra[i], *([prior[i]] if stage > 1 else []))
            last = sent
            if stage < len(hops):
                arrived[i] = lax.ppermute(sent, "seq", hops[stage])
            else:
                passed[i] = lax.ppermute(sent, "seq", swap)
    bf16 = jnp.bfloat16
    local_shapes = [shape(tok, WIDTH), shape(tok, WIDTH), shape(tok, feats, dtype=bf16)]
    own_heads, other_heads, squares = [], [], None
    for i in range(half):
        parts = call(
            functools.partial(local_kernel, (i, half + i)),
            local_shapes * 2,
            (own_first, seeds, queries, keys, values),
            1,
            2 * tok * (feats * WIDTH * 4 + tok * (feats + WIDTH) * 2),
        )
        joined = (*parts[:3], own_prior[i], own_prior[0], *parts[3:], passed[i], passed[0])
        own, other, squares = call(
            functools.partial(join_kernel, i),
            [shape(tok, WIDTH), shape(tok, WIDTH), shape(8, tok)],
            joined if squares is None else (*joined, squares),
            0,
            2 * tok * feats * WIDTH * 8,
        )
        own_heads.append(own)
        other_heads.append(other)
    across = lax.axis_size("tp")
    gathered = [squares] + [
        lax.ppermute(squares, "tp", [(i, (i + k) % across) for i in range(across)])
        for k in range(1, across)
    ]
    return call(
        functools.partial(norm_kernel, half, heads * WIDTH * across),
        shape(tok, heads * WIDTH, dtype=jnp.bfloat16),
        (own_first, gain.reshape(1, -1), *own_heads, *other_heads, *gathered),
        1,
        tok * heads * WIDTH * 3,
    )


def solution(mesh):
    placed = (P("seq", "tp"), P("seq", "tp"), P("seq", "tp"), P("tp", None), P("tp"))
    return jax.shard_map(
        per_device, mesh=mesh, in_specs=placed, out_specs=P("seq", "tp"), check_vma=False
    )
```

time: 59 us -> 54.6 us (0.925)
  the two profiles are of different devices: /device:TPU:16 before, /device:TPU:17 now
where the time goes in v2:
time: 54.6 us; the launch traced here: 54 us
  starting transfers between devices  26.8 us (49%)
  waiting for transfers between devices  14 us (26%)
  Pallas kernels  11.4 us (21%)
  local copies, waits for them, and re-layouts  1.43 us (3%)
    ppermute x12, starting transfers between devices, per_device(): arrived[i] = lax.ppermute(sent, 'seq', hops[stage])  13.2 us
    pallas_call x27, Pallas kernels, call(): pl.pallas_call(kernel, out_shape=outs, in_specs=[SMEM] * scalars + [ANY]...  11.4 us
    ppermute x12, waiting for transfers between devices, per_device(): arrived[i] = lax.ppermute(sent, 'seq', hops[stage])  8.43 us
    ppermute x3, starting transfers between devices, per_device(): lax.ppermute(squares, 'tp', [(i, (i + k) % across) for i in range(across)])  7.45 us
    ppermute x4, starting transfers between devices, per_device(): passed[i] = lax.ppermute(sent, 'seq', swap)  3.23 us
    ppermute x4, starting transfers between devices, per_device(): incoming = [lax.ppermute(part, 'seq', swap) for part in theirs]  3 us
    ppermute x3, waiting for transfers between devices, per_device(): lax.ppermute(squares, 'tp', [(i, (i + k) % across) for i in range(across)])  2.83 us
    ppermute x4, waiting for transfers between devices, per_device(): incoming = [lax.ppermute(part, 'seq', swap) for part in theirs]  2.74 us
  transfers between devices with their start and end apart: 23, of which 10 were waited for; matrix products, arithmetic and copies ran while one was open for 0% of the time, Pallas kernels for 13%

profile of v2, /device:TPU:17, one launch (start us, length us, event | category | flops | bytes accessed | tf_op | source)
XLA Modules:
  0.0 54.0 jit_solution(7829394420234026631)
XLA Ops:
  0.0 2.9 %shard_map.57 = (f32[136,256]{1,0:T(8,128)}, f32[128,256]{1,0:T(8,128)}, f32[128,256]{1,0:T(8,128)}, f32[128,256]{1,0:T(8,128)}) custom-call(s32[1]{0:T(128)} %bitcast.3.first_ref, bf16[8,256]{1,0:T(8,128)(2,1)} %seeds_ref.7, bf16[256,1024]{1,0:T(8,128)(2,1)} %k_ref.7, bf16[256,1024]{1,0:T(8,128)(2,1)} %v_ref.7), custom_call_target="tpu_custom_call" | custom-call | flops 134217728 | bytes 1585156 | tf_op jit(solution)/shard_map/pallas_call | solution.py:151
  2.9 1.3 %collective-permute-start = (f32[136,256]{1,0:T(8,128)}, f32[136,256]{1,0:T(8,128)S(1)}, u32[]{:S(2)}, u32[]{:S(2)}) collective-permute-start(f32[136,256]{1,0:T(8,128)} %get-tuple-element.85), channel_id=1, source_target_pairs={{0,4},{4,0},{8,12},{12,8},{16,20},{20,16},{24,28},{28,24},{1,5},{5... | collective-permute-start | bytes 417800 | tf_op jit(solution)/shard_map/ppermute | solution.py:192
  4.5 1.2 %shard_map.56 = (f32[136,256]{1,0:T(8,128)S(1)}, f32[128,256]{1,0:T(8,128)S(1)}, f32[128,256]{1,0:T(8,128)S(1)}, f32[128,256]{1,0:T(8,128)S(1)}) custom-call(s32[1]{0:T(128)} %bitcast.first_ref, bf16[8,256]{1,0:T(8,128)(2,1)S(1)} %copy-done.3, bf16[256,1024]{1,0:T(8,128)(2,1)S(1)} %copy-done, bf16[256,1024]{1,0:T(8,128)(2,1)S(1)} %copy-done.1), custom_call_target="tpu_custom_call" | custom-call | flops 134217728 | bytes 1585156 | tf_op jit(solution)/shard_map/pallas_call | solution.py:151
  5.7 2.1 %collective-permute-done.incoming_ref = f32[136,256]{1,0:T(8,128)S(1)} collective-permute-done((f32[136,256]{1,0:T(8,128)}, f32[136,256]{1,0:T(8,128)S(1)}, u32[]{:S(2)}, u32[]{:S(2)}) %collective-permute-start) | collective-permute-done | bytes 139296 | tf_op jit(solution)/shard_map/ppermute | solution.py:192
  7.8 0.8 %collective-permute-start.2 = (f32[136,256]{1,0:T(8,128)S(1)}, f32[136,256]{1,0:T(8,128)S(1)}, u32[]{:S(2)}, u32[]{:S(2)}) collective-permute-start(f32[136,256]{1,0:T(8,128)S(1)} %get-tuple-element.86._.totals_ref), channel_id=1, source_target_pairs={{0,8},{4,12},{1,9},{5,13},{2,10},{6,14},{3,11},{7,15}} | collective-permute-start | bytes 417800 | tf_op jit(solution)/shard_map/ppermute | solution.py:213
  8.6 1.2 %collective-permute-start.3 = (f32[128,256]{1,0:T(8,128)S(1)}, f32[128,256]{1,0:T(8,128)S(1)}, u32[]{:S(2)}, u32[]{:S(2)}) collective-permute-start(f32[128,256]{1,0:T(8,128)S(1)} %copy-done.6), channel_id=1, source_target_pairs={{0,4},{4,0},{8,12},{12,8},{16,20},{20,16},{24,28},{28,24},{1,5},{5... | collective-permute-start | bytes 393224 | tf_op jit(solution)/shard_map/ppermute | solution.py:192
  10.6 0.7 %collective-permute-start.4 = (f32[128,256]{1,0:T(8,128)S(1)}, f32[128,256]{1,0:T(8,128)S(1)}, u32[]{:S(2)}, u32[]{:S(2)}) collective-permute-start(f32[128,256]{1,0:T(8,128)S(1)} %get-tuple-element.89._.totals_ref), channel_id=1, source_target_pairs={{0,8},{4,12},{1,9},{5,13},{2,10},{6,14},{3,11},{7,15}} | collective-permute-start | bytes 393224 | tf_op jit(solution)/shard_map/ppermute | solution.py:213
  11.3 1.3 %collective-permute-start.5 = (f32[136,256]{1,0:T(8,128)S(1)}, f32[136,256]{1,0:T(8,128)S(1)}, u32[]{:S(2)}, u32[]{:S(2)}) collective-permute-start(f32[136,256]{1,0:T(8,128)S(1)} %get-tuple-element.90._), channel_id=1, source_target_pairs={{8,16},{12,20},{9,17},{13,21},{10,18},{14,22},{11,19},{15,23}} | collective-permute-start | bytes 417800 | tf_op jit(solution)/shard_map/ppermute | solution.py:213
  12.8 0.7 %collective-permute-start.7 = (f32[128,256]{1,0:T(8,128)S(1)}, f32[128,256]{1,0:T(8,128)S(1)}, u32[]{:S(2)}, u32[]{:S(2)}) collective-permute-start(f32[128,256]{1,0:T(8,128)S(1)} %get-tuple-element.93._.totals_ref), channel_id=1, source_target_pairs={{0,8},{4,12},{1,9},{5,13},{2,10},{6,14},{3,11},{7,15}} | collective-permute-start | bytes 393224 | tf_op jit(solution)/shard_map/ppermute | solution.py:213
  13.6 1.3 %collective-permute-start.8 = (f32[128,256]{1,0:T(8,128)S(1)}, f32[128,256]{1,0:T(8,128)S(1)}, u32[]{:S(2)}, u32[]{:S(2)}) collective-permute-start(f32[128,256]{1,0:T(8,128)S(1)} %get-tuple-element.94._), channel_id=1, source_target_pairs={{8,16},{12,20},{9,17},{13,21},{10,18},{14,22},{11,19},{15,23}} | collective-permute-start | bytes 393224 | tf_op jit(solution)/shard_map/ppermute | solution.py:213
  14.9 2.7 %collective-permute-done.5.arrived_ref = f32[136,256]{1,0:T(8,128)S(1)} collective-permute-done((f32[136,256]{1,0:T(8,128)S(1)}, f32[136,256]{1,0:T(8,128)S(1)}, u32[]{:S(2)}, u32[]{:S(2)}) %collective-permute-start.5) | collective-permute-done | bytes 139296 | tf_op jit(solution)/shard_map/ppermute | solution.py:213
  17.6 1.3 %collective-permute-start.9 = (f32[136,256]{1,0:T(8,128)S(1)}, f32[136,256]{1,0:T(8,128)S(1)}, u32[]{:S(2)}, u32[]{:S(2)}) collective-permute-start(f32[136,256]{1,0:T(8,128)S(1)} %get-tuple-element.96._), channel_id=1, source_target_pairs={{16,24},{20,28},{17,25},{21,29},{18,26},{22,30},{19,27},{23,31}} | collective-permute-start | bytes 417800 | tf_op jit(solution)/shard_map/ppermute | solution.py:213
  19.0 0.7 %collective-permute-start.11 = (f32[128,256]{1,0:T(8,128)S(1)}, f32[128,256]{1,0:T(8,128)S(1)}, u32[]{:S(2)}, u32[]{:S(2)}) collective-permute-start(f32[128,256]{1,0:T(8,128)S(1)} %get-tuple-element.99._.totals_ref), channel_id=1, source_target_pairs={{0,8},{4,12},{1,9},{5,13},{2,10},{6,14},{3,11},{7,15}} | collective-permute-start | bytes 393224 | tf_op jit(solution)/shard_map/ppermute | solution.py:213
  19.7 1.3 %collective-permute-start.12 = (f32[128,256]{1,0:T(8,128)S(1)}, f32[128,256]{1,0:T(8,128)S(1)}, u32[]{:S(2)}, u32[]{:S(2)}) collective-permute-start(f32[128,256]{1,0:T(8,128)S(1)} %get-tuple-element.100._), channel_id=1, source_target_pairs={{8,16},{12,20},{9,17},{13,21},{10,18},{14,22},{11,19},{15,23}} | collective-permute-start | bytes 393224 | tf_op jit(solution)/shard_map/ppermute | solution.py:213
  21.0 1.5 %collective-permute-done.8.arrived_ref = f32[128,256]{1,0:T(8,128)S(1)} collective-permute-done((f32[128,256]{1,0:T(8,128)S(1)}, f32[128,256]{1,0:T(8,128)S(1)}, u32[]{:S(2)}, u32[]{:S(2)}) %collective-permute-start.8) | collective-permute-done | bytes 131104 | tf_op jit(solution)/shard_map/ppermute | solution.py:213
  22.5 1.3 %collective-permute-start.13 = (f32[128,256]{1,0:T(8,128)S(1)}, f32[128,256]{1,0:T(8,128)S(1)}, u32[]{:S(2)}, u32[]{:S(2)}) collective-permute-start(f32[128,256]{1,0:T(8,128)S(1)} %get-tuple-element.102._), channel_id=1, source_target_pairs={{16,24},{20,28},{17,25},{21,29},{18,26},{22,30},{19,27},{23,31}} | collective-permute-start | bytes 393224 | tf_op jit(solution)/shard_map/ppermute | solution.py:213
  23.9 1.3 %collective-permute-start.15 = (f32[128,256]{1,0:T(8,128)S(1)}, f32[128,256]{1,0:T(8,128)S(1)}, u32[]{:S(2)}, u32[]{:S(2)}) collective-permute-start(f32[128,256]{1,0:T(8,128)S(1)} %get-tuple-element.114._), channel_id=1, source_target_pairs={{8,16},{12,20},{9,17},{13,21},{10,18},{14,22},{11,19},{15,23}} | collective-permute-start | bytes 393224 | tf_op jit(solution)/shard_map/ppermute | solution.py:213
  25.2 1.7 %collective-permute-done.12.arrived_ref = f32[128,256]{1,0:T(8,128)S(1)} collective-permute-done((f32[128,256]{1,0:T(8,128)S(1)}, f32[128,256]{1,0:T(8,128)S(1)}, u32[]{:S(2)}, u32[]{:S(2)}) %collective-permute-start.12) | collective-permute-done | bytes 131104 | tf_op jit(solution)/shard_map/ppermute | solution.py:213
  26.9 1.3 %collective-permute-start.16 = (f32[128,256]{1,0:T(8,128)S(1)}, f32[128,256]{1,0:T(8,128)S(1)}, u32[]{:S(2)}, u32[]{:S(2)}) collective-permute-start(f32[128,256]{1,0:T(8,128)S(1)} %get-tuple-element.116._), channel_id=1, source_target_pairs={{16,24},{20,28},{17,25},{21,29},{18,26},{22,30},{19,27},{23,31}} | collective-permute-start | bytes 393224 | tf_op jit(solution)/shard_map/ppermute | solution.py:213
  28.2 2.5 %collective-permute-done.15.arrived_ref = f32[128,256]{1,0:T(8,128)S(1)} collective-permute-done((f32[128,256]{1,0:T(8,128)S(1)}, f32[128,256]{1,0:T(8,128)S(1)}, u32[]{:S(2)}, u32[]{:S(2)}) %collective-permute-start.15) | collective-permute-done | bytes 131104 | tf_op jit(solution)/shard_map/ppermute | solution.py:213
  30.8 1.3 %collective-permute-start.18 = (f32[128,256]{1,0:T(8,128)S(1)}, f32[128,256]{1,0:T(8,128)S(1)}, u32[]{:S(2)}, u32[]{:S(2)}) collective-permute-start(f32[128,256]{1,0:T(8,128)S(1)} %get-tuple-element.130._), channel_id=1, source_target_pairs={{16,24},{20,28},{17,25},{21,29},{18,26},{22,30},{19,27},{23,31}} | collective-permute-start | bytes 393224 | tf_op jit(solution)/shard_map/ppermute | solution.py:213
  32.1 1.3 %collective-permute-start.14 = (f32[128,256]{1,0:T(8,128)S(1)}, f32[128,256]{1,0:T(8,128)S(1)}, u32[]{:S(2)}, u32[]{:S(2)}) collective-permute-start(f32[128,256]{1,0:T(8,128)S(1)} %get-tuple-element.123._), channel_id=1, source_target_pairs={{0,4},{4,0},{8,12},{12,8},{16,20},{20,16},{24,28},{28,24},{1,5},{5... | collective-permute-start | bytes 393224 | tf_op jit(solution)/shard_map/ppermute | solution.py:215
  33.7 1.3 %collective-permute-start.17 = (f32[128,256]{1,0:T(8,128)S(1)}, f32[128,256]{1,0:T(8,128)S(1)}, u32[]{:S(2)}, u32[]{:S(2)}) collective-permute-start(f32[128,256]{1,0:T(8,128)S(1)} %get-tuple-element.137._), channel_id=1, source_target_pairs={{0,4},{4,0},{8,12},{12,8},{16,20},{20,16},{24,28},{28,24},{1,5},{5... | collective-permute-start | bytes 393224 | tf_op jit(solution)/shard_map/ppermute | solution.py:215
  36.1 1.0 %shard_map.55 = (f32[256,128]{1,0:T(8,128)S(1)}, f32[256,128]{1,0:T(8,128)S(1)}, bf16[256,256]{1,0:T(8,128)(2,1)S(1)}, f32[256,128]{1,0:T(8,128)S(1)}, f32[256,1...) custom-call(s32[1]{0:T(128)} %bitcast.first_ref, bf16[8,256]{1,0:T(8,128)(2,1)S(1)} %copy-done.3, ...), custom_call_target="tpu_custom_call" | custom-call | flops 167772160 | bytes 2363396 | tf_op jit(solution)/shard_map/pallas_call | solution.py:151
  37.1 1.0 %shard_map.69 = (f32[256,128]{1,0:T(8,128)S(1)}, f32[256,128]{1,0:T(8,128)S(1)}, bf16[256,256]{1,0:T(8,128)(2,1)S(1)}, f32[256,128]{1,0:T(8,128)S(1)}, f32[256,1...) custom-call(s32[1]{0:T(128)} %bitcast.first_ref, bf16[8,256]{1,0:T(8,128)(2,1)S(1)} %copy-done.3, ...), custom_call_target="tpu_custom_call" | custom-call | flops 167772160 | bytes 2363396 | tf_op jit(solution)/shard_map/pallas_call | solution.py:151
  38.1 1.0 %shard_map.74 = (f32[256,128]{1,0:T(8,128)S(1)}, f32[256,128]{1,0:T(8,128)S(1)}, bf16[256,256]{1,0:T(8,128)(2,1)S(1)}, f32[256,128]{1,0:T(8,128)S(1)}, f32[256,1...) custom-call(s32[1]{0:T(128)} %bitcast.first_ref, bf16[8,256]{1,0:T(8,128)(2,1)S(1)} %copy-done.3, ...), custom_call_target="tpu_custom_call" | custom-call | flops 167772160 | bytes 2363396 | tf_op jit(solution)/shard_map/pallas_call | solution.py:151
  39.1 1.0 %shard_map.78 = (f32[256,128]{1,0:T(8,128)S(1)}, f32[256,128]{1,0:T(8,128)S(1)}, bf16[256,256]{1,0:T(8,128)(2,1)S(1)}, f32[256,128]{1,0:T(8,128)S(1)}, f32[256,1...) custom-call(s32[1]{0:T(128)} %bitcast.first_ref, bf16[8,256]{1,0:T(8,128)(2,1)S(1)} %copy-done.3, ...), custom_call_target="tpu_custom_call" | custom-call | flops 167772160 | bytes 2363396 | tf_op jit(solution)/shard_map/pallas_call | solution.py:151
  42.0 7.0 %collective-permute-start.20 = (f32[8,256]{1,0:T(8,128)S(1)}, f32[8,256]{1,0:T(8,128)S(1)}, u32[]{:S(2)}, u32[]{:S(2)}) collective-permute-start(f32[8,256]{1,0:T(8,128)S(1)} %get-tuple-element.156.refs_8_), channel_id=1, source_target_pairs={{0,1},{1,2},{2,3},{3,0},{4,5},{5,6},{6,7},{7,4},{8,9},{9,10},{10,1... | collective-permute-start | bytes 24584 | tf_op jit(solution)/shard_map/ppermute | solution.py:239
  49.7 1.7 %collective-permute-done.21.refs_10_ = f32[8,256]{1,0:T(8,128)S(1)} collective-permute-done((f32[8,256]{1,0:T(8,128)S(1)}, f32[8,256]{1,0:T(8,128)S(1)}, u32[]{:S(2)}, u32[]{:S(2)}) %collective-permute-start.21) | collective-permute-done | bytes 8224 | tf_op jit(solution)/shard_map/ppermute | solution.py:239
  51.4 0.8 %collective-permute-done.22.refs_11_ = f32[8,256]{1,0:T(8,128)S(1)} collective-permute-done((f32[8,256]{1,0:T(8,128)S(1)}, f32[8,256]{1,0:T(8,128)S(1)}, u32[]{:S(2)}, u32[]{:S(2)}) %collective-permute-start.22) | collective-permute-done | bytes 8224 | tf_op jit(solution)/shard_map/ppermute | solution.py:239
  52.2 0.7 %copy-done.4 = f32[1024]{0:T(1024)S(1)} copy-done((f32[1024]{0:T(1024)S(1)}, f32[1024]{0:T(1024)}, u32[]{:S(2)}) %copy-start.4) | copy-done | bytes 4120
  52.9 1.1 %shard_map.81 = bf16[256,1024]{1,0:T(8,128)(2,1)} custom-call(s32[1]{0:T(128)} %bitcast.first_ref, f32[1,1024]{1,0:T(1,128)S(1)} %bitcast.4, f32[256,128]{1,0:T(8,128)S(1)} %get-tuple-element.110.refs_0_, f32[256,128]{1,0:T(8,128)S(1)} %get-tuple-element.125.refs_1_, f32[256,128]{1,0:T(8,128)S(1)} %get-tuple-element.139.refs_2_, ...), custom_call_target="tpu_custom_call" | custom-call | flops 786432 | bytes 1609732 | tf_op jit(solution)/shard_map/pallas_call | solution.py:151
  (55 shorter events, 5.5 us)
Async XLA Ops:
  0.0 4.5 %copy-start = (bf16[256,1024]{1,0:T(8,128)(2,1)S(1)}, bf16[256,1024]{1,0:T(8,128)(2,1)}, u32[]{:S(2)}) copy-start(bf16[256,1024]{1,0:T(8,128)(2,1)} %k_ref.7) | copy-start | bytes 1572868
  0.0 4.5 %copy-start.1 = (bf16[256,1024]{1,0:T(8,128)(2,1)S(1)}, bf16[256,1024]{1,0:T(8,128)(2,1)}, u32[]{:S(2)}) copy-start(bf16[256,1024]{1,0:T(8,128)(2,1)} %v_ref.7) | copy-start | bytes 1572868
  2.9 1.6 %copy-start.3 = (bf16[8,256]{1,0:T(8,128)(2,1)S(1)}, bf16[8,256]{1,0:T(8,128)(2,1)}, u32[]{:S(2)}) copy-start(bf16[8,256]{1,0:T(8,128)(2,1)} %seeds_ref.7) | copy-start | bytes 12292
  2.9 4.8 %collective-permute-start = (f32[136,256]{1,0:T(8,128)}, f32[136,256]{1,0:T(8,128)S(1)}, u32[]{:S(2)}, u32[]{:S(2)}) collective-permute-start(f32[136,256]{1,0:T(8,128)} %get-tuple-element.85), channel_id=1, source_target_pairs={{0,4},{4,0},{8,12},{12,8},{16,20},{20,16},{24,28},{28,24},{1,5},{5... | collective-permute-start | bytes 417800 | tf_op jit(solution)/shard_map/ppermute | solution.py:192
  4.2 6.3 %collective-permute-start.1 = (f32[128,256]{1,0:T(8,128)}, f32[128,256]{1,0:T(8,128)S(1)}, u32[]{:S(2)}, u32[]{:S(2)}) collective-permute-start(f32[128,256]{1,0:T(8,128)} %get-tuple-element.88), channel_id=1, source_target_pairs={{0,4},{4,0},{8,12},{12,8},{16,20},{20,16},{24,28},{28,24},{1,5},{5... | collective-permute-start | bytes 393224 | tf_op jit(solution)/shard_map/ppermute | solution.py:192
  7.7 0.9 %copy-start.6 = (f32[128,256]{1,0:T(8,128)S(1)}, f32[128,256]{1,0:T(8,128)}, u32[]{:S(2)}) copy-start(f32[128,256]{1,0:T(8,128)} %get-tuple-element.92) | copy-start | bytes 393220
  7.7 2.1 %copy-start.5 = (f32[128,256]{1,0:T(8,128)S(1)}, f32[128,256]{1,0:T(8,128)}, u32[]{:S(2)}) copy-start(f32[128,256]{1,0:T(8,128)} %get-tuple-element.98) | copy-start | bytes 393220
  7.8 3.5 %collective-permute-start.2 = (f32[136,256]{1,0:T(8,128)S(1)}, f32[136,256]{1,0:T(8,128)S(1)}, u32[]{:S(2)}, u32[]{:S(2)}) collective-permute-start(f32[136,256]{1,0:T(8,128)S(1)} %get-tuple-element.86._.totals_ref), channel_id=1, source_target_pairs={{0,8},{4,12},{1,9},{5,13},{2,10},{6,14},{3,11},{7,15}} | collective-permute-start | bytes 417800 | tf_op jit(solution)/shard_map/ppermute | solution.py:213
  8.6 4.2 %collective-permute-start.3 = (f32[128,256]{1,0:T(8,128)S(1)}, f32[128,256]{1,0:T(8,128)S(1)}, u32[]{:S(2)}, u32[]{:S(2)}) collective-permute-start(f32[128,256]{1,0:T(8,128)S(1)} %copy-done.6), channel_id=1, source_target_pairs={{0,4},{4,0},{8,12},{12,8},{16,20},{20,16},{24,28},{28,24},{1,5},{5... | collective-permute-start | bytes 393224 | tf_op jit(solution)/shard_map/ppermute | solution.py:192
  9.9 9.1 %collective-permute-start.6 = (f32[128,256]{1,0:T(8,128)S(1)}, f32[128,256]{1,0:T(8,128)S(1)}, u32[]{:S(2)}, u32[]{:S(2)}) collective-permute-start(f32[128,256]{1,0:T(8,128)S(1)} %copy-done.5), channel_id=1, source_target_pairs={{0,4},{4,0},{8,12},{12,8},{16,20},{20,16},{24,28},{28,24},{1,5},{5... | collective-permute-start | bytes 393224 | tf_op jit(solution)/shard_map/ppermute | solution.py:192
  10.6 3.0 %collective-permute-start.4 = (f32[128,256]{1,0:T(8,128)S(1)}, f32[128,256]{1,0:T(8,128)S(1)}, u32[]{:S(2)}, u32[]{:S(2)}) collective-permute-start(f32[128,256]{1,0:T(8,128)S(1)} %get-tuple-element.89._.totals_ref), channel_id=1, source_target_pairs={{0,8},{4,12},{1,9},{5,13},{2,10},{6,14},{3,11},{7,15}} | collective-permute-start | bytes 393224 | tf_op jit(solution)/shard_map/ppermute | solution.py:213
  11.3 6.3 %collective-permute-start.5 = (f32[136,256]{1,0:T(8,128)S(1)}, f32[136,256]{1,0:T(8,128)S(1)}, u32[]{:S(2)}, u32[]{:S(2)}) collective-permute-start(f32[136,256]{1,0:T(8,128)S(1)} %get-tuple-element.90._), channel_id=1, source_target_pairs={{8,16},{12,20},{9,17},{13,21},{10,18},{14,22},{11,19},{15,23}} | collective-permute-start | bytes 417800 | tf_op jit(solution)/shard_map/ppermute | solution.py:213
  12.8 6.8 %collective-permute-start.7 = (f32[128,256]{1,0:T(8,128)S(1)}, f32[128,256]{1,0:T(8,128)S(1)}, u32[]{:S(2)}, u32[]{:S(2)}) collective-permute-start(f32[128,256]{1,0:T(8,128)S(1)} %get-tuple-element.93._.totals_ref), channel_id=1, source_target_pairs={{0,8},{4,12},{1,9},{5,13},{2,10},{6,14},{3,11},{7,15}} | collective-permute-start | bytes 393224 | tf_op jit(solution)/shard_map/ppermute | solution.py:213
  13.6 8.9 %collective-permute-start.8 = (f32[128,256]{1,0:T(8,128)S(1)}, f32[128,256]{1,0:T(8,128)S(1)}, u32[]{:S(2)}, u32[]{:S(2)}) collective-permute-start(f32[128,256]{1,0:T(8,128)S(1)} %get-tuple-element.94._), channel_id=1, source_target_pairs={{8,16},{12,20},{9,17},{13,21},{10,18},{14,22},{11,19},{15,23}} | collective-permute-start | bytes 393224 | tf_op jit(solution)/shard_map/ppermute | solution.py:213
  17.6 6.2 %collective-permute-start.9 = (f32[136,256]{1,0:T(8,128)S(1)}, f32[136,256]{1,0:T(8,128)S(1)}, u32[]{:S(2)}, u32[]{:S(2)}) collective-permute-start(f32[136,256]{1,0:T(8,128)S(1)} %get-tuple-element.96._), channel_id=1, source_target_pairs={{16,24},{20,28},{17,25},{21,29},{18,26},{22,30},{19,27},{23,31}} | collective-permute-start | bytes 417800 | tf_op jit(solution)/shard_map/ppermute | solution.py:213
  19.0 4.9 %collective-permute-start.11 = (f32[128,256]{1,0:T(8,128)S(1)}, f32[128,256]{1,0:T(8,128)S(1)}, u32[]{:S(2)}, u32[]{:S(2)}) collective-permute-start(f32[128,256]{1,0:T(8,128)S(1)} %get-tuple-element.99._.totals_ref), channel_id=1, source_target_pairs={{0,8},{4,12},{1,9},{5,13},{2,10},{6,14},{3,11},{7,15}} | collective-permute-start | bytes 393224 | tf_op jit(solution)/shard_map/ppermute | solution.py:213
  19.7 7.1 %collective-permute-start.12 = (f32[128,256]{1,0:T(8,128)S(1)}, f32[128,256]{1,0:T(8,128)S(1)}, u32[]{:S(2)}, u32[]{:S(2)}) collective-permute-start(f32[128,256]{1,0:T(8,128)S(1)} %get-tuple-element.100._), channel_id=1, source_target_pairs={{8,16},{12,20},{9,17},{13,21},{10,18},{14,22},{11,19},{15,23}} | collective-permute-start | bytes 393224 | tf_op jit(solution)/shard_map/ppermute | solution.py:213
  22.5 5.7 %collective-permute-start.13 = (f32[128,256]{1,0:T(8,128)S(1)}, f32[128,256]{1,0:T(8,128)S(1)}, u32[]{:S(2)}, u32[]{:S(2)}) collective-permute-start(f32[128,256]{1,0:T(8,128)S(1)} %get-tuple-element.102._), channel_id=1, source_target_pairs={{16,24},{20,28},{17,25},{21,29},{18,26},{22,30},{19,27},{23,31}} | collective-permute-start | bytes 393224 | tf_op jit(solution)/shard_map/ppermute | solution.py:213
  23.9 6.9 %collective-permute-start.15 = (f32[128,256]{1,0:T(8,128)S(1)}, f32[128,256]{1,0:T(8,128)S(1)}, u32[]{:S(2)}, u32[]{:S(2)}) collective-permute-start(f32[128,256]{1,0:T(8,128)S(1)} %get-tuple-element.114._), channel_id=1, source_target_pairs={{8,16},{12,20},{9,17},{13,21},{10,18},{14,22},{11,19},{15,23}} | collective-permute-start | bytes 393224 | tf_op jit(solution)/shard_map/ppermute | solution.py:213
  26.9 6.8 %collective-permute-start.16 = (f32[128,256]{1,0:T(8,128)S(1)}, f32[128,256]{1,0:T(8,128)S(1)}, u32[]{:S(2)}, u32[]{:S(2)}) collective-permute-start(f32[128,256]{1,0:T(8,128)S(1)} %get-tuple-element.116._), channel_id=1, source_target_pairs={{16,24},{20,28},{17,25},{21,29},{18,26},{22,30},{19,27},{23,31}} | collective-permute-start | bytes 393224 | tf_op jit(solution)/shard_map/ppermute | solution.py:213
  30.8 4.2 %collective-permute-start.18 = (f32[128,256]{1,0:T(8,128)S(1)}, f32[128,256]{1,0:T(8,128)S(1)}, u32[]{:S(2)}, u32[]{:S(2)}) collective-permute-start(f32[128,256]{1,0:T(8,128)S(1)} %get-tuple-element.130._), channel_id=1, source_target_pairs={{16,24},{20,28},{17,25},{21,29},{18,26},{22,30},{19,27},{23,31}} | collective-permute-start | bytes 393224 | tf_op jit(solution)/shard_map/ppermute | solution.py:213
  32.1 8.5 %collective-permute-start.14 = (f32[128,256]{1,0:T(8,128)S(1)}, f32[128,256]{1,0:T(8,128)S(1)}, u32[]{:S(2)}, u32[]{:S(2)}) collective-permute-start(f32[128,256]{1,0:T(8,128)S(1)} %get-tuple-element.123._), channel_id=1, source_target_pairs={{0,4},{4,0},{8,12},{12,8},{16,20},{20,16},{24,28},{28,24},{1,5},{5... | collective-permute-start | bytes 393224 | tf_op jit(solution)/shard_map/ppermute | solution.py:215
  33.5 6.6 %collective-permute-start.10 = (f32[136,256]{1,0:T(8,128)S(1)}, f32[136,256]{1,0:T(8,128)S(1)}, u32[]{:S(2)}, u32[]{:S(2)}) collective-permute-start(f32[136,256]{1,0:T(8,128)S(1)} %get-tuple-element.109._), channel_id=1, source_target_pairs={{0,4},{4,0},{8,12},{12,8},{16,20},{20,16},{24,28},{28,24},{1,5},{5... | collective-permute-start | bytes 417800 | tf_op jit(solution)/shard_map/ppermute | solution.py:215
  33.7 7.4 %collective-permute-start.17 = (f32[128,256]{1,0:T(8,128)S(1)}, f32[128,256]{1,0:T(8,128)S(1)}, u32[]{:S(2)}, u32[]{:S(2)}) collective-permute-start(f32[128,256]{1,0:T(8,128)S(1)} %get-tuple-element.137._), channel_id=1, source_target_pairs={{0,4},{4,0},{8,12},{12,8},{16,20},{20,16},{24,28},{28,24},{1,5},{5... | collective-permute-start | bytes 393224 | tf_op jit(solution)/shard_map/ppermute | solution.py:215
  35.0 1.0 %copy-start.2 = (bf16[256,1024]{1,0:T(8,128)(2,1)S(1)}, bf16[256,1024]{1,0:T(8,128)(2,1)}, u32[]{:S(2)}) copy-start(bf16[256,1024]{1,0:T(8,128)(2,1)} %q_ref.7) | copy-start | bytes 1572868
  35.1 6.4 %collective-permute-start.19 = (f32[128,256]{1,0:T(8,128)S(1)}, f32[128,256]{1,0:T(8,128)S(1)}, u32[]{:S(2)}, u32[]{:S(2)}) collective-permute-start(f32[128,256]{1,0:T(8,128)S(1)} %get-tuple-element.149), channel_id=1, source_target_pairs={{0,4},{4,0},{8,12},{12,8},{16,20},{20,16},{24,28},{28,24},{1,5},{5... | collective-permute-start | bytes 393224 | tf_op jit(solution)/shard_map/ppermute | solution.py:215
  42.0 7.8 %collective-permute-start.20 = (f32[8,256]{1,0:T(8,128)S(1)}, f32[8,256]{1,0:T(8,128)S(1)}, u32[]{:S(2)}, u32[]{:S(2)}) collective-permute-start(f32[8,256]{1,0:T(8,128)S(1)} %get-tuple-element.156.refs_8_), channel_id=1, source_target_pairs={{0,1},{1,2},{2,3},{3,0},{4,5},{5,6},{6,7},{7,4},{8,9},{9,10},{10,1... | collective-permute-start | bytes 24584 | tf_op jit(solution)/shard_map/ppermute | solution.py:239
  48.9 2.5 %collective-permute-start.21 = (f32[8,256]{1,0:T(8,128)S(1)}, f32[8,256]{1,0:T(8,128)S(1)}, u32[]{:S(2)}, u32[]{:S(2)}) collective-permute-start(f32[8,256]{1,0:T(8,128)S(1)} %get-tuple-element.156.refs_8_), channel_id=1, source_target_pairs={{0,2},{1,3},{2,0},{3,1},{4,6},{5,7},{6,4},{7,5},{8,10},{9,11},{10,... | collective-permute-start | bytes 24584 | tf_op jit(solution)/shard_map/ppermute | solution.py:239
  49.2 3.1 %collective-permute-start.22 = (f32[8,256]{1,0:T(8,128)S(1)}, f32[8,256]{1,0:T(8,128)S(1)}, u32[]{:S(2)}, u32[]{:S(2)}) collective-permute-start(f32[8,256]{1,0:T(8,128)S(1)} %get-tuple-element.156.refs_8_), channel_id=1, source_target_pairs={{0,3},{1,0},{2,1},{3,2},{4,7},{5,4},{6,5},{7,6},{8,11},{9,8},{10,9... | collective-permute-start | bytes 24584 | tf_op jit(solution)/shard_map/ppermute | solution.py:239
  52.2 0.7 %copy-start.4 = (f32[1024]{0:T(1024)S(1)}, f32[1024]{0:T(1024)}, u32[]{:S(2)}) copy-start(f32[1024]{0:T(1024)} %param.9) | copy-start | bytes 12292

commit v3 on v1

v3 whole, which is shorter than its diff:
```python
import functools

import jax
import jax.numpy as jnp
from jax import lax
from jax.experimental import pallas as pl
from jax.experimental.pallas import tpu as pltpu
from jax.sharding import PartitionSpec as P

WIDTH = 128
MIB = 2**20
DIRECTS = (1, 1)
CROSSES = ()
PARTS = 3
GLUE_COST = 10**9
GAP = 2.1
ORDER = None


NT = (((1,), (1,)), ((), ()))
TN = (((0,), (0,)), ((), ()))
VMEM = pl.BlockSpec(memory_space=pltpu.VMEM)
HBM = pl.BlockSpec(memory_space=pltpu.HBM)
ANY = pl.BlockSpec(memory_space=pl.ANY)
SMEM = pl.BlockSpec(memory_space=pltpu.SMEM)


def first_of(group, half, mine_ref):
    side = lax.rem(mine_ref[0], 2)
    return half * (side if group == 0 else 1 - side)


def rotated(seeds, first):
    heads = seeds.shape[0]
    return pltpu.roll(seeds, lax.rem(heads - first, heads), 0)


def table_of(row):
    square = jnp.broadcast_to(row, (WIDTH, WIDTH))
    return pltpu.roll(square, 0, 1, stride=1, stride_axis=0).astype(jnp.bfloat16)


def phi(x, table):
    mixed = jnp.dot(x, table, preferred_element_type=jnp.float32) * WIDTH ** (-0.25)
    return (jnp.exp(jnp.minimum(mixed, 0.0)) + jnp.maximum(mixed, 0.0)).astype(jnp.bfloat16)


def features(x, seeds, i):
    groups = seeds.shape[1] // WIDTH
    rows = [seeds[i : i + 1, g * WIDTH : (g + 1) * WIDTH] for g in range(groups)]
    return jnp.concatenate([phi(x, table_of(row)) for row in rows], axis=1)


def columns(head):
    if isinstance(head, int):
        return slice(head * WIDTH, (head + 1) * WIDTH)
    return pl.ds(pl.multiple_of(head * WIDTH, WIDTH), WIDTH)


def bounds(heads, parts):
    rows = heads * WIDTH
    cuts = [rows * n // parts // 8 * 8 for n in range(parts + 1)]
    return list(zip(cuts, cuts[1:]))


def overlaps(cuts, head):
    found = []
    for n, (low, high) in enumerate(cuts):
        start, stop = max(low, head * WIDTH), min(high, (head + 1) * WIDTH)
        if start < stop:
            found.append((n, slice(start - low, stop - low), slice(start, stop)))
    return found


def put_states(outs, cuts, seeds, base, at, k_ref, v_ref):
    size = cuts[0][1]
    outs[0][size:, :] = jnp.zeros((outs[0].shape[0] - size, outs[0].shape[1]), jnp.float32)
    for i in range(cuts[-1][1] // WIDTH):
        fk = features(k_ref[:, columns(at + i)], seeds, base + at + i)
        state = lax.dot_general(
            v_ref[:, columns(at + i)], fk, TN, preferred_element_type=jnp.float32
        )
        for n, rows, whole in overlaps(cuts, i):
            outs[n][rows, :] = state[whole.start - i * WIDTH : whole.stop - i * WIDTH, :]
        outs[0][size + i : size + i + 1, :] = jnp.sum(
            fk.astype(jnp.float32), axis=0, keepdims=True
        )


def state_kernel(singles, cuts, which, places_ref, seeds_hbm, k_hbm, v_hbm, *refs):
    extra, refs = (refs[:1], refs[1:]) if which == 0 else ((), refs)
    half = cuts[-1][1] // WIDTH
    alone = sum(singles)
    outs, refs = refs[: len(singles) + len(cuts)], refs[len(singles) + len(cuts) :]
    gain_ref, refs = (refs[0], refs[1:]) if which == 0 else (None, refs)
    seeds_ref, k_ref, v_ref, kd_ref, vd_ref, sems = refs
    first = first_of(which, half, places_ref)
    span = pl.ds(pl.multiple_of(first * WIDTH, WIDTH), half * WIDTH)
    rest = pl.ds(2 * half * WIDTH, kd_ref.shape[1])
    pairs = [(seeds_hbm, seeds_ref)]
    if alone:
        pairs += [(k_hbm.at[:, rest], kd_ref), (v_hbm.at[:, rest], vd_ref)]
    pairs += [(gain_hbm, gain_ref) for gain_hbm in extra]
    pairs += [(k_hbm.at[:, span], k_ref), (v_hbm.at[:, span], v_ref)]
    copies = [pltpu.make_async_copy(a, b, sems.at[n]) for n, (a, b) in enumerate(pairs)]
    for copy in copies:
        copy.start()
    copies[0].wait()
    seeds = seeds_ref[...].astype(jnp.float32)
    if alone:
        copies[1].wait()
        copies[2].wait()
        at = 0
        for n, size in enumerate(singles):
            put_states([outs[n]], bounds(size, 1), seeds, 2 * half, at, kd_ref, vd_ref)
            at += size
    for copy in copies[3 if alone else 1 :]:
        copy.wait()
    put_states(outs[len(singles) :], cuts, rotated(seeds, first), 0, 0, k_ref, v_ref)


def local_kernel(half, work, places_ref, _, seeds_ref, q_ref, k_ref, v_ref, *outs):
    tok = q_ref.shape[0]
    seeds = seeds_ref[...].astype(jnp.float32)
    rows = lax.broadcasted_iota(jnp.int32, (tok, tok), 0)
    causal = lax.broadcasted_iota(jnp.int32, (tok, tok), 1) <= rows
    for n, (group, i) in enumerate(work):
        num_ref, den_ref, fq_ref = outs[3 * n : 3 * n + 3]
        if group == 2:
            head, mine, i = 2 * half + i, seeds, 2 * half + i
        else:
            first = first_of(group, half, places_ref)
            head, mine = first + i, rotated(seeds, first)
        fk = features(k_ref[:, columns(head)], mine, i)
        fq = features(q_ref[:, columns(head)], mine, i)
        fq_ref[...] = fq
        scores = lax.dot_general(fq, fk, NT, preferred_element_type=jnp.float32)
        scores = jnp.where(causal, scores, 0.0)
        num_ref[...] = jnp.dot(
            scores.astype(jnp.bfloat16),
            v_ref[:, columns(head)],
            preferred_element_type=jnp.float32,
        )
        den_ref[...] = jnp.broadcast_to(jnp.sum(scores, axis=1, keepdims=True), (tok, WIDTH))


def send_kernel(places_ref, _, *refs):
    refs[-1][...] = functools.reduce(lambda a, b: a + b, [ref[...] for ref in refs[:-1]])


def pass_kernel(levels, crossed, places_ref, _, *refs):
    arrived, refs = refs[:levels], refs[levels:]
    own_ref = refs[-1]
    sent_ref, ours = (None, refs[:-1]) if crossed else (refs[-2], refs[:-2])
    prior = jnp.zeros(own_ref.shape, jnp.float32)
    for n, ref in enumerate(arrived):
        level = lax.div(places_ref[0], 2)
        prior = jnp.where(level == n + 1, ref[0 : prior.shape[0], :], prior)
    right = lax.rem(places_ref[0], 2) == 1
    if sent_ref is not None:
        sent_ref[...] = prior + jnp.where(right, 0.0, ours[0][...])
    own_ref[...] = prior + jnp.where(right, ours[1][...], 0.0) if len(ours) > 1 else prior


def join_kernel(half, work, places_ref, _, gain_ref, *refs):
    count = len(work)
    heads_refs, squares_ref = refs[-count - 1 : -1], refs[-1]
    squares = jnp.zeros(heads_refs[0].shape, jnp.float32)
    for (group, i, cuts, n, copies), out_ref in zip(work, heads_refs):
        num_ref, den_ref, fq_ref = refs[:3]
        state, total = 0.0, 0.0
        for _ in range(copies):
            parts = refs[3 : 3 + len(cuts)]
            refs = refs[:3] + refs[3 + len(cuts) :]
            rows = [parts[m][at, :] for m, at, _ in overlaps(cuts, n)]
            state = state + (rows[0] if len(rows) == 1 else jnp.concatenate(rows, axis=0))
            total = total + parts[0][cuts[0][1] + n : cuts[0][1] + n + 1, :]
        refs = refs[3:]
        wide = jnp.concatenate([state, jnp.broadcast_to(total, state.shape)], axis=0)
        upper = wide.astype(jnp.bfloat16)
        lower = (wide - upper.astype(jnp.float32)).astype(jnp.bfloat16)
        fq = fq_ref[...]
        both = lax.dot_general(fq, upper, NT, preferred_element_type=jnp.float32)
        both = both + lax.dot_general(fq, lower, NT, preferred_element_type=jnp.float32)
        head = (num_ref[...] + both[:, :WIDTH]) / (den_ref[...] + both[:, WIDTH:])
        place = 2 * half + i if group == 2 else first_of(group, half, places_ref) + i
        out_ref[...] = head * gain_ref[:, columns(place)]
        squares = squares + head * head
    rows = jnp.broadcast_to(jnp.sum(squares, axis=1, keepdims=True), squares.shape)
    squares_ref[...] = rows.T[0:8, :]
    if len(refs) > count + 1:
        squares_ref[...] += refs[0][...]


def norm_kernel(half, entries, work, places_ref, *refs):
    heads, squares, out_ref = refs[: len(work)], refs[len(work) : -1], refs[-1]
    tok = out_ref.shape[0]
    overall = functools.reduce(lambda a, b: a + b, [ref[...] for ref in squares])
    factor = lax.rsqrt(overall / entries + 1e-06)
    wide = jnp.broadcast_to(factor[0:1, :], (WIDTH, tok)).T
    for (group, i), source in zip(work, heads):
        place = 2 * half + i if group == 2 else first_of(group, half, places_ref) + i
        out_ref[:, columns(place)] = (source[...] * wide).astype(jnp.bfloat16)


def call(kernel, outs, ins, flops, scratch=(), specs=(), place=VMEM, limit=16 * MIB):
    moved = sum(x.size * x.dtype.itemsize for x in ins)
    moved += sum(x.size * jnp.dtype(x.dtype).itemsize for x in jax.tree.leaves(outs))
    return pl.pallas_call(
        kernel,
        out_shape=outs,
        in_specs=[SMEM, *specs] + [place] * (len(ins) - 1 - len(specs)),
        out_specs=jax.tree.map(lambda _: VMEM, outs),
        scratch_shapes=list(scratch),
        compiler_params=pltpu.CompilerParams(vmem_limit_bytes=limit),
        cost_estimate=pl.CostEstimate(flops=flops, bytes_accessed=moved, transcendentals=0),
    )(*ins)


def per_device(queries, keys, values, seeds, gain):
    f32, bf16 = jnp.float32, jnp.bfloat16
    tok = queries.shape[0]
    heads, feats = seeds.shape
    singles = DIRECTS + CROSSES
    alone = sum(singles)
    half = (heads - alone) // 2
    count = lax.axis_size("seq")
    depth = count // 2
    across = lax.axis_size("tp")
    mine = lax.axis_index("seq")
    places = mine.reshape(1)
    shape = lambda *dims, dtype=f32: jax.ShapeDtypeStruct(dims, dtype)
    cuts = bounds(half, PARTS)

    def state_shapes(cuts):
        return [shape(b - a + (8 if a == 0 else 0), feats) for a, b in cuts]

    def states(singles, which, limit):
        part = pltpu.VMEM((tok, half * WIDTH), keys.dtype)
        rest = pltpu.VMEM((tok, max(1, alone) * WIDTH), keys.dtype)
        return call(
            functools.partial(state_kernel, singles, cuts, which),
            [x for size in singles for x in state_shapes(bounds(size, 1))]
            + state_shapes(cuts)
            + ([shape(1, heads * WIDTH)] if which == 0 else []),
            (places, seeds, keys, values, *([gain.reshape(1, -1)] if which == 0 else [])),
            (sum(singles) + half) * tok * feats * WIDTH * 4,
            [pltpu.VMEM(seeds.shape, seeds.dtype), part, part, rest, rest]
            + [pltpu.SemaphoreType.DMA((5,))],
            place=HBM,
            limit=limit,
        )

    swap = [(i, i ^ 1) for i in range(count)]
    first = states(singles, 1, 60 * MIB)
    direct, cross = first[: len(DIRECTS)], first[len(DIRECTS) : len(singles)]
    theirs = first[len(singles) :]
    incoming = [lax.ppermute(part, "seq", swap) for part in [*theirs, *cross]]
    *ours, gain = states((), 0, 40 * MIB)
    chunks = [*[(part,) for part in direct], *zip([*ours, *cross], incoming)]
    total = len(chunks)
    locals_, arrivals, own, passed = {}, {}, [None] * total, [None] * total
    work = [[(2, i) for i in range(alone)][n : n + 2] for n in range(0, alone, 2)]
    work += [[(0, i), (1, i)] for i in range(half)]
    homes = [(n, i) for n, size in enumerate(singles) for i in range(size)]
    last = places

    def hop(stage, i):
        nonlocal last
        parts = chunks[i] if stage == 1 else (arrivals[stage - 1, i], *chunks[i])
        sent = parts[0]
        if len(parts) > 1:
            sent = call(
                send_kernel,
                shape(*sent.shape),
                (places, last, *parts),
                GLUE_COST,
                specs=[ANY],
            )
            last = sent
        pairs = [(2 * stage - 2 + s, 2 * stage + s) for s in range(2)]
        arrivals[stage, i] = lax.ppermute(sent, "seq", pairs)

    def hand(i):
        nonlocal last
        crossed = i >= len(DIRECTS) + PARTS
        like = shape(*chunks[i][0].shape)
        came = [arrivals[z, i] for z in range(1, depth)]
        *sent, own[i] = call(
            functools.partial(pass_kernel, depth - 1, crossed),
            [like] if crossed else [like, like],
            (places, last, *came, *chunks[i]),
            GLUE_COST,
            specs=[ANY],
        )
        last = own[i] if crossed else sent[0]
        if not crossed:
            passed[i] = lax.ppermute(last, "seq", swap)

    def local(piece):
        nonlocal last
        shapes = [shape(tok, WIDTH), shape(tok, WIDTH), shape(tok, feats, dtype=bf16)]
        parts = call(
            functools.partial(local_kernel, half, work[piece]),
            shapes * len(work[piece]),
            (places, last, seeds, queries, keys, values),
            len(work[piece]) * tok * (feats * WIDTH * 4 + tok * (feats + WIDTH) * 2),
            specs=[ANY],
        )
        last = parts[0]
        for n, key in enumerate(work[piece]):
            locals_[key] = parts[3 * n : 3 * n + 3]

    results, squares = {}, None

    def join(todo):
        nonlocal last, squares
        plan, ins = [], []
        for group, i in todo:
            if group == 2:
                n, at = homes[i]
                plan.append((2, i, bounds(singles[n], 1), at, 2 if n < len(DIRECTS) else 1))
                if n < len(DIRECTS):
                    arrays = [own[n], passed[n]]
                else:
                    arrays = [own[n + PARTS]]
            else:
                arrays = (own if group == 0 else passed)[len(DIRECTS) : len(DIRECTS) + PARTS]
                used = max(n for n, _, _ in overlaps(cuts, i)) + 1
                plan.append((group, i, cuts[:used], i, 1))
                arrays = arrays[:used]
            ins += [*locals_[group, i], *arrays]
        *outs, squares = call(
            functools.partial(join_kernel, half, plan),
            [shape(tok, WIDTH)] * len(todo) + [shape(8, tok)],
            (places, last, gain, *ins, *([] if squares is None else [squares])),
            len(todo) * tok * feats * WIDTH * 8,
            specs=[ANY],
        )
        last = squares
        results.update(zip(todo, outs))

    hops = [
        (i + GAP * (stage - 1), stage, i) for stage in range(1, depth + 1) for i in range(total)
    ]
    order = [("X" if stage == depth else stage, i) for _, stage, i in sorted(hops)]
    if ORDER and depth == 4 and total == 5:
        order = ORDER
    singles_done = [(2, i) for i in range(alone)]
    rest = [("L", i) for i in range(len(work))]
    rest += [("J", singles_done), ("J", [(0, i) for i in range(half)])]
    rest += [("J", [(1, i) for i in range(half - 1)]), ("J", [(1, half - 1)])]
    for kind, i in [*order, *rest]:
        if kind == "X":
            hand(i)
        elif kind == "L":
            if work[i][0] not in locals_:
                local(i)
        elif kind == "J":
            if i and i[0] not in results:
                join(i)
        else:
            hop(kind, i)
    gathered = [squares] + [
        lax.ppermute(squares, "tp", [(i, (i ^ k) if across == 4 else (i + k) % across) for i in range(across)])
        for k in range(1, across)
    ]
    return call(
        functools.partial(norm_kernel, half, heads * WIDTH * across, list(results)),
        shape(tok, heads * WIDTH, dtype=bf16),
        (places, *results.values(), *gathered),
        tok * heads * WIDTH * 3,
    )


def solution(mesh):
    placed = (P("seq", "tp"), P("seq", "tp"), P("seq", "tp"), P("tp", None), P("tp"))
    return jax.shard_map(
        per_device, mesh=mesh, in_specs=placed, out_specs=P("seq", "tp"), check_vma=False
    )
```

time: 59 us -> 49.5 us (0.84)
  the two profiles are of different devices: /device:TPU:16 before, /device:TPU:17 now
where the time goes in v3:
time: 49.5 us; the launch traced here: 48.9 us
  starting transfers between devices  29.3 us (59%)
  Pallas kernels  11.7 us (24%)
  waiting for transfers between devices  7.25 us (15%)
    ppermute x15, starting transfers between devices, hop(): arrivals[stage, i] = lax.ppermute(sent, 'seq', pairs)  18 us
    pallas_call x29, Pallas kernels, call(): pl.pallas_call(kernel, out_shape=outs, in_specs=[SMEM, *specs] + [place]...  11.7 us
    ppermute x3, starting transfers between devices, per_device(): lax.ppermute(squares, 'tp', [(i, i ^ k if across == 4 else (i + k) % acro...  5.12 us
    ppermute x15, waiting for transfers between devices, hop(): arrivals[stage, i] = lax.ppermute(sent, 'seq', pairs)  3.6 us
    ppermute x5, starting transfers between devices, hand(): passed[i] = lax.ppermute(last, 'seq', swap)  3.45 us
    ppermute x3, starting transfers between devices, per_device(): incoming = [lax.ppermute(part, 'seq', swap) for part in [*theirs, *cross]]  2.81 us
    ppermute x3, waiting for transfers between devices, per_device(): lax.ppermute(squares, 'tp', [(i, i ^ k if across == 4 else (i + k) % acro...  2.03 us
  transfers between devices with their start and end apart: 26, of which 9 were waited for; matrix products, arithmetic and copies ran while one was open for 0% of the time, Pallas kernels for 14%

profile of v3, /device:TPU:17, one launch (start us, length us, event | category | flops | bytes accessed | tf_op | source)
XLA Modules:
  0.0 48.9 jit_solution(4501948663524815681)
XLA Ops:
  0.0 3.3 %shard_map.56 = (f32[136,256]{1,0:T(8,128)}, f32[136,256]{1,0:T(8,128)}, f32[136,256]{1,0:T(8,128)}, f32[128,256]{1,0:T(8,128)}, f32[128,256]{1,0:T(8,128)}) custom-call(s32[1]{0:T(128)} %bitcast.places_ref._, bf16[8,256]{1,0:T(8,128)(2,1)} %seeds_ref.7, bf16[256,1024]{1,0:T(8,128)(2,1)} %k_ref.7, bf16[256,1024]{1,0:T(8,128)(2,1)} %v_ref.7), custom_call_target="tpu_custom_call" | custom-call | flops 167772160 | bytes 1732612 | tf_op jit(solution)/shard_map/pallas_call | solution.py:209
  3.3 1.3 %collective-permute-start = (f32[136,256]{1,0:T(8,128)}, f32[136,256]{1,0:T(8,128)S(1)}, u32[]{:S(2)}, u32[]{:S(2)}) collective-permute-start(f32[136,256]{1,0:T(8,128)} %get-tuple-element.61), channel_id=1, source_target_pairs={{0,4},{4,0},{8,12},{12,8},{16,20},{20,16},{24,28},{28,24},{1,5},{5... | collective-permute-start | bytes 417800 | tf_op jit(solution)/shard_map/ppermute | solution.py:258
  4.6 0.8 %collective-permute-start.1 = (f32[136,256]{1,0:T(8,128)}, f32[136,256]{1,0:T(8,128)S(1)}, u32[]{:S(2)}, u32[]{:S(2)}) collective-permute-start(f32[136,256]{1,0:T(8,128)} %get-tuple-element.62.refs_1_.refs_3_), channel_id=1, source_target_pairs={{0,8},{4,12},{1,9},{5,13},{2,10},{6,14},{3,11},{7,15}} | collective-permute-start | bytes 417800 | tf_op jit(solution)/shard_map/ppermute | solution.py:282
  5.7 1.2 %collective-permute-start.4 = (f32[128,256]{1,0:T(8,128)}, f32[128,256]{1,0:T(8,128)S(1)}, u32[]{:S(2)}, u32[]{:S(2)}) collective-permute-start(f32[128,256]{1,0:T(8,128)} %get-tuple-element.67), channel_id=1, source_target_pairs={{0,4},{4,0},{8,12},{12,8},{16,20},{20,16},{24,28},{28,24},{1,5},{5... | collective-permute-start | bytes 393224 | tf_op jit(solution)/shard_map/ppermute | solution.py:258
  7.7 1.0 %shard_map.55 = (f32[136,256]{1,0:T(8,128)S(1)}, f32[128,256]{1,0:T(8,128)S(1)}, f32[128,256]{1,0:T(8,128)S(1)}, f32[1,1024]{1,0:T(1,128)S(1)}) custom-call(s32[1]{0:T(128)} %bitcast.places_ref._, bf16[8,256]{1,0:T(8,128)(2,1)S(1)} %copy-done.3, bf16[256,1024]{1,0:T(8,128)(2,1)S(1)} %copy-done, bf16[256,1024]{1,0:T(8,128)(2,1)S(1)} %copy-done.1, ...), custom_call_target="tpu_custom_call" | custom-call | flops 100663296 | bytes 1462276 | tf_op jit(solution)/shard_map/pallas_call | solution.py:209
  8.7 0.8 %collective-permute-start.5 = (f32[136,256]{1,0:T(8,128)S(1)}, f32[136,256]{1,0:T(8,128)S(1)}, u32[]{:S(2)}, u32[]{:S(2)}) collective-permute-start(f32[136,256]{1,0:T(8,128)S(1)} %shard_map.57._), channel_id=1, source_target_pairs={{0,8},{4,12},{1,9},{5,13},{2,10},{6,14},{3,11},{7,15}} | collective-permute-start | bytes 417800 | tf_op jit(solution)/shard_map/ppermute | solution.py:282
  9.6 1.3 %collective-permute-start.6 = (f32[136,256]{1,0:T(8,128)S(1)}, f32[136,256]{1,0:T(8,128)S(1)}, u32[]{:S(2)}, u32[]{:S(2)}) collective-permute-start(f32[136,256]{1,0:T(8,128)S(1)} %shard_map.58._), channel_id=1, source_target_pairs={{8,16},{12,20},{9,17},{13,21},{10,18},{14,22},{11,19},{15,23}} | collective-permute-start | bytes 417800 | tf_op jit(solution)/shard_map/ppermute | solution.py:282
  11.2 0.8 %collective-permute-start.7 = (f32[128,256]{1,0:T(8,128)S(1)}, f32[128,256]{1,0:T(8,128)S(1)}, u32[]{:S(2)}, u32[]{:S(2)}) collective-permute-start(f32[128,256]{1,0:T(8,128)S(1)} %shard_map.59._), channel_id=1, source_target_pairs={{0,8},{4,12},{1,9},{5,13},{2,10},{6,14},{3,11},{7,15}} | collective-permute-start | bytes 393224 | tf_op jit(solution)/shard_map/ppermute | solution.py:282
  12.1 1.3 %collective-permute-start.8 = (f32[136,256]{1,0:T(8,128)S(1)}, f32[136,256]{1,0:T(8,128)S(1)}, u32[]{:S(2)}, u32[]{:S(2)}) collective-permute-start(f32[136,256]{1,0:T(8,128)S(1)} %shard_map.60._), channel_id=1, source_target_pairs={{8,16},{12,20},{9,17},{13,21},{10,18},{14,22},{11,19},{15,23}} | collective-permute-start | bytes 417800 | tf_op jit(solution)/shard_map/ppermute | solution.py:282
  14.0 0.7 %collective-permute-start.9 = (f32[128,256]{1,0:T(8,128)S(1)}, f32[128,256]{1,0:T(8,128)S(1)}, u32[]{:S(2)}, u32[]{:S(2)}) collective-permute-start(f32[128,256]{1,0:T(8,128)S(1)} %shard_map.61._), channel_id=1, source_target_pairs={{0,8},{4,12},{1,9},{5,13},{2,10},{6,14},{3,11},{7,15}} | collective-permute-start | bytes 393224 | tf_op jit(solution)/shard_map/ppermute | solution.py:282
  14.7 1.3 %collective-permute-start.10 = (f32[136,256]{1,0:T(8,128)S(1)}, f32[136,256]{1,0:T(8,128)S(1)}, u32[]{:S(2)}, u32[]{:S(2)}) collective-permute-start(f32[136,256]{1,0:T(8,128)S(1)} %shard_map.62._), channel_id=1, source_target_pairs={{8,16},{12,20},{9,17},{13,21},{10,18},{14,22},{11,19},{15,23}} | collective-permute-start | bytes 417800 | tf_op jit(solution)/shard_map/ppermute | solution.py:282
  16.1 2.6 %collective-permute-start.11 = (f32[136,256]{1,0:T(8,128)S(1)}, f32[136,256]{1,0:T(8,128)S(1)}, u32[]{:S(2)}, u32[]{:S(2)}) collective-permute-start(f32[136,256]{1,0:T(8,128)S(1)} %shard_map.63._), channel_id=1, source_target_pairs={{16,24},{20,28},{17,25},{21,29},{18,26},{22,30},{19,27},{23,31}} | collective-permute-start | bytes 417800 | tf_op jit(solution)/shard_map/ppermute | solution.py:282
  18.7 1.3 %collective-permute-start.12 = (f32[128,256]{1,0:T(8,128)S(1)}, f32[128,256]{1,0:T(8,128)S(1)}, u32[]{:S(2)}, u32[]{:S(2)}) collective-permute-start(f32[128,256]{1,0:T(8,128)S(1)} %shard_map.64._), channel_id=1, source_target_pairs={{8,16},{12,20},{9,17},{13,21},{10,18},{14,22},{11,19},{15,23}} | collective-permute-start | bytes 393224 | tf_op jit(solution)/shard_map/ppermute | solution.py:282
  20.1 1.3 %collective-permute-start.13 = (f32[136,256]{1,0:T(8,128)S(1)}, f32[136,256]{1,0:T(8,128)S(1)}, u32[]{:S(2)}, u32[]{:S(2)}) collective-permute-start(f32[136,256]{1,0:T(8,128)S(1)} %shard_map.65._), channel_id=1, source_target_pairs={{16,24},{20,28},{17,25},{21,29},{18,26},{22,30},{19,27},{23,31}} | collective-permute-start | bytes 417800 | tf_op jit(solution)/shard_map/ppermute | solution.py:282
  21.4 1.3 %collective-permute-start.14 = (f32[128,256]{1,0:T(8,128)S(1)}, f32[128,256]{1,0:T(8,128)S(1)}, u32[]{:S(2)}, u32[]{:S(2)}) collective-permute-start(f32[128,256]{1,0:T(8,128)S(1)} %shard_map.66._), channel_id=1, source_target_pairs={{8,16},{12,20},{9,17},{13,21},{10,18},{14,22},{11,19},{15,23}} | collective-permute-start | bytes 393224 | tf_op jit(solution)/shard_map/ppermute | solution.py:282
  23.3 1.3 %collective-permute-start.15 = (f32[136,256]{1,0:T(8,128)S(1)}, f32[136,256]{1,0:T(8,128)S(1)}, u32[]{:S(2)}, u32[]{:S(2)}) collective-permute-start(f32[136,256]{1,0:T(8,128)S(1)} %shard_map.67._), channel_id=1, source_target_pairs={{16,24},{20,28},{17,25},{21,29},{18,26},{22,30},{19,27},{23,31}} | collective-permute-start | bytes 417800 | tf_op jit(solution)/shard_map/ppermute | solution.py:282
  25.2 0.9 %collective-permute-done.12.refs_0_.refs_1_ = f32[128,256]{1,0:T(8,128)S(1)} collective-permute-done((f32[128,256]{1,0:T(8,128)S(1)}, f32[128,256]{1,0:T(8,128)S(1)}, u32[]{:S(2)}, u32[]{:S(2)}) %collective-permute-start.12) | collective-permute-done | bytes 131104 | tf_op jit(solution)/shard_map/ppermute | solution.py:282
  26.1 1.3 %collective-permute-start.16 = (f32[128,256]{1,0:T(8,128)S(1)}, f32[128,256]{1,0:T(8,128)S(1)}, u32[]{:S(2)}, u32[]{:S(2)}) collective-permute-start(f32[128,256]{1,0:T(8,128)S(1)} %shard_map.69._), channel_id=1, source_target_pairs={{16,24},{20,28},{17,25},{21,29},{18,26},{22,30},{19,27},{23,31}} | collective-permute-start | bytes 393224 | tf_op jit(solution)/shard_map/ppermute | solution.py:282
  27.8 1.1 %collective-permute-done.14.refs_0_.refs_1_ = f32[128,256]{1,0:T(8,128)S(1)} collective-permute-done((f32[128,256]{1,0:T(8,128)S(1)}, f32[128,256]{1,0:T(8,128)S(1)}, u32[]{:S(2)}, u32[]{:S(2)}) %collective-permute-start.14) | collective-permute-done | bytes 131104 | tf_op jit(solution)/shard_map/ppermute | solution.py:282
  28.9 1.3 %collective-permute-start.17 = (f32[128,256]{1,0:T(8,128)S(1)}, f32[128,256]{1,0:T(8,128)S(1)}, u32[]{:S(2)}, u32[]{:S(2)}) collective-permute-start(f32[128,256]{1,0:T(8,128)S(1)} %shard_map.71._), channel_id=1, source_target_pairs={{16,24},{20,28},{17,25},{21,29},{18,26},{22,30},{19,27},{23,31}} | collective-permute-start | bytes 393224 | tf_op jit(solution)/shard_map/ppermute | solution.py:282
  30.8 1.2 %collective-permute-start.21 = (f32[128,256]{1,0:T(8,128)S(1)}, f32[128,256]{1,0:T(8,128)S(1)}, u32[]{:S(2)}, u32[]{:S(2)}) collective-permute-start(f32[128,256]{1,0:T(8,128)S(1)} %get-tuple-element.71._), channel_id=1, source_target_pairs={{0,4},{4,0},{8,12},{12,8},{16,20},{20,16},{24,28},{28,24},{1,5},{5... | collective-permute-start | bytes 393224 | tf_op jit(solution)/shard_map/ppermute | solution.py:298
  31.9 1.0 %collective-permute-done.17.refs_2_ = f32[128,256]{1,0:T(8,128)S(1)} collective-permute-done((f32[128,256]{1,0:T(8,128)S(1)}, f32[128,256]{1,0:T(8,128)S(1)}, u32[]{:S(2)}, u32[]{:S(2)}) %collective-permute-start.17) | collective-permute-done | bytes 131104 | tf_op jit(solution)/shard_map/ppermute | solution.py:282
  33.0 1.1 %collective-permute-start.22 = (f32[128,256]{1,0:T(8,128)S(1)}, f32[128,256]{1,0:T(8,128)S(1)}, u32[]{:S(2)}, u32[]{:S(2)}) collective-permute-start(f32[128,256]{1,0:T(8,128)S(1)} %get-tuple-element.72._), channel_id=1, source_target_pairs={{0,4},{4,0},{8,12},{12,8},{16,20},{20,16},{24,28},{28,24},{1,5},{5... | collective-permute-start | bytes 393224 | tf_op jit(solution)/shard_map/ppermute | solution.py:298
  34.1 1.0 %shard_map.75 = (f32[256,128]{1,0:T(8,128)S(1)}, f32[256,128]{1,0:T(8,128)S(1)}, bf16[256,256]{1,0:T(8,128)(2,1)S(1)}, f32[256,128]{1,0:T(8,128)S(1)}, f32[256,1...) custom-call(s32[1]{0:T(128)} %bitcast.places_ref._, f32[128,256]{1,0:T(8,128)S(1)} %get-tuple-element.72._, ...), custom_call_target="tpu_custom_call" | custom-call | flops 167772160 | bytes 2494468 | tf_op jit(solution)/shard_map/pallas_call | solution.py:209
  35.0 1.0 %shard_map.76 = (f32[256,128]{1,0:T(8,128)S(1)}, f32[256,128]{1,0:T(8,128)S(1)}, bf16[256,256]{1,0:T(8,128)(2,1)S(1)}, f32[256,128]{1,0:T(8,128)S(1)}, f32[256,1...) custom-call(s32[1]{0:T(128)} %bitcast.places_ref._, f32[256,128]{1,0:T(8,128)S(1)} %get-tuple-element.73._.refs_0_, ...), custom_call_target="tpu_custom_call" | custom-call | flops 167772160 | bytes 2494468 | tf_op jit(solution)/shard_map/pallas_call | solution.py:209
  36.1 1.0 %shard_map.77 = (f32[256,128]{1,0:T(8,128)S(1)}, f32[256,128]{1,0:T(8,128)S(1)}, bf16[256,256]{1,0:T(8,128)(2,1)S(1)}, f32[256,128]{1,0:T(8,128)S(1)}, f32[256,1...) custom-call(s32[1]{0:T(128)} %bitcast.places_ref._, f32[256,128]{1,0:T(8,128)S(1)} %get-tuple-element.74._.refs_0_, ...), custom_call_target="tpu_custom_call" | custom-call | flops 167772160 | bytes 2494468 | tf_op jit(solution)/shard_map/pallas_call | solution.py:209
  37.1 1.0 %shard_map.78 = (f32[256,128]{1,0:T(8,128)S(1)}, f32[256,128]{1,0:T(8,128)S(1)}, bf16[256,256]{1,0:T(8,128)(2,1)S(1)}, f32[256,128]{1,0:T(8,128)S(1)}, f32[256,1...) custom-call(s32[1]{0:T(128)} %bitcast.places_ref._, f32[256,128]{1,0:T(8,128)S(1)} %get-tuple-element.75._.refs_4_, ...), custom_call_target="tpu_custom_call" | custom-call | flops 167772160 | bytes 2494468 | tf_op jit(solution)/shard_map/pallas_call | solution.py:209
  39.6 0.8 %collective-permute-done.22.refs_5_ = f32[128,256]{1,0:T(8,128)S(1)} collective-permute-done((f32[128,256]{1,0:T(8,128)S(1)}, f32[128,256]{1,0:T(8,128)S(1)}, u32[]{:S(2)}, u32[]{:S(2)}) %collective-permute-start.22) | collective-permute-done | bytes 131104 | tf_op jit(solution)/shard_map/ppermute | solution.py:298
  40.7 4.6 %collective-permute-start.25 = (f32[8,256]{1,0:T(8,128)S(1)}, f32[8,256]{1,0:T(8,128)S(1)}, u32[]{:S(2)}, u32[]{:S(2)}) collective-permute-start(f32[8,256]{1,0:T(8,128)S(1)} %get-tuple-element.114.refs_8_), channel_id=1, source_target_pairs={{0,3},{1,2},{2,1},{3,0},{4,7},{5,6},{6,5},{7,4},{8,11},{9,10},{10,... | collective-permute-start | bytes 24584 | tf_op jit(solution)/shard_map/ppermute | solution.py:365
  45.9 0.9 %collective-permute-done.25.refs_11_ = f32[8,256]{1,0:T(8,128)S(1)} collective-permute-done((f32[8,256]{1,0:T(8,128)S(1)}, f32[8,256]{1,0:T(8,128)S(1)}, u32[]{:S(2)}, u32[]{:S(2)}) %collective-permute-start.25) | collective-permute-done | bytes 8224 | tf_op jit(solution)/shard_map/ppermute | solution.py:365
  46.8 1.1 %collective-permute-done.24.refs_10_ = f32[8,256]{1,0:T(8,128)S(1)} collective-permute-done((f32[8,256]{1,0:T(8,128)S(1)}, f32[8,256]{1,0:T(8,128)S(1)}, u32[]{:S(2)}, u32[]{:S(2)}) %collective-permute-start.24) | collective-permute-done | bytes 8224 | tf_op jit(solution)/shard_map/ppermute | solution.py:365
  47.9 1.0 %shard_map.83 = bf16[256,1024]{1,0:T(8,128)(2,1)} custom-call(s32[1]{0:T(128)} %bitcast.places_ref._, f32[256,128]{1,0:T(8,128)S(1)} %get-tuple-element.85.refs_0_, f32[256,128]{1,0:T(8,128)S(1)} %get-tuple-element.86.refs_1_, f32[256,128]{1,0:T(8,128)S(1)} %get-tuple-element.97.refs_2_, f32[256,128]{1,0:T(8,128)S(1)} %get-tuple-element.98.refs_3_, ...), custom_call_target="tpu_custom_call" | custom-call | flops 786432 | bytes 1605636 | tf_op jit(solution)/shard_map/pallas_call | solution.py:209
  (63 shorter events, 6.7 us)
Async XLA Ops:
  0.0 7.6 %copy-start = (bf16[256,1024]{1,0:T(8,128)(2,1)S(1)}, bf16[256,1024]{1,0:T(8,128)(2,1)}, u32[]{:S(2)}) copy-start(bf16[256,1024]{1,0:T(8,128)(2,1)} %k_ref.7) | copy-start | bytes 1572868
  0.0 7.6 %copy-start.1 = (bf16[256,1024]{1,0:T(8,128)(2,1)S(1)}, bf16[256,1024]{1,0:T(8,128)(2,1)}, u32[]{:S(2)}) copy-start(bf16[256,1024]{1,0:T(8,128)(2,1)} %v_ref.7) | copy-start | bytes 1572868
  3.3 5.3 %collective-permute-start = (f32[136,256]{1,0:T(8,128)}, f32[136,256]{1,0:T(8,128)S(1)}, u32[]{:S(2)}, u32[]{:S(2)}) collective-permute-start(f32[136,256]{1,0:T(8,128)} %get-tuple-element.61), channel_id=1, source_target_pairs={{0,4},{4,0},{8,12},{12,8},{16,20},{20,16},{24,28},{28,24},{1,5},{5... | collective-permute-start | bytes 417800 | tf_op jit(solution)/shard_map/ppermute | solution.py:258
  4.6 3.0 %copy-start.4 = (f32[1024]{0:T(1024)S(1)}, f32[1024]{0:T(1024)}, u32[]{:S(2)}) copy-start(f32[1024]{0:T(1024)} %param.9) | copy-start | bytes 12292
  4.6 3.0 %copy-start.3 = (bf16[8,256]{1,0:T(8,128)(2,1)S(1)}, bf16[8,256]{1,0:T(8,128)(2,1)}, u32[]{:S(2)}) copy-start(bf16[8,256]{1,0:T(8,128)(2,1)} %seeds_ref.7) | copy-start | bytes 12292
  4.6 4.9 %collective-permute-start.1 = (f32[136,256]{1,0:T(8,128)}, f32[136,256]{1,0:T(8,128)S(1)}, u32[]{:S(2)}, u32[]{:S(2)}) collective-permute-start(f32[136,256]{1,0:T(8,128)} %get-tuple-element.62.refs_1_.refs_3_), channel_id=1, source_target_pairs={{0,8},{4,12},{1,9},{5,13},{2,10},{6,14},{3,11},{7,15}} | collective-permute-start | bytes 417800 | tf_op jit(solution)/shard_map/ppermute | solution.py:282
  5.4 5.8 %collective-permute-start.2 = (f32[128,256]{1,0:T(8,128)}, f32[128,256]{1,0:T(8,128)S(1)}, u32[]{:S(2)}, u32[]{:S(2)}) collective-permute-start(f32[128,256]{1,0:T(8,128)} %get-tuple-element.64), channel_id=1, source_target_pairs={{0,4},{4,0},{8,12},{12,8},{16,20},{20,16},{24,28},{28,24},{1,5},{5... | collective-permute-start | bytes 393224 | tf_op jit(solution)/shard_map/ppermute | solution.py:258
  5.7 8.3 %collective-permute-start.4 = (f32[128,256]{1,0:T(8,128)}, f32[128,256]{1,0:T(8,128)S(1)}, u32[]{:S(2)}, u32[]{:S(2)}) collective-permute-start(f32[128,256]{1,0:T(8,128)} %get-tuple-element.67), channel_id=1, source_target_pairs={{0,4},{4,0},{8,12},{12,8},{16,20},{20,16},{24,28},{28,24},{1,5},{5... | collective-permute-start | bytes 393224 | tf_op jit(solution)/shard_map/ppermute | solution.py:258
  7.0 5.1 %collective-permute-start.3 = (f32[136,256]{1,0:T(8,128)}, f32[136,256]{1,0:T(8,128)S(1)}, u32[]{:S(2)}, u32[]{:S(2)}) collective-permute-start(f32[136,256]{1,0:T(8,128)} %get-tuple-element.65.refs_1_.refs_3_), channel_id=1, source_target_pairs={{0,8},{4,12},{1,9},{5,13},{2,10},{6,14},{3,11},{7,15}} | collective-permute-start | bytes 417800 | tf_op jit(solution)/shard_map/ppermute | solution.py:282
  8.7 0.9 %copy-start.6 = (f32[136,256]{1,0:T(8,128)S(1)}, f32[136,256]{1,0:T(8,128)}, u32[]{:S(2)}) copy-start(f32[136,256]{1,0:T(8,128)} %get-tuple-element.62.refs_1_.refs_3_) | copy-start | bytes 417796
  8.7 6.0 %collective-permute-start.5 = (f32[136,256]{1,0:T(8,128)S(1)}, f32[136,256]{1,0:T(8,128)S(1)}, u32[]{:S(2)}, u32[]{:S(2)}) collective-permute-start(f32[136,256]{1,0:T(8,128)S(1)} %shard_map.57._), channel_id=1, source_target_pairs={{0,8},{4,12},{1,9},{5,13},{2,10},{6,14},{3,11},{7,15}} | collective-permute-start | bytes 417800 | tf_op jit(solution)/shard_map/ppermute | solution.py:282
  9.6 6.4 %collective-permute-start.6 = (f32[136,256]{1,0:T(8,128)S(1)}, f32[136,256]{1,0:T(8,128)S(1)}, u32[]{:S(2)}, u32[]{:S(2)}) collective-permute-start(f32[136,256]{1,0:T(8,128)S(1)} %shard_map.58._), channel_id=1, source_target_pairs={{8,16},{12,20},{9,17},{13,21},{10,18},{14,22},{11,19},{15,23}} | collective-permute-start | bytes 417800 | tf_op jit(solution)/shard_map/ppermute | solution.py:282
  11.2 7.5 %collective-permute-start.7 = (f32[128,256]{1,0:T(8,128)S(1)}, f32[128,256]{1,0:T(8,128)S(1)}, u32[]{:S(2)}, u32[]{:S(2)}) collective-permute-start(f32[128,256]{1,0:T(8,128)S(1)} %shard_map.59._), channel_id=1, source_target_pairs={{0,8},{4,12},{1,9},{5,13},{2,10},{6,14},{3,11},{7,15}} | collective-permute-start | bytes 393224 | tf_op jit(solution)/shard_map/ppermute | solution.py:282
  12.1 7.9 %collective-permute-start.8 = (f32[136,256]{1,0:T(8,128)S(1)}, f32[136,256]{1,0:T(8,128)S(1)}, u32[]{:S(2)}, u32[]{:S(2)}) collective-permute-start(f32[136,256]{1,0:T(8,128)S(1)} %shard_map.60._), channel_id=1, source_target_pairs={{8,16},{12,20},{9,17},{13,21},{10,18},{14,22},{11,19},{15,23}} | collective-permute-start | bytes 417800 | tf_op jit(solution)/shard_map/ppermute | solution.py:282
  14.0 7.3 %collective-permute-start.9 = (f32[128,256]{1,0:T(8,128)S(1)}, f32[128,256]{1,0:T(8,128)S(1)}, u32[]{:S(2)}, u32[]{:S(2)}) collective-permute-start(f32[128,256]{1,0:T(8,128)S(1)} %shard_map.61._), channel_id=1, source_target_pairs={{0,8},{4,12},{1,9},{5,13},{2,10},{6,14},{3,11},{7,15}} | collective-permute-start | bytes 393224 | tf_op jit(solution)/shard_map/ppermute | solution.py:282
  14.7 8.6 %collective-permute-start.10 = (f32[136,256]{1,0:T(8,128)S(1)}, f32[136,256]{1,0:T(8,128)S(1)}, u32[]{:S(2)}, u32[]{:S(2)}) collective-permute-start(f32[136,256]{1,0:T(8,128)S(1)} %shard_map.62._), channel_id=1, source_target_pairs={{8,16},{12,20},{9,17},{13,21},{10,18},{14,22},{11,19},{15,23}} | collective-permute-start | bytes 417800 | tf_op jit(solution)/shard_map/ppermute | solution.py:282
  16.1 8.6 %collective-permute-start.11 = (f32[136,256]{1,0:T(8,128)S(1)}, f32[136,256]{1,0:T(8,128)S(1)}, u32[]{:S(2)}, u32[]{:S(2)}) collective-permute-start(f32[136,256]{1,0:T(8,128)S(1)} %shard_map.63._), channel_id=1, source_target_pairs={{16,24},{20,28},{17,25},{21,29},{18,26},{22,30},{19,27},{23,31}} | collective-permute-start | bytes 417800 | tf_op jit(solution)/shard_map/ppermute | solution.py:282
  18.7 7.3 %collective-permute-start.12 = (f32[128,256]{1,0:T(8,128)S(1)}, f32[128,256]{1,0:T(8,128)S(1)}, u32[]{:S(2)}, u32[]{:S(2)}) collective-permute-start(f32[128,256]{1,0:T(8,128)S(1)} %shard_map.64._), channel_id=1, source_target_pairs={{8,16},{12,20},{9,17},{13,21},{10,18},{14,22},{11,19},{15,23}} | collective-permute-start | bytes 393224 | tf_op jit(solution)/shard_map/ppermute | solution.py:282
  20.1 7.3 %collective-permute-start.13 = (f32[136,256]{1,0:T(8,128)S(1)}, f32[136,256]{1,0:T(8,128)S(1)}, u32[]{:S(2)}, u32[]{:S(2)}) collective-permute-start(f32[136,256]{1,0:T(8,128)S(1)} %shard_map.65._), channel_id=1, source_target_pairs={{16,24},{20,28},{17,25},{21,29},{18,26},{22,30},{19,27},{23,31}} | collective-permute-start | bytes 417800 | tf_op jit(solution)/shard_map/ppermute | solution.py:282
  21.4 7.5 %collective-permute-start.14 = (f32[128,256]{1,0:T(8,128)S(1)}, f32[128,256]{1,0:T(8,128)S(1)}, u32[]{:S(2)}, u32[]{:S(2)}) collective-permute-start(f32[128,256]{1,0:T(8,128)S(1)} %shard_map.66._), channel_id=1, source_target_pairs={{8,16},{12,20},{9,17},{13,21},{10,18},{14,22},{11,19},{15,23}} | collective-permute-start | bytes 393224 | tf_op jit(solution)/shard_map/ppermute | solution.py:282
  23.3 6.9 %collective-permute-start.15 = (f32[136,256]{1,0:T(8,128)S(1)}, f32[136,256]{1,0:T(8,128)S(1)}, u32[]{:S(2)}, u32[]{:S(2)}) collective-permute-start(f32[136,256]{1,0:T(8,128)S(1)} %shard_map.67._), channel_id=1, source_target_pairs={{16,24},{20,28},{17,25},{21,29},{18,26},{22,30},{19,27},{23,31}} | collective-permute-start | bytes 417800 | tf_op jit(solution)/shard_map/ppermute | solution.py:282
  24.7 13.4 %collective-permute-start.18 = (f32[136,256]{1,0:T(8,128)S(1)}, f32[136,256]{1,0:T(8,128)S(1)}, u32[]{:S(2)}, u32[]{:S(2)}) collective-permute-start(f32[136,256]{1,0:T(8,128)S(1)} %get-tuple-element.68._), channel_id=1, source_target_pairs={{0,4},{4,0},{8,12},{12,8},{16,20},{20,16},{24,28},{28,24},{1,5},{5... | collective-permute-start | bytes 417800 | tf_op jit(solution)/shard_map/ppermute | solution.py:298
  26.1 4.6 %collective-permute-start.16 = (f32[128,256]{1,0:T(8,128)S(1)}, f32[128,256]{1,0:T(8,128)S(1)}, u32[]{:S(2)}, u32[]{:S(2)}) collective-permute-start(f32[128,256]{1,0:T(8,128)S(1)} %shard_map.69._), channel_id=1, source_target_pairs={{16,24},{20,28},{17,25},{21,29},{18,26},{22,30},{19,27},{23,31}} | collective-permute-start | bytes 393224 | tf_op jit(solution)/shard_map/ppermute | solution.py:282
  27.4 10.6 %collective-permute-start.19 = (f32[136,256]{1,0:T(8,128)S(1)}, f32[136,256]{1,0:T(8,128)S(1)}, u32[]{:S(2)}, u32[]{:S(2)}) collective-permute-start(f32[136,256]{1,0:T(8,128)S(1)} %get-tuple-element.69._), channel_id=1, source_target_pairs={{0,4},{4,0},{8,12},{12,8},{16,20},{20,16},{24,28},{28,24},{1,5},{5... | collective-permute-start | bytes 417800 | tf_op jit(solution)/shard_map/ppermute | solution.py:298
  28.9 4.0 %collective-permute-start.17 = (f32[128,256]{1,0:T(8,128)S(1)}, f32[128,256]{1,0:T(8,128)S(1)}, u32[]{:S(2)}, u32[]{:S(2)}) collective-permute-start(f32[128,256]{1,0:T(8,128)S(1)} %shard_map.71._), channel_id=1, source_target_pairs={{16,24},{20,28},{17,25},{21,29},{18,26},{22,30},{19,27},{23,31}} | collective-permute-start | bytes 393224 | tf_op jit(solution)/shard_map/ppermute | solution.py:282
  30.3 8.8 %collective-permute-start.20 = (f32[136,256]{1,0:T(8,128)S(1)}, f32[136,256]{1,0:T(8,128)S(1)}, u32[]{:S(2)}, u32[]{:S(2)}) collective-permute-start(f32[136,256]{1,0:T(8,128)S(1)} %get-tuple-element.70._), channel_id=1, source_target_pairs={{0,4},{4,0},{8,12},{12,8},{16,20},{20,16},{24,28},{28,24},{1,5},{5... | collective-permute-start | bytes 417800 | tf_op jit(solution)/shard_map/ppermute | solution.py:298
  30.7 3.3 %copy-start.2 = (bf16[256,1024]{1,0:T(8,128)(2,1)S(1)}, bf16[256,1024]{1,0:T(8,128)(2,1)}, u32[]{:S(2)}) copy-start(bf16[256,1024]{1,0:T(8,128)(2,1)} %q_ref.7) | copy-start | bytes 1572868
  30.8 8.4 %collective-permute-start.21 = (f32[128,256]{1,0:T(8,128)S(1)}, f32[128,256]{1,0:T(8,128)S(1)}, u32[]{:S(2)}, u32[]{:S(2)}) collective-permute-start(f32[128,256]{1,0:T(8,128)S(1)} %get-tuple-element.71._), channel_id=1, source_target_pairs={{0,4},{4,0},{8,12},{12,8},{16,20},{20,16},{24,28},{28,24},{1,5},{5... | collective-permute-start | bytes 393224 | tf_op jit(solution)/shard_map/ppermute | solution.py:298
  33.0 7.4 %collective-permute-start.22 = (f32[128,256]{1,0:T(8,128)S(1)}, f32[128,256]{1,0:T(8,128)S(1)}, u32[]{:S(2)}, u32[]{:S(2)}) collective-permute-start(f32[128,256]{1,0:T(8,128)S(1)} %get-tuple-element.72._), channel_id=1, source_target_pairs={{0,4},{4,0},{8,12},{12,8},{16,20},{20,16},{24,28},{28,24},{1,5},{5... | collective-permute-start | bytes 393224 | tf_op jit(solution)/shard_map/ppermute | solution.py:298
  40.7 6.1 %collective-permute-start.25 = (f32[8,256]{1,0:T(8,128)S(1)}, f32[8,256]{1,0:T(8,128)S(1)}, u32[]{:S(2)}, u32[]{:S(2)}) collective-permute-start(f32[8,256]{1,0:T(8,128)S(1)} %get-tuple-element.114.refs_8_), channel_id=1, source_target_pairs={{0,3},{1,2},{2,1},{3,0},{4,7},{5,6},{6,5},{7,4},{8,11},{9,10},{10,... | collective-permute-start | bytes 24584 | tf_op jit(solution)/shard_map/ppermute | solution.py:365
  45.4 2.5 %collective-permute-start.24 = (f32[8,256]{1,0:T(8,128)S(1)}, f32[8,256]{1,0:T(8,128)S(1)}, u32[]{:S(2)}, u32[]{:S(2)}) collective-permute-start(f32[8,256]{1,0:T(8,128)S(1)} %get-tuple-element.114.refs_8_), channel_id=1, source_target_pairs={{0,2},{1,3},{2,0},{3,1},{4,6},{5,7},{6,4},{7,5},{8,10},{9,11},{10,... | collective-permute-start | bytes 24584 | tf_op jit(solution)/shard_map/ppermute | solution.py:365
  45.5 2.4 %collective-permute-start.23 = (f32[8,256]{1,0:T(8,128)S(1)}, f32[8,256]{1,0:T(8,128)S(1)}, u32[]{:S(2)}, u32[]{:S(2)}) collective-permute-start(f32[8,256]{1,0:T(8,128)S(1)} %get-tuple-element.114.refs_8_), channel_id=1, source_target_pairs={{0,1},{1,0},{2,3},{3,2},{4,5},{5,4},{6,7},{7,6},{8,9},{9,8},{10,11... | collective-permute-start | bytes 24584 | tf_op jit(solution)/shard_map/ppermute | solution.py:365
  (1 other events, 0.9 us)

commit v4 on v3

--- a/solution.py
+++ b/solution.py
@@ -14,7 +14,7 @@
 PARTS = 3
 GLUE_COST = 10**9
 GAP = 2.1
-ORDER = None
+ORDER = [(1, 0), (1, 1), (1, 2), (2, 0), (1, 3), (2, 1), (1, 4), (2, 2), (3, 0), (2, 3), (3, 1), (2, 4), (3, 2), ('X', 0), (3, 3), ('X', 1), (3, 4), ('X', 2), ('L', 0), ('X', 3), ('X', 4), ('L', 1), ('J', [(2, 0), (2, 1)]), ('L', 2), ('L', 3), ('J', [(0, 0), (0, 1), (0, 2)]), ('J', [(1, 0), (1, 1)]), ('J', [(1, 2)])]
 
 
 NT = (((1,), (1,)), ((), ()))
@@ -162,7 +162,7 @@
     own_ref[...] = prior + jnp.where(right, ours[1][...], 0.0) if len(ours) > 1 else prior
 
 
-def join_kernel(half, work, places_ref, _, gain_ref, *refs):
+def join_kernel(half, work, final, places_ref, _, gain_ref, *refs):
     count = len(work)
     heads_refs, squares_ref = refs[-count - 1 : -1], refs[-1]
     squares = jnp.zeros(heads_refs[0].shape, jnp.float32)
@@ -186,10 +186,11 @@
         place = 2 * half + i if group == 2 else first_of(group, half, places_ref) + i
         out_ref[...] = head * gain_ref[:, columns(place)]
         squares = squares + head * head
-    rows = jnp.broadcast_to(jnp.sum(squares, axis=1, keepdims=True), squares.shape)
-    squares_ref[...] = rows.T[0:8, :]
     if len(refs) > count + 1:
-        squares_ref[...] += refs[0][...]
+        squares = squares + refs[0][...]
+    if final:
+        squares = jnp.broadcast_to(jnp.sum(squares, axis=1, keepdims=True), squares.shape).T[0:8, :]
+    squares_ref[...] = squares
 
 
 def norm_kernel(half, entries, work, places_ref, *refs):
@@ -315,6 +316,7 @@
 
     def join(todo):
         nonlocal last, squares
+        final = len(results) + len(todo) == heads
         plan, ins = [], []
         for group, i in todo:
             if group == 2:
@@ -331,8 +333,8 @@
                 arrays = arrays[:used]
             ins += [*locals_[group, i], *arrays]
         *outs, squares = call(
-            functools.partial(join_kernel, half, plan),
-            [shape(tok, WIDTH)] * len(todo) + [shape(8, tok)],
+            functools.partial(join_kernel, half, plan, final),
+            [shape(tok, WIDTH)] * len(todo) + [shape(8, tok) if final else shape(tok, WIDTH)],
             (places, last, gain, *ins, *([] if squares is None else [squares])),
             len(todo) * tok * feats * WIDTH * 8,
             specs=[ANY],

time: 49.5 us -> 49.2 us (level)
    ppermute x5, waiting for transfers between devices: 0.77 us -> 1.92 us  [hand(): passed[i] = lax.ppermute(last, 'seq', swap)]
    ppermute x15, waiting for transfers between devices: 3.6 us -> 2.64 us  [hop(): arrivals[stage, i] = lax.ppermute(sent, 'seq', pairs)]
  transfers between devices with their start and end apart: 26 -> 26, of which waited for: 9 -> 8; matrix products, arithmetic and copies ran while one was open for 0% -> 0% of each run, Pallas kernels for 14% -> 14%
where the time goes in v4:
time: 49.2 us; the launch traced here: 48.9 us
  starting transfers between devices  29.4 us (60%)
  Pallas kernels  11.4 us (23%)
  waiting for transfers between devices  7.45 us (15%)
    ppermute x15, starting transfers between devices, hop(): arrivals[stage, i] = lax.ppermute(sent, 'seq', pairs)  18.1 us
    pallas_call x29, Pallas kernels, call(): pl.pallas_call(kernel, out_shape=outs, in_specs=[SMEM, *specs] + [place]...  11.4 us
    ppermute x3, starting transfers between devices, per_device(): lax.ppermute(squares, 'tp', [(i, i ^ k if across == 4 else (i + k) % acro...  5.27 us
    ppermute x5, starting transfers between devices, hand(): passed[i] = lax.ppermute(last, 'seq', swap)  3.25 us
    ppermute x3, starting transfers between devices, per_device(): incoming = [lax.ppermute(part, 'seq', swap) for part in [*theirs, *cross]]  2.81 us
    ppermute x15, waiting for transfers between devices, hop(): arrivals[stage, i] = lax.ppermute(sent, 'seq', pairs)  2.64 us
    ppermute x3, waiting for transfers between devices, per_device(): lax.ppermute(squares, 'tp', [(i, i ^ k if across == 4 else (i + k) % acro...  2.03 us
    ppermute x5, waiting for transfers between devices, hand(): passed[i] = lax.ppermute(last, 'seq', swap)  1.92 us
  transfers between devices with their start and end apart: 26, of which 8 were waited for; matrix products, arithmetic and copies ran while one was open for 0% of the time, Pallas kernels for 14%

profile of v4, /device:TPU:17, one launch (start us, length us, event | category | flops | bytes accessed | tf_op | source)
XLA Modules:
  0.0 48.9 jit_solution(8838077386369466937)
XLA Ops:
  0.0 3.3 %shard_map.56 = (f32[136,256]{1,0:T(8,128)}, f32[136,256]{1,0:T(8,128)}, f32[136,256]{1,0:T(8,128)}, f32[128,256]{1,0:T(8,128)}, f32[128,256]{1,0:T(8,128)}) custom-call(s32[1]{0:T(128)} %bitcast.places_ref._, bf16[8,256]{1,0:T(8,128)(2,1)} %seeds_ref.7, bf16[256,1024]{1,0:T(8,128)(2,1)} %k_ref.7, bf16[256,1024]{1,0:T(8,128)(2,1)} %v_ref.7), custom_call_target="tpu_custom_call" | custom-call | flops 167772160 | bytes 1732612 | tf_op jit(solution)/shard_map/pallas_call | solution.py:210
  3.3 1.3 %collective-permute-start = (f32[136,256]{1,0:T(8,128)}, f32[136,256]{1,0:T(8,128)S(1)}, u32[]{:S(2)}, u32[]{:S(2)}) collective-permute-start(f32[136,256]{1,0:T(8,128)} %get-tuple-element.61), channel_id=1, source_target_pairs={{0,4},{4,0},{8,12},{12,8},{16,20},{20,16},{24,28},{28,24},{1,5},{5... | collective-permute-start | bytes 417800 | tf_op jit(solution)/shard_map/ppermute | solution.py:259
  4.6 0.8 %collective-permute-start.1 = (f32[136,256]{1,0:T(8,128)}, f32[136,256]{1,0:T(8,128)S(1)}, u32[]{:S(2)}, u32[]{:S(2)}) collective-permute-start(f32[136,256]{1,0:T(8,128)} %get-tuple-element.62.refs_1_.refs_3_), channel_id=1, source_target_pairs={{0,8},{4,12},{1,9},{5,13},{2,10},{6,14},{3,11},{7,15}} | collective-permute-start | bytes 417800 | tf_op jit(solution)/shard_map/ppermute | solution.py:283
  5.7 1.2 %collective-permute-start.4 = (f32[128,256]{1,0:T(8,128)}, f32[128,256]{1,0:T(8,128)S(1)}, u32[]{:S(2)}, u32[]{:S(2)}) collective-permute-start(f32[128,256]{1,0:T(8,128)} %get-tuple-element.67), channel_id=1, source_target_pairs={{0,4},{4,0},{8,12},{12,8},{16,20},{20,16},{24,28},{28,24},{1,5},{5... | collective-permute-start | bytes 393224 | tf_op jit(solution)/shard_map/ppermute | solution.py:259
  7.0 0.7 %collective-permute-start.3 = (f32[136,256]{1,0:T(8,128)}, f32[136,256]{1,0:T(8,128)S(1)}, u32[]{:S(2)}, u32[]{:S(2)}) collective-permute-start(f32[136,256]{1,0:T(8,128)} %get-tuple-element.65.refs_1_.refs_3_), channel_id=1, source_target_pairs={{0,8},{4,12},{1,9},{5,13},{2,10},{6,14},{3,11},{7,15}} | collective-permute-start | bytes 417800 | tf_op jit(solution)/shard_map/ppermute | solution.py:283
  7.7 1.0 %shard_map.55 = (f32[136,256]{1,0:T(8,128)S(1)}, f32[128,256]{1,0:T(8,128)S(1)}, f32[128,256]{1,0:T(8,128)S(1)}, f32[1,1024]{1,0:T(1,128)S(1)}) custom-call(s32[1]{0:T(128)} %bitcast.places_ref._, bf16[8,256]{1,0:T(8,128)(2,1)S(1)} %copy-done.3, bf16[256,1024]{1,0:T(8,128)(2,1)S(1)} %copy-done, bf16[256,1024]{1,0:T(8,128)(2,1)S(1)} %copy-done.1, ...), custom_call_target="tpu_custom_call" | custom-call | flops 100663296 | bytes 1462276 | tf_op jit(solution)/shard_map/pallas_call | solution.py:210
  8.7 0.8 %collective-permute-start.5 = (f32[136,256]{1,0:T(8,128)S(1)}, f32[136,256]{1,0:T(8,128)S(1)}, u32[]{:S(2)}, u32[]{:S(2)}) collective-permute-start(f32[136,256]{1,0:T(8,128)S(1)} %shard_map.57._), channel_id=1, source_target_pairs={{0,8},{4,12},{1,9},{5,13},{2,10},{6,14},{3,11},{7,15}} | collective-permute-start | bytes 417800 | tf_op jit(solution)/shard_map/ppermute | solution.py:283
  9.6 1.3 %collective-permute-start.6 = (f32[136,256]{1,0:T(8,128)S(1)}, f32[136,256]{1,0:T(8,128)S(1)}, u32[]{:S(2)}, u32[]{:S(2)}) collective-permute-start(f32[136,256]{1,0:T(8,128)S(1)} %shard_map.58._), channel_id=1, source_target_pairs={{8,16},{12,20},{9,17},{13,21},{10,18},{14,22},{11,19},{15,23}} | collective-permute-start | bytes 417800 | tf_op jit(solution)/shard_map/ppermute | solution.py:283
  11.2 0.8 %collective-permute-start.7 = (f32[128,256]{1,0:T(8,128)S(1)}, f32[128,256]{1,0:T(8,128)S(1)}, u32[]{:S(2)}, u32[]{:S(2)}) collective-permute-start(f32[128,256]{1,0:T(8,128)S(1)} %shard_map.59._), channel_id=1, source_target_pairs={{0,8},{4,12},{1,9},{5,13},{2,10},{6,14},{3,11},{7,15}} | collective-permute-start | bytes 393224 | tf_op jit(solution)/shard_map/ppermute | solution.py:283
  12.1 1.3 %collective-permute-start.8 = (f32[136,256]{1,0:T(8,128)S(1)}, f32[136,256]{1,0:T(8,128)S(1)}, u32[]{:S(2)}, u32[]{:S(2)}) collective-permute-start(f32[136,256]{1,0:T(8,128)S(1)} %shard_map.60._), channel_id=1, source_target_pairs={{8,16},{12,20},{9,17},{13,21},{10,18},{14,22},{11,19},{15,23}} | collective-permute-start | bytes 417800 | tf_op jit(solution)/shard_map/ppermute | solution.py:283
  14.0 0.7 %collective-permute-start.9 = (f32[128,256]{1,0:T(8,128)S(1)}, f32[128,256]{1,0:T(8,128)S(1)}, u32[]{:S(2)}, u32[]{:S(2)}) collective-permute-start(f32[128,256]{1,0:T(8,128)S(1)} %shard_map.61._), channel_id=1, source_target_pairs={{0,8},{4,12},{1,9},{5,13},{2,10},{6,14},{3,11},{7,15}} | collective-permute-start | bytes 393224 | tf_op jit(solution)/shard_map/ppermute | solution.py:283
  14.7 1.3 %collective-permute-start.10 = (f32[136,256]{1,0:T(8,128)S(1)}, f32[136,256]{1,0:T(8,128)S(1)}, u32[]{:S(2)}, u32[]{:S(2)}) collective-permute-start(f32[136,256]{1,0:T(8,128)S(1)} %shard_map.62._), channel_id=1, source_target_pairs={{8,16},{12,20},{9,17},{13,21},{10,18},{14,22},{11,19},{15,23}} | collective-permute-start | bytes 417800 | tf_op jit(solution)/shard_map/ppermute | solution.py:283
  16.1 2.6 %collective-permute-start.11 = (f32[136,256]{1,0:T(8,128)S(1)}, f32[136,256]{1,0:T(8,128)S(1)}, u32[]{:S(2)}, u32[]{:S(2)}) collective-permute-start(f32[136,256]{1,0:T(8,128)S(1)} %shard_map.63._), channel_id=1, source_target_pairs={{16,24},{20,28},{17,25},{21,29},{18,26},{22,30},{19,27},{23,31}} | collective-permute-start | bytes 417800 | tf_op jit(solution)/shard_map/ppermute | solution.py:283
  18.7 1.3 %collective-permute-start.12 = (f32[128,256]{1,0:T(8,128)S(1)}, f32[128,256]{1,0:T(8,128)S(1)}, u32[]{:S(2)}, u32[]{:S(2)}) collective-permute-start(f32[128,256]{1,0:T(8,128)S(1)} %shard_map.64._), channel_id=1, source_target_pairs={{8,16},{12,20},{9,17},{13,21},{10,18},{14,22},{11,19},{15,23}} | collective-permute-start | bytes 393224 | tf_op jit(solution)/shard_map/ppermute | solution.py:283
  20.1 1.3 %collective-permute-start.13 = (f32[136,256]{1,0:T(8,128)S(1)}, f32[136,256]{1,0:T(8,128)S(1)}, u32[]{:S(2)}, u32[]{:S(2)}) collective-permute-start(f32[136,256]{1,0:T(8,128)S(1)} %shard_map.65._), channel_id=1, source_target_pairs={{16,24},{20,28},{17,25},{21,29},{18,26},{22,30},{19,27},{23,31}} | collective-permute-start | bytes 417800 | tf_op jit(solution)/shard_map/ppermute | solution.py:283
  21.4 1.3 %collective-permute-start.14 = (f32[128,256]{1,0:T(8,128)S(1)}, f32[128,256]{1,0:T(8,128)S(1)}, u32[]{:S(2)}, u32[]{:S(2)}) collective-permute-start(f32[128,256]{1,0:T(8,128)S(1)} %shard_map.66._), channel_id=1, source_target_pairs={{8,16},{12,20},{9,17},{13,21},{10,18},{14,22},{11,19},{15,23}} | collective-permute-start | bytes 393224 | tf_op jit(solution)/shard_map/ppermute | solution.py:283
  23.3 1.3 %collective-permute-start.15 = (f32[136,256]{1,0:T(8,128)S(1)}, f32[136,256]{1,0:T(8,128)S(1)}, u32[]{:S(2)}, u32[]{:S(2)}) collective-permute-start(f32[136,256]{1,0:T(8,128)S(1)} %shard_map.67._), channel_id=1, source_target_pairs={{16,24},{20,28},{17,25},{21,29},{18,26},{22,30},{19,27},{23,31}} | collective-permute-start | bytes 417800 | tf_op jit(solution)/shard_map/ppermute | solution.py:283
  25.2 0.9 %collective-permute-done.12.refs_0_.refs_1_ = f32[128,256]{1,0:T(8,128)S(1)} collective-permute-done((f32[128,256]{1,0:T(8,128)S(1)}, f32[128,256]{1,0:T(8,128)S(1)}, u32[]{:S(2)}, u32[]{:S(2)}) %collective-permute-start.12) | collective-permute-done | bytes 131104 | tf_op jit(solution)/shard_map/ppermute | solution.py:283
  26.1 1.3 %collective-permute-start.16 = (f32[128,256]{1,0:T(8,128)S(1)}, f32[128,256]{1,0:T(8,128)S(1)}, u32[]{:S(2)}, u32[]{:S(2)}) collective-permute-start(f32[128,256]{1,0:T(8,128)S(1)} %shard_map.69._), channel_id=1, source_target_pairs={{16,24},{20,28},{17,25},{21,29},{18,26},{22,30},{19,27},{23,31}} | collective-permute-start | bytes 393224 | tf_op jit(solution)/shard_map/ppermute | solution.py:283
  27.8 1.1 %collective-permute-done.14.refs_0_.refs_1_ = f32[128,256]{1,0:T(8,128)S(1)} collective-permute-done((f32[128,256]{1,0:T(8,128)S(1)}, f32[128,256]{1,0:T(8,128)S(1)}, u32[]{:S(2)}, u32[]{:S(2)}) %collective-permute-start.14) | collective-permute-done | bytes 131104 | tf_op jit(solution)/shard_map/ppermute | solution.py:283
  28.9 1.4 %collective-permute-start.17 = (f32[128,256]{1,0:T(8,128)S(1)}, f32[128,256]{1,0:T(8,128)S(1)}, u32[]{:S(2)}, u32[]{:S(2)}) collective-permute-start(f32[128,256]{1,0:T(8,128)S(1)} %shard_map.71._), channel_id=1, source_target_pairs={{16,24},{20,28},{17,25},{21,29},{18,26},{22,30},{19,27},{23,31}} | collective-permute-start | bytes 393224 | tf_op jit(solution)/shard_map/ppermute | solution.py:283
  30.8 1.0 %shard_map.73 = (f32[256,128]{1,0:T(8,128)S(1)}, f32[256,128]{1,0:T(8,128)S(1)}, bf16[256,256]{1,0:T(8,128)(2,1)S(1)}, f32[256,128]{1,0:T(8,128)S(1)}, f32[256,1...) custom-call(s32[1]{0:T(128)} %bitcast.places_ref._, f32[136,256]{1,0:T(8,128)S(1)} %get-tuple-element.70._, ...), custom_call_target="tpu_custom_call" | custom-call | flops 167772160 | bytes 2502660 | tf_op jit(solution)/shard_map/pallas_call | solution.py:210
  31.9 1.2 %collective-permute-start.21 = (f32[128,256]{1,0:T(8,128)S(1)}, f32[128,256]{1,0:T(8,128)S(1)}, u32[]{:S(2)}, u32[]{:S(2)}) collective-permute-start(f32[128,256]{1,0:T(8,128)S(1)} %get-tuple-element.72._), channel_id=1, source_target_pairs={{0,4},{4,0},{8,12},{12,8},{16,20},{20,16},{24,28},{28,24},{1,5},{5... | collective-permute-start | bytes 393224 | tf_op jit(solution)/shard_map/ppermute | solution.py:299
  33.1 0.9 %collective-permute-start.22 = (f32[128,256]{1,0:T(8,128)S(1)}, f32[128,256]{1,0:T(8,128)S(1)}, u32[]{:S(2)}, u32[]{:S(2)}) collective-permute-start(f32[128,256]{1,0:T(8,128)S(1)} %get-tuple-element.73._), channel_id=1, source_target_pairs={{0,4},{4,0},{8,12},{12,8},{16,20},{20,16},{24,28},{28,24},{1,5},{5... | collective-permute-start | bytes 393224 | tf_op jit(solution)/shard_map/ppermute | solution.py:299
  34.1 1.0 %shard_map.76 = (f32[256,128]{1,0:T(8,128)S(1)}, f32[256,128]{1,0:T(8,128)S(1)}, bf16[256,256]{1,0:T(8,128)(2,1)S(1)}, f32[256,128]{1,0:T(8,128)S(1)}, f32[256,1...) custom-call(s32[1]{0:T(128)} %bitcast.places_ref._, f32[128,256]{1,0:T(8,128)S(1)} %get-tuple-element.73._, ...), custom_call_target="tpu_custom_call" | custom-call | flops 167772160 | bytes 2494468 | tf_op jit(solution)/shard_map/pallas_call | solution.py:210
  35.4 1.0 %shard_map.78 = (f32[256,128]{1,0:T(8,128)S(1)}, f32[256,128]{1,0:T(8,128)S(1)}, bf16[256,256]{1,0:T(8,128)(2,1)S(1)}, f32[256,128]{1,0:T(8,128)S(1)}, f32[256,1...) custom-call(s32[1]{0:T(128)} %bitcast.places_ref._, f32[256,128]{1,0:T(8,128)S(1)} %get-tuple-element.85._.refs_15_, ...), custom_call_target="tpu_custom_call" | custom-call | flops 167772160 | bytes 2494468 | tf_op jit(solution)/shard_map/pallas_call | solution.py:210
  36.5 1.0 %shard_map.79 = (f32[256,128]{1,0:T(8,128)S(1)}, f32[256,128]{1,0:T(8,128)S(1)}, bf16[256,256]{1,0:T(8,128)(2,1)S(1)}, f32[256,128]{1,0:T(8,128)S(1)}, f32[256,1...) custom-call(s32[1]{0:T(128)} %bitcast.places_ref._, f32[256,128]{1,0:T(8,128)S(1)} %get-tuple-element.86._.refs_4_, ...), custom_call_target="tpu_custom_call" | custom-call | flops 167772160 | bytes 2494468 | tf_op jit(solution)/shard_map/pallas_call | solution.py:210
  38.3 1.9 %collective-permute-done.22.refs_5_ = f32[128,256]{1,0:T(8,128)S(1)} collective-permute-done((f32[128,256]{1,0:T(8,128)S(1)}, f32[128,256]{1,0:T(8,128)S(1)}, u32[]{:S(2)}, u32[]{:S(2)}) %collective-permute-start.22) | collective-permute-done | bytes 131104 | tf_op jit(solution)/shard_map/ppermute | solution.py:299
  40.6 4.8 %collective-permute-start.25 = (f32[8,256]{1,0:T(8,128)S(1)}, f32[8,256]{1,0:T(8,128)S(1)}, u32[]{:S(2)}, u32[]{:S(2)}) collective-permute-start(f32[8,256]{1,0:T(8,128)S(1)} %get-tuple-element.114.refs_8_), channel_id=1, source_target_pairs={{0,3},{1,2},{2,1},{3,0},{4,7},{5,6},{6,5},{7,4},{8,11},{9,10},{10,... | collective-permute-start | bytes 24584 | tf_op jit(solution)/shard_map/ppermute | solution.py:367
  45.9 0.9 %collective-permute-done.25.refs_11_ = f32[8,256]{1,0:T(8,128)S(1)} collective-permute-done((f32[8,256]{1,0:T(8,128)S(1)}, f32[8,256]{1,0:T(8,128)S(1)}, u32[]{:S(2)}, u32[]{:S(2)}) %collective-permute-start.25) | collective-permute-done | bytes 8224 | tf_op jit(solution)/shard_map/ppermute | solution.py:367
  46.8 1.1 %collective-permute-done.24.refs_10_ = f32[8,256]{1,0:T(8,128)S(1)} collective-permute-done((f32[8,256]{1,0:T(8,128)S(1)}, f32[8,256]{1,0:T(8,128)S(1)}, u32[]{:S(2)}, u32[]{:S(2)}) %collective-permute-start.24) | collective-permute-done | bytes 8224 | tf_op jit(solution)/shard_map/ppermute | solution.py:367
  47.9 1.0 %shard_map.83 = bf16[256,1024]{1,0:T(8,128)(2,1)} custom-call(s32[1]{0:T(128)} %bitcast.places_ref._, f32[256,128]{1,0:T(8,128)S(1)} %get-tuple-element.83.refs_0_, f32[256,128]{1,0:T(8,128)S(1)} %get-tuple-element.84.refs_1_, f32[256,128]{1,0:T(8,128)S(1)} %get-tuple-element.97.refs_2_, f32[256,128]{1,0:T(8,128)S(1)} %get-tuple-element.98.refs_3_, ...), custom_call_target="tpu_custom_call" | custom-call | flops 786432 | bytes 1605636 | tf_op jit(solution)/shard_map/pallas_call | solution.py:210
  (63 shorter events, 5.7 us)
Async XLA Ops:
  0.0 7.6 %copy-start = (bf16[256,1024]{1,0:T(8,128)(2,1)S(1)}, bf16[256,1024]{1,0:T(8,128)(2,1)}, u32[]{:S(2)}) copy-start(bf16[256,1024]{1,0:T(8,128)(2,1)} %k_ref.7) | copy-start | bytes 1572868
  0.0 7.6 %copy-start.1 = (bf16[256,1024]{1,0:T(8,128)(2,1)S(1)}, bf16[256,1024]{1,0:T(8,128)(2,1)}, u32[]{:S(2)}) copy-start(bf16[256,1024]{1,0:T(8,128)(2,1)} %v_ref.7) | copy-start | bytes 1572868
  3.3 5.3 %collective-permute-start = (f32[136,256]{1,0:T(8,128)}, f32[136,256]{1,0:T(8,128)S(1)}, u32[]{:S(2)}, u32[]{:S(2)}) collective-permute-start(f32[136,256]{1,0:T(8,128)} %get-tuple-element.61), channel_id=1, source_target_pairs={{0,4},{4,0},{8,12},{12,8},{16,20},{20,16},{24,28},{28,24},{1,5},{5... | collective-permute-start | bytes 417800 | tf_op jit(solution)/shard_map/ppermute | solution.py:259
  4.6 3.0 %copy-start.4 = (f32[1024]{0:T(1024)S(1)}, f32[1024]{0:T(1024)}, u32[]{:S(2)}) copy-start(f32[1024]{0:T(1024)} %param.9) | copy-start | bytes 12292
  4.6 3.0 %copy-start.3 = (bf16[8,256]{1,0:T(8,128)(2,1)S(1)}, bf16[8,256]{1,0:T(8,128)(2,1)}, u32[]{:S(2)}) copy-start(bf16[8,256]{1,0:T(8,128)(2,1)} %seeds_ref.7) | copy-start | bytes 12292
  4.6 4.9 %collective-permute-start.1 = (f32[136,256]{1,0:T(8,128)}, f32[136,256]{1,0:T(8,128)S(1)}, u32[]{:S(2)}, u32[]{:S(2)}) collective-permute-start(f32[136,256]{1,0:T(8,128)} %get-tuple-element.62.refs_1_.refs_3_), channel_id=1, source_target_pairs={{0,8},{4,12},{1,9},{5,13},{2,10},{6,14},{3,11},{7,15}} | collective-permute-start | bytes 417800 | tf_op jit(solution)/shard_map/ppermute | solution.py:283
  5.4 5.8 %collective-permute-start.2 = (f32[128,256]{1,0:T(8,128)}, f32[128,256]{1,0:T(8,128)S(1)}, u32[]{:S(2)}, u32[]{:S(2)}) collective-permute-start(f32[128,256]{1,0:T(8,128)} %get-tuple-element.64), channel_id=1, source_target_pairs={{0,4},{4,0},{8,12},{12,8},{16,20},{20,16},{24,28},{28,24},{1,5},{5... | collective-permute-start | bytes 393224 | tf_op jit(solution)/shard_map/ppermute | solution.py:259
  5.7 8.3 %collective-permute-start.4 = (f32[128,256]{1,0:T(8,128)}, f32[128,256]{1,0:T(8,128)S(1)}, u32[]{:S(2)}, u32[]{:S(2)}) collective-permute-start(f32[128,256]{1,0:T(8,128)} %get-tuple-element.67), channel_id=1, source_target_pairs={{0,4},{4,0},{8,12},{12,8},{16,20},{20,16},{24,28},{28,24},{1,5},{5... | collective-permute-start | bytes 393224 | tf_op jit(solution)/shard_map/ppermute | solution.py:259
  7.0 5.1 %collective-permute-start.3 = (f32[136,256]{1,0:T(8,128)}, f32[136,256]{1,0:T(8,128)S(1)}, u32[]{:S(2)}, u32[]{:S(2)}) collective-permute-start(f32[136,256]{1,0:T(8,128)} %get-tuple-element.65.refs_1_.refs_3_), channel_id=1, source_target_pairs={{0,8},{4,12},{1,9},{5,13},{2,10},{6,14},{3,11},{7,15}} | collective-permute-start | bytes 417800 | tf_op jit(solution)/shard_map/ppermute | solution.py:283
  8.7 0.9 %copy-start.6 = (f32[136,256]{1,0:T(8,128)S(1)}, f32[136,256]{1,0:T(8,128)}, u32[]{:S(2)}) copy-start(f32[136,256]{1,0:T(8,128)} %get-tuple-element.62.refs_1_.refs_3_) | copy-start | bytes 417796
  8.7 6.0 %collective-permute-start.5 = (f32[136,256]{1,0:T(8,128)S(1)}, f32[136,256]{1,0:T(8,128)S(1)}, u32[]{:S(2)}, u32[]{:S(2)}) collective-permute-start(f32[136,256]{1,0:T(8,128)S(1)} %shard_map.57._), channel_id=1, source_target_pairs={{0,8},{4,12},{1,9},{5,13},{2,10},{6,14},{3,11},{7,15}} | collective-permute-start | bytes 417800 | tf_op jit(solution)/shard_map/ppermute | solution.py:283
  9.6 6.4 %collective-permute-start.6 = (f32[136,256]{1,0:T(8,128)S(1)}, f32[136,256]{1,0:T(8,128)S(1)}, u32[]{:S(2)}, u32[]{:S(2)}) collective-permute-start(f32[136,256]{1,0:T(8,128)S(1)} %shard_map.58._), channel_id=1, source_target_pairs={{8,16},{12,20},{9,17},{13,21},{10,18},{14,22},{11,19},{15,23}} | collective-permute-start | bytes 417800 | tf_op jit(solution)/shard_map/ppermute | solution.py:283
  11.2 7.5 %collective-permute-start.7 = (f32[128,256]{1,0:T(8,128)S(1)}, f32[128,256]{1,0:T(8,128)S(1)}, u32[]{:S(2)}, u32[]{:S(2)}) collective-permute-start(f32[128,256]{1,0:T(8,128)S(1)} %shard_map.59._), channel_id=1, source_target_pairs={{0,8},{4,12},{1,9},{5,13},{2,10},{6,14},{3,11},{7,15}} | collective-permute-start | bytes 393224 | tf_op jit(solution)/shard_map/ppermute | solution.py:283
  12.1 7.9 %collective-permute-start.8 = (f32[136,256]{1,0:T(8,128)S(1)}, f32[136,256]{1,0:T(8,128)S(1)}, u32[]{:S(2)}, u32[]{:S(2)}) collective-permute-start(f32[136,256]{1,0:T(8,128)S(1)} %shard_map.60._), channel_id=1, source_target_pairs={{8,16},{12,20},{9,17},{13,21},{10,18},{14,22},{11,19},{15,23}} | collective-permute-start | bytes 417800 | tf_op jit(solution)/shard_map/ppermute | solution.py:283
  14.0 7.3 %collective-permute-start.9 = (f32[128,256]{1,0:T(8,128)S(1)}, f32[128,256]{1,0:T(8,128)S(1)}, u32[]{:S(2)}, u32[]{:S(2)}) collective-permute-start(f32[128,256]{1,0:T(8,128)S(1)} %shard_map.61._), channel_id=1, source_target_pairs={{0,8},{4,12},{1,9},{5,13},{2,10},{6,14},{3,11},{7,15}} | collective-permute-start | bytes 393224 | tf_op jit(solution)/shard_map/ppermute | solution.py:283
  14.7 8.6 %collective-permute-start.10 = (f32[136,256]{1,0:T(8,128)S(1)}, f32[136,256]{1,0:T(8,128)S(1)}, u32[]{:S(2)}, u32[]{:S(2)}) collective-permute-start(f32[136,256]{1,0:T(8,128)S(1)} %shard_map.62._), channel_id=1, source_target_pairs={{8,16},{12,20},{9,17},{13,21},{10,18},{14,22},{11,19},{15,23}} | collective-permute-start | bytes 417800 | tf_op jit(solution)/shard_map/ppermute | solution.py:283
  16.1 8.6 %collective-permute-start.11 = (f32[136,256]{1,0:T(8,128)S(1)}, f32[136,256]{1,0:T(8,128)S(1)}, u32[]{:S(2)}, u32[]{:S(2)}) collective-permute-start(f32[136,256]{1,0:T(8,128)S(1)} %shard_map.63._), channel_id=1, source_target_pairs={{16,24},{20,28},{17,25},{21,29},{18,26},{22,30},{19,27},{23,31}} | collective-permute-start | bytes 417800 | tf_op jit(solution)/shard_map/ppermute | solution.py:283
  18.7 7.3 %collective-permute-start.12 = (f32[128,256]{1,0:T(8,128)S(1)}, f32[128,256]{1,0:T(8,128)S(1)}, u32[]{:S(2)}, u32[]{:S(2)}) collective-permute-start(f32[128,256]{1,0:T(8,128)S(1)} %shard_map.64._), channel_id=1, source_target_pairs={{8,16},{12,20},{9,17},{13,21},{10,18},{14,22},{11,19},{15,23}} | collective-permute-start | bytes 393224 | tf_op jit(solution)/shard_map/ppermute | solution.py:283
  20.1 7.3 %collective-permute-start.13 = (f32[136,256]{1,0:T(8,128)S(1)}, f32[136,256]{1,0:T(8,128)S(1)}, u32[]{:S(2)}, u32[]{:S(2)}) collective-permute-start(f32[136,256]{1,0:T(8,128)S(1)} %shard_map.65._), channel_id=1, source_target_pairs={{16,24},{20,28},{17,25},{21,29},{18,26},{22,30},{19,27},{23,31}} | collective-permute-start | bytes 417800 | tf_op jit(solution)/shard_map/ppermute | solution.py:283
  21.4 7.5 %collective-permute-start.14 = (f32[128,256]{1,0:T(8,128)S(1)}, f32[128,256]{1,0:T(8,128)S(1)}, u32[]{:S(2)}, u32[]{:S(2)}) collective-permute-start(f32[128,256]{1,0:T(8,128)S(1)} %shard_map.66._), channel_id=1, source_target_pairs={{8,16},{12,20},{9,17},{13,21},{10,18},{14,22},{11,19},{15,23}} | collective-permute-start | bytes 393224 | tf_op jit(solution)/shard_map/ppermute | solution.py:283
  23.3 7.0 %collective-permute-start.15 = (f32[136,256]{1,0:T(8,128)S(1)}, f32[136,256]{1,0:T(8,128)S(1)}, u32[]{:S(2)}, u32[]{:S(2)}) collective-permute-start(f32[136,256]{1,0:T(8,128)S(1)} %shard_map.67._), channel_id=1, source_target_pairs={{16,24},{20,28},{17,25},{21,29},{18,26},{22,30},{19,27},{23,31}} | collective-permute-start | bytes 417800 | tf_op jit(solution)/shard_map/ppermute | solution.py:283
  24.7 10.3 %collective-permute-start.18 = (f32[136,256]{1,0:T(8,128)S(1)}, f32[136,256]{1,0:T(8,128)S(1)}, u32[]{:S(2)}, u32[]{:S(2)}) collective-permute-start(f32[136,256]{1,0:T(8,128)S(1)} %get-tuple-element.68._), channel_id=1, source_target_pairs={{0,4},{4,0},{8,12},{12,8},{16,20},{20,16},{24,28},{28,24},{1,5},{5... | collective-permute-start | bytes 417800 | tf_op jit(solution)/shard_map/ppermute | solution.py:299
  26.1 5.8 %collective-permute-start.16 = (f32[128,256]{1,0:T(8,128)S(1)}, f32[128,256]{1,0:T(8,128)S(1)}, u32[]{:S(2)}, u32[]{:S(2)}) collective-permute-start(f32[128,256]{1,0:T(8,128)S(1)} %shard_map.69._), channel_id=1, source_target_pairs={{16,24},{20,28},{17,25},{21,29},{18,26},{22,30},{19,27},{23,31}} | collective-permute-start | bytes 393224 | tf_op jit(solution)/shard_map/ppermute | solution.py:283
  27.5 7.6 %collective-permute-start.19 = (f32[136,256]{1,0:T(8,128)S(1)}, f32[136,256]{1,0:T(8,128)S(1)}, u32[]{:S(2)}, u32[]{:S(2)}) collective-permute-start(f32[136,256]{1,0:T(8,128)S(1)} %get-tuple-element.69._), channel_id=1, source_target_pairs={{0,4},{4,0},{8,12},{12,8},{16,20},{20,16},{24,28},{28,24},{1,5},{5... | collective-permute-start | bytes 417800 | tf_op jit(solution)/shard_map/ppermute | solution.py:299
  28.9 1.9 %copy-start.2 = (bf16[256,1024]{1,0:T(8,128)(2,1)S(1)}, bf16[256,1024]{1,0:T(8,128)(2,1)}, u32[]{:S(2)}) copy-start(bf16[256,1024]{1,0:T(8,128)(2,1)} %q_ref.7) | copy-start | bytes 1572868
  28.9 4.2 %collective-permute-start.17 = (f32[128,256]{1,0:T(8,128)S(1)}, f32[128,256]{1,0:T(8,128)S(1)}, u32[]{:S(2)}, u32[]{:S(2)}) collective-permute-start(f32[128,256]{1,0:T(8,128)S(1)} %shard_map.71._), channel_id=1, source_target_pairs={{16,24},{20,28},{17,25},{21,29},{18,26},{22,30},{19,27},{23,31}} | collective-permute-start | bytes 393224 | tf_op jit(solution)/shard_map/ppermute | solution.py:283
  30.4 7.5 %collective-permute-start.20 = (f32[136,256]{1,0:T(8,128)S(1)}, f32[136,256]{1,0:T(8,128)S(1)}, u32[]{:S(2)}, u32[]{:S(2)}) collective-permute-start(f32[136,256]{1,0:T(8,128)S(1)} %get-tuple-element.70._), channel_id=1, source_target_pairs={{0,4},{4,0},{8,12},{12,8},{16,20},{20,16},{24,28},{28,24},{1,5},{5... | collective-permute-start | bytes 417800 | tf_op jit(solution)/shard_map/ppermute | solution.py:299
  31.9 6.0 %collective-permute-start.21 = (f32[128,256]{1,0:T(8,128)S(1)}, f32[128,256]{1,0:T(8,128)S(1)}, u32[]{:S(2)}, u32[]{:S(2)}) collective-permute-start(f32[128,256]{1,0:T(8,128)S(1)} %get-tuple-element.72._), channel_id=1, source_target_pairs={{0,4},{4,0},{8,12},{12,8},{16,20},{20,16},{24,28},{28,24},{1,5},{5... | collective-permute-start | bytes 393224 | tf_op jit(solution)/shard_map/ppermute | solution.py:299
  33.1 7.0 %collective-permute-start.22 = (f32[128,256]{1,0:T(8,128)S(1)}, f32[128,256]{1,0:T(8,128)S(1)}, u32[]{:S(2)}, u32[]{:S(2)}) collective-permute-start(f32[128,256]{1,0:T(8,128)S(1)} %get-tuple-element.73._), channel_id=1, source_target_pairs={{0,4},{4,0},{8,12},{12,8},{16,20},{20,16},{24,28},{28,24},{1,5},{5... | collective-permute-start | bytes 393224 | tf_op jit(solution)/shard_map/ppermute | solution.py:299
  40.6 6.2 %collective-permute-start.25 = (f32[8,256]{1,0:T(8,128)S(1)}, f32[8,256]{1,0:T(8,128)S(1)}, u32[]{:S(2)}, u32[]{:S(2)}) collective-permute-start(f32[8,256]{1,0:T(8,128)S(1)} %get-tuple-element.114.refs_8_), channel_id=1, source_target_pairs={{0,3},{1,2},{2,1},{3,0},{4,7},{5,6},{6,5},{7,4},{8,11},{9,10},{10,... | collective-permute-start | bytes 24584 | tf_op jit(solution)/shard_map/ppermute | solution.py:367
  45.4 2.5 %collective-permute-start.24 = (f32[8,256]{1,0:T(8,128)S(1)}, f32[8,256]{1,0:T(8,128)S(1)}, u32[]{:S(2)}, u32[]{:S(2)}) collective-permute-start(f32[8,256]{1,0:T(8,128)S(1)} %get-tuple-element.114.refs_8_), channel_id=1, source_target_pairs={{0,2},{1,3},{2,0},{3,1},{4,6},{5,7},{6,4},{7,5},{8,10},{9,11},{10,... | collective-permute-start | bytes 24584 | tf_op jit(solution)/shard_map/ppermute | solution.py:367
  45.5 2.4 %collective-permute-start.23 = (f32[8,256]{1,0:T(8,128)S(1)}, f32[8,256]{1,0:T(8,128)S(1)}, u32[]{:S(2)}, u32[]{:S(2)}) collective-permute-start(f32[8,256]{1,0:T(8,128)S(1)} %get-tuple-element.114.refs_8_), channel_id=1, source_target_pairs={{0,1},{1,0},{2,3},{3,2},{4,5},{5,4},{6,7},{7,6},{8,9},{9,8},{10,11... | collective-permute-start | bytes 24584 | tf_op jit(solution)/shard_map/ppermute | solution.py:367
  (1 other events, 0.9 us)

commit v5 on v4

--- a/solution.py
+++ b/solution.py
@@ -75,16 +75,17 @@
 def put_states(outs, cuts, seeds, base, at, k_ref, v_ref):
     size = cuts[0][1]
     outs[0][size:, :] = jnp.zeros((outs[0].shape[0] - size, outs[0].shape[1]), jnp.float32)
-    for i in range(cuts[-1][1] // WIDTH):
-        fk = features(k_ref[:, columns(at + i)], seeds, base + at + i)
-        state = lax.dot_general(
-            v_ref[:, columns(at + i)], fk, TN, preferred_element_type=jnp.float32
-        )
+    heads = range(cuts[-1][1] // WIDTH)
+    fks = [features(k_ref[:, columns(at + i)], seeds, base + at + i) for i in heads]
+    states = [
+        lax.dot_general(v_ref[:, columns(at + i)], fks[i], TN, preferred_element_type=jnp.float32)
+        for i in heads
+    ]
+    sums = [jnp.sum(fk.astype(jnp.float32), axis=0, keepdims=True) for fk in fks]
+    for i in heads:
         for n, rows, whole in overlaps(cuts, i):
-            outs[n][rows, :] = state[whole.start - i * WIDTH : whole.stop - i * WIDTH, :]
-        outs[0][size + i : size + i + 1, :] = jnp.sum(
-            fk.astype(jnp.float32), axis=0, keepdims=True
-        )
+            outs[n][rows, :] = states[i][whole.start - i * WIDTH : whole.stop - i * WIDTH, :]
+        outs[0][size + i : size + i + 1, :] = sums[i]
 
 
 def state_kernel(singles, cuts, which, places_ref, seeds_hbm, k_hbm, v_hbm, *refs):
@@ -124,24 +125,34 @@
     seeds = seeds_ref[...].astype(jnp.float32)
     rows = lax.broadcasted_iota(jnp.int32, (tok, tok), 0)
     causal = lax.broadcasted_iota(jnp.int32, (tok, tok), 1) <= rows
-    for n, (group, i) in enumerate(work):
-        num_ref, den_ref, fq_ref = outs[3 * n : 3 * n + 3]
+    places = []
+    for group, i in work:
         if group == 2:
-            head, mine, i = 2 * half + i, seeds, 2 * half + i
+            places.append((2 * half + i, seeds, 2 * half + i))
         else:
             first = first_of(group, half, places_ref)
-            head, mine = first + i, rotated(seeds, first)
-        fk = features(k_ref[:, columns(head)], mine, i)
-        fq = features(q_ref[:, columns(head)], mine, i)
-        fq_ref[...] = fq
-        scores = lax.dot_general(fq, fk, NT, preferred_element_type=jnp.float32)
-        scores = jnp.where(causal, scores, 0.0)
-        num_ref[...] = jnp.dot(
-            scores.astype(jnp.bfloat16),
+            places.append((first + i, rotated(seeds, first), i))
+    fks = [features(k_ref[:, columns(head)], mine, i) for head, mine, i in places]
+    fqs = [features(q_ref[:, columns(head)], mine, i) for head, mine, i in places]
+    scores = [
+        lax.dot_general(fq, fk, NT, preferred_element_type=jnp.float32)
+        for fq, fk in zip(fqs, fks)
+    ]
+    scores = [jnp.where(causal, score, 0.0) for score in scores]
+    nums = [
+        jnp.dot(
+            score.astype(jnp.bfloat16),
             v_ref[:, columns(head)],
             preferred_element_type=jnp.float32,
         )
-        den_ref[...] = jnp.broadcast_to(jnp.sum(scores, axis=1, keepdims=True), (tok, WIDTH))
+        for score, (head, _, _) in zip(scores, places)
+    ]
+    dens = [jnp.sum(score, axis=1, keepdims=True) for score in scores]
+    for n in range(len(work)):
+        num_ref, den_ref, fq_ref = outs[3 * n : 3 * n + 3]
+        fq_ref[...] = fqs[n]
+        num_ref[...] = nums[n]
+        den_ref[...] = jnp.broadcast_to(dens[n], (tok, WIDTH))
 
 
 def send_kernel(places_ref, _, *refs):

time: 49.2 us -> 48.8 us (level)
  Pallas kernels: 11.4 us -> 9.79 us
  starting transfers between devices: 29.4 us -> 30.2 us
    pallas_call x29, Pallas kernels: 11.4 us -> 9.79 us  [call(): pl.pallas_call(kernel, out_shape=outs, in_specs=[SMEM, *specs] + [place]...]
    ppermute x5, starting transfers between devices: 3.25 us -> 4.14 us  [hand(): passed[i] = lax.ppermute(last, 'seq', swap)]
    ppermute x5, waiting for transfers between devices: 1.92 us -> 2.75 us  [hand(): passed[i] = lax.ppermute(last, 'seq', swap)]
    ppermute x15, waiting for transfers between devices: 2.64 us -> 2.02 us  [hop(): arrivals[stage, i] = lax.ppermute(sent, 'seq', pairs)]
  transfers between devices with their start and end apart: 26 -> 26, of which waited for: 8 -> 9; matrix products, arithmetic and copies ran while one was open for 0% -> 0% of each run, Pallas kernels for 14% -> 11%
where the time goes in v5:
time: 48.8 us; the launch traced here: 48.5 us
  starting transfers between devices  30.2 us (62%)
  Pallas kernels  9.79 us (20%)
  waiting for transfers between devices  7.94 us (16%)
    ppermute x15, starting transfers between devices, hop(): arrivals[stage, i] = lax.ppermute(sent, 'seq', pairs)  18.1 us
    pallas_call x29, Pallas kernels, call(): pl.pallas_call(kernel, out_shape=outs, in_specs=[SMEM, *specs] + [place]...  9.79 us
    ppermute x3, starting transfers between devices, per_device(): lax.ppermute(squares, 'tp', [(i, i ^ k if across == 4 else (i + k) % acro...  5.13 us
    ppermute x5, starting transfers between devices, hand(): passed[i] = lax.ppermute(last, 'seq', swap)  4.14 us
    ppermute x3, starting transfers between devices, per_device(): incoming = [lax.ppermute(part, 'seq', swap) for part in [*theirs, *cross]]  2.81 us
    ppermute x5, waiting for transfers between devices, hand(): passed[i] = lax.ppermute(last, 'seq', swap)  2.75 us
    ppermute x3, waiting for transfers between devices, per_device(): lax.ppermute(squares, 'tp', [(i, i ^ k if across == 4 else (i + k) % acro...  2.03 us
    ppermute x15, waiting for transfers between devices, hop(): arrivals[stage, i] = lax.ppermute(sent, 'seq', pairs)  2.02 us
  transfers between devices with their start and end apart: 26, of which 9 were waited for; matrix products, arithmetic and copies ran while one was open for 0% of the time, Pallas kernels for 11%

profile of v5, /device:TPU:17, one launch (start us, length us, event | category | flops | bytes accessed | tf_op | source)
XLA Modules:
  0.0 48.5 jit_solution(9210084517047679332)
XLA Ops:
  0.0 3.1 %shard_map.56 = (f32[136,256]{1,0:T(8,128)}, f32[136,256]{1,0:T(8,128)}, f32[136,256]{1,0:T(8,128)}, f32[128,256]{1,0:T(8,128)}, f32[128,256]{1,0:T(8,128)}) custom-call(s32[1]{0:T(128)} %bitcast.places_ref._, bf16[8,256]{1,0:T(8,128)(2,1)} %seeds_ref.7, bf16[256,1024]{1,0:T(8,128)(2,1)} %k_ref.7, bf16[256,1024]{1,0:T(8,128)(2,1)} %v_ref.7), custom_call_target="tpu_custom_call" | custom-call | flops 167772160 | bytes 1732612 | tf_op jit(solution)/shard_map/pallas_call | solution.py:221
  3.1 1.3 %collective-permute-start = (f32[136,256]{1,0:T(8,128)}, f32[136,256]{1,0:T(8,128)S(1)}, u32[]{:S(2)}, u32[]{:S(2)}) collective-permute-start(f32[136,256]{1,0:T(8,128)} %get-tuple-element.61), channel_id=1, source_target_pairs={{0,4},{4,0},{8,12},{12,8},{16,20},{20,16},{24,28},{28,24},{1,5},{5... | collective-permute-start | bytes 417800 | tf_op jit(solution)/shard_map/ppermute | solution.py:270
  4.3 0.8 %collective-permute-start.1 = (f32[136,256]{1,0:T(8,128)}, f32[136,256]{1,0:T(8,128)S(1)}, u32[]{:S(2)}, u32[]{:S(2)}) collective-permute-start(f32[136,256]{1,0:T(8,128)} %get-tuple-element.62.refs_1_.refs_3_), channel_id=1, source_target_pairs={{0,8},{4,12},{1,9},{5,13},{2,10},{6,14},{3,11},{7,15}} | collective-permute-start | bytes 417800 | tf_op jit(solution)/shard_map/ppermute | solution.py:294
  5.5 1.2 %collective-permute-start.4 = (f32[128,256]{1,0:T(8,128)}, f32[128,256]{1,0:T(8,128)S(1)}, u32[]{:S(2)}, u32[]{:S(2)}) collective-permute-start(f32[128,256]{1,0:T(8,128)} %get-tuple-element.67), channel_id=1, source_target_pairs={{0,4},{4,0},{8,12},{12,8},{16,20},{20,16},{24,28},{28,24},{1,5},{5... | collective-permute-start | bytes 393224 | tf_op jit(solution)/shard_map/ppermute | solution.py:270
  7.4 0.7 %shard_map.55 = (f32[136,256]{1,0:T(8,128)S(1)}, f32[128,256]{1,0:T(8,128)S(1)}, f32[128,256]{1,0:T(8,128)S(1)}, f32[1,1024]{1,0:T(1,128)S(1)}) custom-call(s32[1]{0:T(128)} %bitcast.places_ref._, bf16[8,256]{1,0:T(8,128)(2,1)S(1)} %copy-done.3, bf16[256,1024]{1,0:T(8,128)(2,1)S(1)} %copy-done, bf16[256,1024]{1,0:T(8,128)(2,1)S(1)} %copy-done.1, ...), custom_call_target="tpu_custom_call" | custom-call | flops 100663296 | bytes 1462276 | tf_op jit(solution)/shard_map/pallas_call | solution.py:221
  8.2 0.8 %collective-permute-start.5 = (f32[136,256]{1,0:T(8,128)S(1)}, f32[136,256]{1,0:T(8,128)S(1)}, u32[]{:S(2)}, u32[]{:S(2)}) collective-permute-start(f32[136,256]{1,0:T(8,128)S(1)} %shard_map.57._), channel_id=1, source_target_pairs={{0,8},{4,12},{1,9},{5,13},{2,10},{6,14},{3,11},{7,15}} | collective-permute-start | bytes 417800 | tf_op jit(solution)/shard_map/ppermute | solution.py:294
  9.1 1.3 %collective-permute-start.6 = (f32[136,256]{1,0:T(8,128)S(1)}, f32[136,256]{1,0:T(8,128)S(1)}, u32[]{:S(2)}, u32[]{:S(2)}) collective-permute-start(f32[136,256]{1,0:T(8,128)S(1)} %shard_map.58._), channel_id=1, source_target_pairs={{8,16},{12,20},{9,17},{13,21},{10,18},{14,22},{11,19},{15,23}} | collective-permute-start | bytes 417800 | tf_op jit(solution)/shard_map/ppermute | solution.py:294
  10.9 0.8 %collective-permute-start.7 = (f32[128,256]{1,0:T(8,128)S(1)}, f32[128,256]{1,0:T(8,128)S(1)}, u32[]{:S(2)}, u32[]{:S(2)}) collective-permute-start(f32[128,256]{1,0:T(8,128)S(1)} %shard_map.59._), channel_id=1, source_target_pairs={{0,8},{4,12},{1,9},{5,13},{2,10},{6,14},{3,11},{7,15}} | collective-permute-start | bytes 393224 | tf_op jit(solution)/shard_map/ppermute | solution.py:294
  11.8 1.3 %collective-permute-start.8 = (f32[136,256]{1,0:T(8,128)S(1)}, f32[136,256]{1,0:T(8,128)S(1)}, u32[]{:S(2)}, u32[]{:S(2)}) collective-permute-start(f32[136,256]{1,0:T(8,128)S(1)} %shard_map.60._), channel_id=1, source_target_pairs={{8,16},{12,20},{9,17},{13,21},{10,18},{14,22},{11,19},{15,23}} | collective-permute-start | bytes 417800 | tf_op jit(solution)/shard_map/ppermute | solution.py:294
  13.7 0.7 %collective-permute-start.9 = (f32[128,256]{1,0:T(8,128)S(1)}, f32[128,256]{1,0:T(8,128)S(1)}, u32[]{:S(2)}, u32[]{:S(2)}) collective-permute-start(f32[128,256]{1,0:T(8,128)S(1)} %shard_map.61._), channel_id=1, source_target_pairs={{0,8},{4,12},{1,9},{5,13},{2,10},{6,14},{3,11},{7,15}} | collective-permute-start | bytes 393224 | tf_op jit(solution)/shard_map/ppermute | solution.py:294
  14.5 1.3 %collective-permute-start.10 = (f32[136,256]{1,0:T(8,128)S(1)}, f32[136,256]{1,0:T(8,128)S(1)}, u32[]{:S(2)}, u32[]{:S(2)}) collective-permute-start(f32[136,256]{1,0:T(8,128)S(1)} %shard_map.62._), channel_id=1, source_target_pairs={{8,16},{12,20},{9,17},{13,21},{10,18},{14,22},{11,19},{15,23}} | collective-permute-start | bytes 417800 | tf_op jit(solution)/shard_map/ppermute | solution.py:294
  15.8 2.6 %collective-permute-start.11 = (f32[136,256]{1,0:T(8,128)S(1)}, f32[136,256]{1,0:T(8,128)S(1)}, u32[]{:S(2)}, u32[]{:S(2)}) collective-permute-start(f32[136,256]{1,0:T(8,128)S(1)} %shard_map.63._), channel_id=1, source_target_pairs={{16,24},{20,28},{17,25},{21,29},{18,26},{22,30},{19,27},{23,31}} | collective-permute-start | bytes 417800 | tf_op jit(solution)/shard_map/ppermute | solution.py:294
  18.4 1.3 %collective-permute-start.12 = (f32[128,256]{1,0:T(8,128)S(1)}, f32[128,256]{1,0:T(8,128)S(1)}, u32[]{:S(2)}, u32[]{:S(2)}) collective-permute-start(f32[128,256]{1,0:T(8,128)S(1)} %shard_map.64._), channel_id=1, source_target_pairs={{8,16},{12,20},{9,17},{13,21},{10,18},{14,22},{11,19},{15,23}} | collective-permute-start | bytes 393224 | tf_op jit(solution)/shard_map/ppermute | solution.py:294
  19.8 1.3 %collective-permute-start.13 = (f32[136,256]{1,0:T(8,128)S(1)}, f32[136,256]{1,0:T(8,128)S(1)}, u32[]{:S(2)}, u32[]{:S(2)}) collective-permute-start(f32[136,256]{1,0:T(8,128)S(1)} %shard_map.65._), channel_id=1, source_target_pairs={{16,24},{20,28},{17,25},{21,29},{18,26},{22,30},{19,27},{23,31}} | collective-permute-start | bytes 417800 | tf_op jit(solution)/shard_map/ppermute | solution.py:294
  21.1 1.3 %collective-permute-start.14 = (f32[128,256]{1,0:T(8,128)S(1)}, f32[128,256]{1,0:T(8,128)S(1)}, u32[]{:S(2)}, u32[]{:S(2)}) collective-permute-start(f32[128,256]{1,0:T(8,128)S(1)} %shard_map.66._), channel_id=1, source_target_pairs={{8,16},{12,20},{9,17},{13,21},{10,18},{14,22},{11,19},{15,23}} | collective-permute-start | bytes 393224 | tf_op jit(solution)/shard_map/ppermute | solution.py:294
  22.6 1.3 %collective-permute-start.15 = (f32[136,256]{1,0:T(8,128)S(1)}, f32[136,256]{1,0:T(8,128)S(1)}, u32[]{:S(2)}, u32[]{:S(2)}) collective-permute-start(f32[136,256]{1,0:T(8,128)S(1)} %shard_map.67._), channel_id=1, source_target_pairs={{16,24},{20,28},{17,25},{21,29},{18,26},{22,30},{19,27},{23,31}} | collective-permute-start | bytes 417800 | tf_op jit(solution)/shard_map/ppermute | solution.py:294
  23.9 0.9 %collective-permute-start.18 = (f32[136,256]{1,0:T(8,128)S(1)}, f32[136,256]{1,0:T(8,128)S(1)}, u32[]{:S(2)}, u32[]{:S(2)}) collective-permute-start(f32[136,256]{1,0:T(8,128)S(1)} %get-tuple-element.68._), channel_id=1, source_target_pairs={{0,4},{4,0},{8,12},{12,8},{16,20},{20,16},{24,28},{28,24},{1,5},{5... | collective-permute-start | bytes 417800 | tf_op jit(solution)/shard_map/ppermute | solution.py:310
  24.9 0.8 %collective-permute-done.12.refs_0_.refs_1_ = f32[128,256]{1,0:T(8,128)S(1)} collective-permute-done((f32[128,256]{1,0:T(8,128)S(1)}, f32[128,256]{1,0:T(8,128)S(1)}, u32[]{:S(2)}, u32[]{:S(2)}) %collective-permute-start.12) | collective-permute-done | bytes 131104 | tf_op jit(solution)/shard_map/ppermute | solution.py:294
  25.7 1.3 %collective-permute-start.16 = (f32[128,256]{1,0:T(8,128)S(1)}, f32[128,256]{1,0:T(8,128)S(1)}, u32[]{:S(2)}, u32[]{:S(2)}) collective-permute-start(f32[128,256]{1,0:T(8,128)S(1)} %shard_map.69._), channel_id=1, source_target_pairs={{16,24},{20,28},{17,25},{21,29},{18,26},{22,30},{19,27},{23,31}} | collective-permute-start | bytes 393224 | tf_op jit(solution)/shard_map/ppermute | solution.py:294
  27.5 1.1 %collective-permute-done.14.refs_0_.refs_1_ = f32[128,256]{1,0:T(8,128)S(1)} collective-permute-done((f32[128,256]{1,0:T(8,128)S(1)}, f32[128,256]{1,0:T(8,128)S(1)}, u32[]{:S(2)}, u32[]{:S(2)}) %collective-permute-start.14) | collective-permute-done | bytes 131104 | tf_op jit(solution)/shard_map/ppermute | solution.py:294
  28.6 1.4 %collective-permute-start.17 = (f32[128,256]{1,0:T(8,128)S(1)}, f32[128,256]{1,0:T(8,128)S(1)}, u32[]{:S(2)}, u32[]{:S(2)}) collective-permute-start(f32[128,256]{1,0:T(8,128)S(1)} %shard_map.71._), channel_id=1, source_target_pairs={{16,24},{20,28},{17,25},{21,29},{18,26},{22,30},{19,27},{23,31}} | collective-permute-start | bytes 393224 | tf_op jit(solution)/shard_map/ppermute | solution.py:294
  30.5 0.7 %shard_map.73 = (f32[256,128]{1,0:T(8,128)S(1)}, f32[256,128]{1,0:T(8,128)S(1)}, bf16[256,256]{1,0:T(8,128)(2,1)S(1)}, f32[256,128]{1,0:T(8,128)S(1)}, f32[256,1...) custom-call(s32[1]{0:T(128)} %bitcast.places_ref._, f32[136,256]{1,0:T(8,128)S(1)} %get-tuple-element.70._, ...), custom_call_target="tpu_custom_call" | custom-call | flops 167772160 | bytes 2502660 | tf_op jit(solution)/shard_map/pallas_call | solution.py:221
  31.3 1.2 %collective-permute-start.21 = (f32[128,256]{1,0:T(8,128)S(1)}, f32[128,256]{1,0:T(8,128)S(1)}, u32[]{:S(2)}, u32[]{:S(2)}) collective-permute-start(f32[128,256]{1,0:T(8,128)S(1)} %get-tuple-element.72._), channel_id=1, source_target_pairs={{0,4},{4,0},{8,12},{12,8},{16,20},{20,16},{24,28},{28,24},{1,5},{5... | collective-permute-start | bytes 393224 | tf_op jit(solution)/shard_map/ppermute | solution.py:310
  32.6 1.2 %collective-permute-start.22 = (f32[128,256]{1,0:T(8,128)S(1)}, f32[128,256]{1,0:T(8,128)S(1)}, u32[]{:S(2)}, u32[]{:S(2)}) collective-permute-start(f32[128,256]{1,0:T(8,128)S(1)} %get-tuple-element.73._), channel_id=1, source_target_pairs={{0,4},{4,0},{8,12},{12,8},{16,20},{20,16},{24,28},{28,24},{1,5},{5... | collective-permute-start | bytes 393224 | tf_op jit(solution)/shard_map/ppermute | solution.py:310
  33.8 0.7 %shard_map.76 = (f32[256,128]{1,0:T(8,128)S(1)}, f32[256,128]{1,0:T(8,128)S(1)}, bf16[256,256]{1,0:T(8,128)(2,1)S(1)}, f32[256,128]{1,0:T(8,128)S(1)}, f32[256,1...) custom-call(s32[1]{0:T(128)} %bitcast.places_ref._, f32[128,256]{1,0:T(8,128)S(1)} %get-tuple-element.73._, ...), custom_call_target="tpu_custom_call" | custom-call | flops 167772160 | bytes 2494468 | tf_op jit(solution)/shard_map/pallas_call | solution.py:221
  34.9 0.7 %shard_map.78 = (f32[256,128]{1,0:T(8,128)S(1)}, f32[256,128]{1,0:T(8,128)S(1)}, bf16[256,256]{1,0:T(8,128)(2,1)S(1)}, f32[256,128]{1,0:T(8,128)S(1)}, f32[256,1...) custom-call(s32[1]{0:T(128)} %bitcast.places_ref._, f32[256,128]{1,0:T(8,128)S(1)} %get-tuple-element.85._.refs_15_, ...), custom_call_target="tpu_custom_call" | custom-call | flops 167772160 | bytes 2494468 | tf_op jit(solution)/shard_map/pallas_call | solution.py:221
  35.6 0.7 %shard_map.79 = (f32[256,128]{1,0:T(8,128)S(1)}, f32[256,128]{1,0:T(8,128)S(1)}, bf16[256,256]{1,0:T(8,128)(2,1)S(1)}, f32[256,128]{1,0:T(8,128)S(1)}, f32[256,1...) custom-call(s32[1]{0:T(128)} %bitcast.places_ref._, f32[256,128]{1,0:T(8,128)S(1)} %get-tuple-element.86._.refs_4_, ...), custom_call_target="tpu_custom_call" | custom-call | flops 167772160 | bytes 2494468 | tf_op jit(solution)/shard_map/pallas_call | solution.py:221
  37.7 2.3 %collective-permute-done.22.refs_5_ = f32[128,256]{1,0:T(8,128)S(1)} collective-permute-done((f32[128,256]{1,0:T(8,128)S(1)}, f32[128,256]{1,0:T(8,128)S(1)}, u32[]{:S(2)}, u32[]{:S(2)}) %collective-permute-start.22) | collective-permute-done | bytes 131104 | tf_op jit(solution)/shard_map/ppermute | solution.py:310
  40.3 4.7 %collective-permute-start.25 = (f32[8,256]{1,0:T(8,128)S(1)}, f32[8,256]{1,0:T(8,128)S(1)}, u32[]{:S(2)}, u32[]{:S(2)}) collective-permute-start(f32[8,256]{1,0:T(8,128)S(1)} %get-tuple-element.114.refs_8_), channel_id=1, source_target_pairs={{0,3},{1,2},{2,1},{3,0},{4,7},{5,6},{6,5},{7,4},{8,11},{9,10},{10,... | collective-permute-start | bytes 24584 | tf_op jit(solution)/shard_map/ppermute | solution.py:378
  45.4 1.1 %collective-permute-done.25.refs_11_ = f32[8,256]{1,0:T(8,128)S(1)} collective-permute-done((f32[8,256]{1,0:T(8,128)S(1)}, f32[8,256]{1,0:T(8,128)S(1)}, u32[]{:S(2)}, u32[]{:S(2)}) %collective-permute-start.25) | collective-permute-done | bytes 8224 | tf_op jit(solution)/shard_map/ppermute | solution.py:378
  46.5 0.9 %collective-permute-done.24.refs_10_ = f32[8,256]{1,0:T(8,128)S(1)} collective-permute-done((f32[8,256]{1,0:T(8,128)S(1)}, f32[8,256]{1,0:T(8,128)S(1)}, u32[]{:S(2)}, u32[]{:S(2)}) %collective-permute-start.24) | collective-permute-done | bytes 8224 | tf_op jit(solution)/shard_map/ppermute | solution.py:378
  47.5 1.0 %shard_map.83 = bf16[256,1024]{1,0:T(8,128)(2,1)} custom-call(s32[1]{0:T(128)} %bitcast.places_ref._, f32[256,128]{1,0:T(8,128)S(1)} %get-tuple-element.83.refs_0_, f32[256,128]{1,0:T(8,128)S(1)} %get-tuple-element.84.refs_1_, f32[256,128]{1,0:T(8,128)S(1)} %get-tuple-element.97.refs_2_, f32[256,128]{1,0:T(8,128)S(1)} %get-tuple-element.98.refs_3_, ...), custom_call_target="tpu_custom_call" | custom-call | flops 786432 | bytes 1605636 | tf_op jit(solution)/shard_map/pallas_call | solution.py:221
  (63 shorter events, 6.3 us)
Async XLA Ops:
  0.0 7.3 %copy-start = (bf16[256,1024]{1,0:T(8,128)(2,1)S(1)}, bf16[256,1024]{1,0:T(8,128)(2,1)}, u32[]{:S(2)}) copy-start(bf16[256,1024]{1,0:T(8,128)(2,1)} %k_ref.7) | copy-start | bytes 1572868
  0.0 7.3 %copy-start.1 = (bf16[256,1024]{1,0:T(8,128)(2,1)S(1)}, bf16[256,1024]{1,0:T(8,128)(2,1)}, u32[]{:S(2)}) copy-start(bf16[256,1024]{1,0:T(8,128)(2,1)} %v_ref.7) | copy-start | bytes 1572868
  3.1 5.1 %collective-permute-start = (f32[136,256]{1,0:T(8,128)}, f32[136,256]{1,0:T(8,128)S(1)}, u32[]{:S(2)}, u32[]{:S(2)}) collective-permute-start(f32[136,256]{1,0:T(8,128)} %get-tuple-element.61), channel_id=1, source_target_pairs={{0,4},{4,0},{8,12},{12,8},{16,20},{20,16},{24,28},{28,24},{1,5},{5... | collective-permute-start | bytes 417800 | tf_op jit(solution)/shard_map/ppermute | solution.py:270
  4.3 3.0 %copy-start.4 = (f32[1024]{0:T(1024)S(1)}, f32[1024]{0:T(1024)}, u32[]{:S(2)}) copy-start(f32[1024]{0:T(1024)} %param.9) | copy-start | bytes 12292
  4.3 3.0 %copy-start.3 = (bf16[8,256]{1,0:T(8,128)(2,1)S(1)}, bf16[8,256]{1,0:T(8,128)(2,1)}, u32[]{:S(2)}) copy-start(bf16[8,256]{1,0:T(8,128)(2,1)} %seeds_ref.7) | copy-start | bytes 12292
  4.3 4.6 %collective-permute-start.1 = (f32[136,256]{1,0:T(8,128)}, f32[136,256]{1,0:T(8,128)S(1)}, u32[]{:S(2)}, u32[]{:S(2)}) collective-permute-start(f32[136,256]{1,0:T(8,128)} %get-tuple-element.62.refs_1_.refs_3_), channel_id=1, source_target_pairs={{0,8},{4,12},{1,9},{5,13},{2,10},{6,14},{3,11},{7,15}} | collective-permute-start | bytes 417800 | tf_op jit(solution)/shard_map/ppermute | solution.py:294
  5.1 5.8 %collective-permute-start.2 = (f32[128,256]{1,0:T(8,128)}, f32[128,256]{1,0:T(8,128)S(1)}, u32[]{:S(2)}, u32[]{:S(2)}) collective-permute-start(f32[128,256]{1,0:T(8,128)} %get-tuple-element.64), channel_id=1, source_target_pairs={{0,4},{4,0},{8,12},{12,8},{16,20},{20,16},{24,28},{28,24},{1,5},{5... | collective-permute-start | bytes 393224 | tf_op jit(solution)/shard_map/ppermute | solution.py:270
  5.5 8.3 %collective-permute-start.4 = (f32[128,256]{1,0:T(8,128)}, f32[128,256]{1,0:T(8,128)S(1)}, u32[]{:S(2)}, u32[]{:S(2)}) collective-permute-start(f32[128,256]{1,0:T(8,128)} %get-tuple-element.67), channel_id=1, source_target_pairs={{0,4},{4,0},{8,12},{12,8},{16,20},{20,16},{24,28},{28,24},{1,5},{5... | collective-permute-start | bytes 393224 | tf_op jit(solution)/shard_map/ppermute | solution.py:270
  6.7 5.1 %collective-permute-start.3 = (f32[136,256]{1,0:T(8,128)}, f32[136,256]{1,0:T(8,128)S(1)}, u32[]{:S(2)}, u32[]{:S(2)}) collective-permute-start(f32[136,256]{1,0:T(8,128)} %get-tuple-element.65.refs_1_.refs_3_), channel_id=1, source_target_pairs={{0,8},{4,12},{1,9},{5,13},{2,10},{6,14},{3,11},{7,15}} | collective-permute-start | bytes 417800 | tf_op jit(solution)/shard_map/ppermute | solution.py:294
  8.1 0.9 %copy-start.6 = (f32[136,256]{1,0:T(8,128)S(1)}, f32[136,256]{1,0:T(8,128)}, u32[]{:S(2)}) copy-start(f32[136,256]{1,0:T(8,128)} %get-tuple-element.62.refs_1_.refs_3_) | copy-start | bytes 417796
  8.2 6.3 %collective-permute-start.5 = (f32[136,256]{1,0:T(8,128)S(1)}, f32[136,256]{1,0:T(8,128)S(1)}, u32[]{:S(2)}, u32[]{:S(2)}) collective-permute-start(f32[136,256]{1,0:T(8,128)S(1)} %shard_map.57._), channel_id=1, source_target_pairs={{0,8},{4,12},{1,9},{5,13},{2,10},{6,14},{3,11},{7,15}} | collective-permute-start | bytes 417800 | tf_op jit(solution)/shard_map/ppermute | solution.py:294
  9.1 6.7 %collective-permute-start.6 = (f32[136,256]{1,0:T(8,128)S(1)}, f32[136,256]{1,0:T(8,128)S(1)}, u32[]{:S(2)}, u32[]{:S(2)}) collective-permute-start(f32[136,256]{1,0:T(8,128)S(1)} %shard_map.58._), channel_id=1, source_target_pairs={{8,16},{12,20},{9,17},{13,21},{10,18},{14,22},{11,19},{15,23}} | collective-permute-start | bytes 417800 | tf_op jit(solution)/shard_map/ppermute | solution.py:294
  10.9 7.5 %collective-permute-start.7 = (f32[128,256]{1,0:T(8,128)S(1)}, f32[128,256]{1,0:T(8,128)S(1)}, u32[]{:S(2)}, u32[]{:S(2)}) collective-permute-start(f32[128,256]{1,0:T(8,128)S(1)} %shard_map.59._), channel_id=1, source_target_pairs={{0,8},{4,12},{1,9},{5,13},{2,10},{6,14},{3,11},{7,15}} | collective-permute-start | bytes 393224 | tf_op jit(solution)/shard_map/ppermute | solution.py:294
  11.8 7.9 %collective-permute-start.8 = (f32[136,256]{1,0:T(8,128)S(1)}, f32[136,256]{1,0:T(8,128)S(1)}, u32[]{:S(2)}, u32[]{:S(2)}) collective-permute-start(f32[136,256]{1,0:T(8,128)S(1)} %shard_map.60._), channel_id=1, source_target_pairs={{8,16},{12,20},{9,17},{13,21},{10,18},{14,22},{11,19},{15,23}} | collective-permute-start | bytes 417800 | tf_op jit(solution)/shard_map/ppermute | solution.py:294
  13.7 7.3 %collective-permute-start.9 = (f32[128,256]{1,0:T(8,128)S(1)}, f32[128,256]{1,0:T(8,128)S(1)}, u32[]{:S(2)}, u32[]{:S(2)}) collective-permute-start(f32[128,256]{1,0:T(8,128)S(1)} %shard_map.61._), channel_id=1, source_target_pairs={{0,8},{4,12},{1,9},{5,13},{2,10},{6,14},{3,11},{7,15}} | collective-permute-start | bytes 393224 | tf_op jit(solution)/shard_map/ppermute | solution.py:294
  14.5 8.1 %collective-permute-start.10 = (f32[136,256]{1,0:T(8,128)S(1)}, f32[136,256]{1,0:T(8,128)S(1)}, u32[]{:S(2)}, u32[]{:S(2)}) collective-permute-start(f32[136,256]{1,0:T(8,128)S(1)} %shard_map.62._), channel_id=1, source_target_pairs={{8,16},{12,20},{9,17},{13,21},{10,18},{14,22},{11,19},{15,23}} | collective-permute-start | bytes 417800 | tf_op jit(solution)/shard_map/ppermute | solution.py:294
  15.8 8.1 %collective-permute-start.11 = (f32[136,256]{1,0:T(8,128)S(1)}, f32[136,256]{1,0:T(8,128)S(1)}, u32[]{:S(2)}, u32[]{:S(2)}) collective-permute-start(f32[136,256]{1,0:T(8,128)S(1)} %shard_map.63._), channel_id=1, source_target_pairs={{16,24},{20,28},{17,25},{21,29},{18,26},{22,30},{19,27},{23,31}} | collective-permute-start | bytes 417800 | tf_op jit(solution)/shard_map/ppermute | solution.py:294
  18.4 7.2 %collective-permute-start.12 = (f32[128,256]{1,0:T(8,128)S(1)}, f32[128,256]{1,0:T(8,128)S(1)}, u32[]{:S(2)}, u32[]{:S(2)}) collective-permute-start(f32[128,256]{1,0:T(8,128)S(1)} %shard_map.64._), channel_id=1, source_target_pairs={{8,16},{12,20},{9,17},{13,21},{10,18},{14,22},{11,19},{15,23}} | collective-permute-start | bytes 393224 | tf_op jit(solution)/shard_map/ppermute | solution.py:294
  19.8 7.2 %collective-permute-start.13 = (f32[136,256]{1,0:T(8,128)S(1)}, f32[136,256]{1,0:T(8,128)S(1)}, u32[]{:S(2)}, u32[]{:S(2)}) collective-permute-start(f32[136,256]{1,0:T(8,128)S(1)} %shard_map.65._), channel_id=1, source_target_pairs={{16,24},{20,28},{17,25},{21,29},{18,26},{22,30},{19,27},{23,31}} | collective-permute-start | bytes 417800 | tf_op jit(solution)/shard_map/ppermute | solution.py:294
  21.1 7.5 %collective-permute-start.14 = (f32[128,256]{1,0:T(8,128)S(1)}, f32[128,256]{1,0:T(8,128)S(1)}, u32[]{:S(2)}, u32[]{:S(2)}) collective-permute-start(f32[128,256]{1,0:T(8,128)S(1)} %shard_map.66._), channel_id=1, source_target_pairs={{8,16},{12,20},{9,17},{13,21},{10,18},{14,22},{11,19},{15,23}} | collective-permute-start | bytes 393224 | tf_op jit(solution)/shard_map/ppermute | solution.py:294
  22.6 7.5 %collective-permute-start.15 = (f32[136,256]{1,0:T(8,128)S(1)}, f32[136,256]{1,0:T(8,128)S(1)}, u32[]{:S(2)}, u32[]{:S(2)}) collective-permute-start(f32[136,256]{1,0:T(8,128)S(1)} %shard_map.67._), channel_id=1, source_target_pairs={{16,24},{20,28},{17,25},{21,29},{18,26},{22,30},{19,27},{23,31}} | collective-permute-start | bytes 417800 | tf_op jit(solution)/shard_map/ppermute | solution.py:294
  23.9 10.6 %collective-permute-start.18 = (f32[136,256]{1,0:T(8,128)S(1)}, f32[136,256]{1,0:T(8,128)S(1)}, u32[]{:S(2)}, u32[]{:S(2)}) collective-permute-start(f32[136,256]{1,0:T(8,128)S(1)} %get-tuple-element.68._), channel_id=1, source_target_pairs={{0,4},{4,0},{8,12},{12,8},{16,20},{20,16},{24,28},{28,24},{1,5},{5... | collective-permute-start | bytes 417800 | tf_op jit(solution)/shard_map/ppermute | solution.py:310
  25.7 5.6 %collective-permute-start.16 = (f32[128,256]{1,0:T(8,128)S(1)}, f32[128,256]{1,0:T(8,128)S(1)}, u32[]{:S(2)}, u32[]{:S(2)}) collective-permute-start(f32[128,256]{1,0:T(8,128)S(1)} %shard_map.69._), channel_id=1, source_target_pairs={{16,24},{20,28},{17,25},{21,29},{18,26},{22,30},{19,27},{23,31}} | collective-permute-start | bytes 393224 | tf_op jit(solution)/shard_map/ppermute | solution.py:294
  27.0 7.5 %collective-permute-start.19 = (f32[136,256]{1,0:T(8,128)S(1)}, f32[136,256]{1,0:T(8,128)S(1)}, u32[]{:S(2)}, u32[]{:S(2)}) collective-permute-start(f32[136,256]{1,0:T(8,128)S(1)} %get-tuple-element.69._), channel_id=1, source_target_pairs={{0,4},{4,0},{8,12},{12,8},{16,20},{20,16},{24,28},{28,24},{1,5},{5... | collective-permute-start | bytes 417800 | tf_op jit(solution)/shard_map/ppermute | solution.py:310
  28.6 1.9 %copy-start.2 = (bf16[256,1024]{1,0:T(8,128)(2,1)S(1)}, bf16[256,1024]{1,0:T(8,128)(2,1)}, u32[]{:S(2)}) copy-start(bf16[256,1024]{1,0:T(8,128)(2,1)} %q_ref.7) | copy-start | bytes 1572868
  28.6 3.9 %collective-permute-start.17 = (f32[128,256]{1,0:T(8,128)S(1)}, f32[128,256]{1,0:T(8,128)S(1)}, u32[]{:S(2)}, u32[]{:S(2)}) collective-permute-start(f32[128,256]{1,0:T(8,128)S(1)} %shard_map.71._), channel_id=1, source_target_pairs={{16,24},{20,28},{17,25},{21,29},{18,26},{22,30},{19,27},{23,31}} | collective-permute-start | bytes 393224 | tf_op jit(solution)/shard_map/ppermute | solution.py:294
  30.2 7.1 %collective-permute-start.20 = (f32[136,256]{1,0:T(8,128)S(1)}, f32[136,256]{1,0:T(8,128)S(1)}, u32[]{:S(2)}, u32[]{:S(2)}) collective-permute-start(f32[136,256]{1,0:T(8,128)S(1)} %get-tuple-element.70._), channel_id=1, source_target_pairs={{0,4},{4,0},{8,12},{12,8},{16,20},{20,16},{24,28},{28,24},{1,5},{5... | collective-permute-start | bytes 417800 | tf_op jit(solution)/shard_map/ppermute | solution.py:310
  31.3 6.0 %collective-permute-start.21 = (f32[128,256]{1,0:T(8,128)S(1)}, f32[128,256]{1,0:T(8,128)S(1)}, u32[]{:S(2)}, u32[]{:S(2)}) collective-permute-start(f32[128,256]{1,0:T(8,128)S(1)} %get-tuple-element.72._), channel_id=1, source_target_pairs={{0,4},{4,0},{8,12},{12,8},{16,20},{20,16},{24,28},{28,24},{1,5},{5... | collective-permute-start | bytes 393224 | tf_op jit(solution)/shard_map/ppermute | solution.py:310
  32.6 7.3 %collective-permute-start.22 = (f32[128,256]{1,0:T(8,128)S(1)}, f32[128,256]{1,0:T(8,128)S(1)}, u32[]{:S(2)}, u32[]{:S(2)}) collective-permute-start(f32[128,256]{1,0:T(8,128)S(1)} %get-tuple-element.73._), channel_id=1, source_target_pairs={{0,4},{4,0},{8,12},{12,8},{16,20},{20,16},{24,28},{28,24},{1,5},{5... | collective-permute-start | bytes 393224 | tf_op jit(solution)/shard_map/ppermute | solution.py:310
  40.3 6.2 %collective-permute-start.25 = (f32[8,256]{1,0:T(8,128)S(1)}, f32[8,256]{1,0:T(8,128)S(1)}, u32[]{:S(2)}, u32[]{:S(2)}) collective-permute-start(f32[8,256]{1,0:T(8,128)S(1)} %get-tuple-element.114.refs_8_), channel_id=1, source_target_pairs={{0,3},{1,2},{2,1},{3,0},{4,7},{5,6},{6,5},{7,4},{8,11},{9,10},{10,... | collective-permute-start | bytes 24584 | tf_op jit(solution)/shard_map/ppermute | solution.py:378
  45.0 2.5 %collective-permute-start.24 = (f32[8,256]{1,0:T(8,128)S(1)}, f32[8,256]{1,0:T(8,128)S(1)}, u32[]{:S(2)}, u32[]{:S(2)}) collective-permute-start(f32[8,256]{1,0:T(8,128)S(1)} %get-tuple-element.114.refs_8_), channel_id=1, source_target_pairs={{0,2},{1,3},{2,0},{3,1},{4,6},{5,7},{6,4},{7,5},{8,10},{9,11},{10,... | collective-permute-start | bytes 24584 | tf_op jit(solution)/shard_map/ppermute | solution.py:378
  45.2 2.3 %collective-permute-start.23 = (f32[8,256]{1,0:T(8,128)S(1)}, f32[8,256]{1,0:T(8,128)S(1)}, u32[]{:S(2)}, u32[]{:S(2)}) collective-permute-start(f32[8,256]{1,0:T(8,128)S(1)} %get-tuple-element.114.refs_8_), channel_id=1, source_target_pairs={{0,1},{1,0},{2,3},{3,2},{4,5},{5,4},{6,7},{7,6},{8,9},{9,8},{10,11... | collective-permute-start | bytes 24584 | tf_op jit(solution)/shard_map/ppermute | solution.py:378
  (1 other events, 0.9 us)

commit v6 on v5

--- a/solution.py
+++ b/solution.py
@@ -72,20 +72,26 @@
     return found
 
 
-def put_states(outs, cuts, seeds, base, at, k_ref, v_ref):
-    size = cuts[0][1]
-    outs[0][size:, :] = jnp.zeros((outs[0].shape[0] - size, outs[0].shape[1]), jnp.float32)
-    heads = range(cuts[-1][1] // WIDTH)
-    fks = [features(k_ref[:, columns(at + i)], seeds, base + at + i) for i in heads]
+def put_states(jobs):
+    places = [(job, i) for job in jobs for i in range(job[1][-1][1] // WIDTH)]
+    fks = [
+        features(k_ref[:, columns(at + i)], seeds, base + at + i)
+        for (_, _, seeds, base, at, k_ref, _), i in places
+    ]
     states = [
-        lax.dot_general(v_ref[:, columns(at + i)], fks[i], TN, preferred_element_type=jnp.float32)
-        for i in heads
+        lax.dot_general(v_ref[:, columns(at + i)], fk, TN, preferred_element_type=jnp.float32)
+        for ((_, _, _, _, at, _, v_ref), i), fk in zip(places, fks)
     ]
     sums = [jnp.sum(fk.astype(jnp.float32), axis=0, keepdims=True) for fk in fks]
-    for i in heads:
+    for ((outs, cuts, *_), i), state, total in zip(places, states, sums):
+        size = cuts[0][1]
+        if i == 0:
+            outs[0][size:, :] = jnp.zeros(
+                (outs[0].shape[0] - size, outs[0].shape[1]), jnp.float32
+            )
         for n, rows, whole in overlaps(cuts, i):
-            outs[n][rows, :] = states[i][whole.start - i * WIDTH : whole.stop - i * WIDTH, :]
-        outs[0][size + i : size + i + 1, :] = sums[i]
+            outs[n][rows, :] = state[whole.start - i * WIDTH : whole.stop - i * WIDTH, :]
+        outs[0][size + i : size + i + 1, :] = total
 
 
 def state_kernel(singles, cuts, which, places_ref, seeds_hbm, k_hbm, v_hbm, *refs):
@@ -108,16 +114,14 @@
         copy.start()
     copies[0].wait()
     seeds = seeds_ref[...].astype(jnp.float32)
-    if alone:
-        copies[1].wait()
-        copies[2].wait()
-        at = 0
-        for n, size in enumerate(singles):
-            put_states([outs[n]], bounds(size, 1), seeds, 2 * half, at, kd_ref, vd_ref)
-            at += size
-    for copy in copies[3 if alone else 1 :]:
+    for copy in copies[1:]:
         copy.wait()
-    put_states(outs[len(singles) :], cuts, rotated(seeds, first), 0, 0, k_ref, v_ref)
+    jobs, at = [], 0
+    for n, size in enumerate(singles):
+        jobs.append(([outs[n]], bounds(size, 1), seeds, 2 * half, at, kd_ref, vd_ref))
+        at += size
+    jobs.append((outs[len(singles) :], cuts, rotated(seeds, first), 0, 0, k_ref, v_ref))
+    put_states(jobs)
 
 
 def local_kernel(half, work, places_ref, _, seeds_ref, q_ref, k_ref, v_ref, *outs):

time: 48.8 us -> 48.5 us (level)
  no operation moved by 1% of the time
where the time goes in v6:
time: 48.5 us; the launch traced here: 48.1 us
  starting transfers between devices  30.2 us (62%)
  Pallas kernels  9.47 us (20%)
  waiting for transfers between devices  7.92 us (16%)
    ppermute x15, starting transfers between devices, hop(): arrivals[stage, i] = lax.ppermute(sent, 'seq', pairs)  18.1 us
    pallas_call x29, Pallas kernels, call(): pl.pallas_call(kernel, out_shape=outs, in_specs=[SMEM, *specs] + [place]...  9.47 us
    ppermute x3, starting transfers between devices, per_device(): lax.ppermute(squares, 'tp', [(i, i ^ k if across == 4 else (i + k) % acro...  5.14 us
    ppermute x5, starting transfers between devices, hand(): passed[i] = lax.ppermute(last, 'seq', swap)  4.16 us
    ppermute x3, starting transfers between devices, per_device(): incoming = [lax.ppermute(part, 'seq', swap) for part in [*theirs, *cross]]  2.81 us
    ppermute x5, waiting for transfers between devices, hand(): passed[i] = lax.ppermute(last, 'seq', swap)  2.74 us
    ppermute x3, waiting for transfers between devices, per_device(): lax.ppermute(squares, 'tp', [(i, i ^ k if across == 4 else (i + k) % acro...  2.03 us
    ppermute x15, waiting for transfers between devices, hop(): arrivals[stage, i] = lax.ppermute(sent, 'seq', pairs)  2.01 us
  transfers between devices with their start and end apart: 26, of which 9 were waited for; matrix products, arithmetic and copies ran while one was open for 0% of the time, Pallas kernels for 11%

profile of v6, /device:TPU:17, one launch (start us, length us, event | category | flops | bytes accessed | tf_op | source)
XLA Modules:
  0.0 48.1 jit_solution(5109143286017509096)
XLA Ops:
  0.0 2.7 %shard_map.56 = (f32[136,256]{1,0:T(8,128)}, f32[136,256]{1,0:T(8,128)}, f32[136,256]{1,0:T(8,128)}, f32[128,256]{1,0:T(8,128)}, f32[128,256]{1,0:T(8,128)}) custom-call(s32[1]{0:T(128)} %bitcast.places_ref._, bf16[8,256]{1,0:T(8,128)(2,1)} %seeds_ref.7, bf16[256,1024]{1,0:T(8,128)(2,1)} %k_ref.7, bf16[256,1024]{1,0:T(8,128)(2,1)} %v_ref.7), custom_call_target="tpu_custom_call" | custom-call | flops 167772160 | bytes 1732612 | tf_op jit(solution)/shard_map/pallas_call | solution.py:225
  2.8 1.3 %collective-permute-start = (f32[136,256]{1,0:T(8,128)}, f32[136,256]{1,0:T(8,128)S(1)}, u32[]{:S(2)}, u32[]{:S(2)}) collective-permute-start(f32[136,256]{1,0:T(8,128)} %get-tuple-element.61), channel_id=1, source_target_pairs={{0,4},{4,0},{8,12},{12,8},{16,20},{20,16},{24,28},{28,24},{1,5},{5... | collective-permute-start | bytes 417800 | tf_op jit(solution)/shard_map/ppermute | solution.py:274
  4.0 0.8 %collective-permute-start.1 = (f32[136,256]{1,0:T(8,128)}, f32[136,256]{1,0:T(8,128)S(1)}, u32[]{:S(2)}, u32[]{:S(2)}) collective-permute-start(f32[136,256]{1,0:T(8,128)} %get-tuple-element.62.refs_1_.refs_3_), channel_id=1, source_target_pairs={{0,8},{4,12},{1,9},{5,13},{2,10},{6,14},{3,11},{7,15}} | collective-permute-start | bytes 417800 | tf_op jit(solution)/shard_map/ppermute | solution.py:298
  5.2 1.2 %collective-permute-start.4 = (f32[128,256]{1,0:T(8,128)}, f32[128,256]{1,0:T(8,128)S(1)}, u32[]{:S(2)}, u32[]{:S(2)}) collective-permute-start(f32[128,256]{1,0:T(8,128)} %get-tuple-element.67), channel_id=1, source_target_pairs={{0,4},{4,0},{8,12},{12,8},{16,20},{20,16},{24,28},{28,24},{1,5},{5... | collective-permute-start | bytes 393224 | tf_op jit(solution)/shard_map/ppermute | solution.py:274
  7.1 0.7 %shard_map.55 = (f32[136,256]{1,0:T(8,128)S(1)}, f32[128,256]{1,0:T(8,128)S(1)}, f32[128,256]{1,0:T(8,128)S(1)}, f32[1,1024]{1,0:T(1,128)S(1)}) custom-call(s32[1]{0:T(128)} %bitcast.places_ref._, bf16[8,256]{1,0:T(8,128)(2,1)S(1)} %copy-done.3, bf16[256,1024]{1,0:T(8,128)(2,1)S(1)} %copy-done, bf16[256,1024]{1,0:T(8,128)(2,1)S(1)} %copy-done.1, ...), custom_call_target="tpu_custom_call" | custom-call | flops 100663296 | bytes 1462276 | tf_op jit(solution)/shard_map/pallas_call | solution.py:225
  7.9 0.8 %collective-permute-start.5 = (f32[136,256]{1,0:T(8,128)S(1)}, f32[136,256]{1,0:T(8,128)S(1)}, u32[]{:S(2)}, u32[]{:S(2)}) collective-permute-start(f32[136,256]{1,0:T(8,128)S(1)} %shard_map.57._), channel_id=1, source_target_pairs={{0,8},{4,12},{1,9},{5,13},{2,10},{6,14},{3,11},{7,15}} | collective-permute-start | bytes 417800 | tf_op jit(solution)/shard_map/ppermute | solution.py:298
  8.8 1.3 %collective-permute-start.6 = (f32[136,256]{1,0:T(8,128)S(1)}, f32[136,256]{1,0:T(8,128)S(1)}, u32[]{:S(2)}, u32[]{:S(2)}) collective-permute-start(f32[136,256]{1,0:T(8,128)S(1)} %shard_map.58._), channel_id=1, source_target_pairs={{8,16},{12,20},{9,17},{13,21},{10,18},{14,22},{11,19},{15,23}} | collective-permute-start | bytes 417800 | tf_op jit(solution)/shard_map/ppermute | solution.py:298
  10.6 0.8 %collective-permute-start.7 = (f32[128,256]{1,0:T(8,128)S(1)}, f32[128,256]{1,0:T(8,128)S(1)}, u32[]{:S(2)}, u32[]{:S(2)}) collective-permute-start(f32[128,256]{1,0:T(8,128)S(1)} %shard_map.59._), channel_id=1, source_target_pairs={{0,8},{4,12},{1,9},{5,13},{2,10},{6,14},{3,11},{7,15}} | collective-permute-start | bytes 393224 | tf_op jit(solution)/shard_map/ppermute | solution.py:298
  11.5 1.3 %collective-permute-start.8 = (f32[136,256]{1,0:T(8,128)S(1)}, f32[136,256]{1,0:T(8,128)S(1)}, u32[]{:S(2)}, u32[]{:S(2)}) collective-permute-start(f32[136,256]{1,0:T(8,128)S(1)} %shard_map.60._), channel_id=1, source_target_pairs={{8,16},{12,20},{9,17},{13,21},{10,18},{14,22},{11,19},{15,23}} | collective-permute-start | bytes 417800 | tf_op jit(solution)/shard_map/ppermute | solution.py:298
  13.4 0.7 %collective-permute-start.9 = (f32[128,256]{1,0:T(8,128)S(1)}, f32[128,256]{1,0:T(8,128)S(1)}, u32[]{:S(2)}, u32[]{:S(2)}) collective-permute-start(f32[128,256]{1,0:T(8,128)S(1)} %shard_map.61._), channel_id=1, source_target_pairs={{0,8},{4,12},{1,9},{5,13},{2,10},{6,14},{3,11},{7,15}} | collective-permute-start | bytes 393224 | tf_op jit(solution)/shard_map/ppermute | solution.py:298
  14.2 1.3 %collective-permute-start.10 = (f32[136,256]{1,0:T(8,128)S(1)}, f32[136,256]{1,0:T(8,128)S(1)}, u32[]{:S(2)}, u32[]{:S(2)}) collective-permute-start(f32[136,256]{1,0:T(8,128)S(1)} %shard_map.62._), channel_id=1, source_target_pairs={{8,16},{12,20},{9,17},{13,21},{10,18},{14,22},{11,19},{15,23}} | collective-permute-start | bytes 417800 | tf_op jit(solution)/shard_map/ppermute | solution.py:298
  15.5 2.6 %collective-permute-start.11 = (f32[136,256]{1,0:T(8,128)S(1)}, f32[136,256]{1,0:T(8,128)S(1)}, u32[]{:S(2)}, u32[]{:S(2)}) collective-permute-start(f32[136,256]{1,0:T(8,128)S(1)} %shard_map.63._), channel_id=1, source_target_pairs={{16,24},{20,28},{17,25},{21,29},{18,26},{22,30},{19,27},{23,31}} | collective-permute-start | bytes 417800 | tf_op jit(solution)/shard_map/ppermute | solution.py:298
  18.1 1.3 %collective-permute-start.12 = (f32[128,256]{1,0:T(8,128)S(1)}, f32[128,256]{1,0:T(8,128)S(1)}, u32[]{:S(2)}, u32[]{:S(2)}) collective-permute-start(f32[128,256]{1,0:T(8,128)S(1)} %shard_map.64._), channel_id=1, source_target_pairs={{8,16},{12,20},{9,17},{13,21},{10,18},{14,22},{11,19},{15,23}} | collective-permute-start | bytes 393224 | tf_op jit(solution)/shard_map/ppermute | solution.py:298
  19.5 1.3 %collective-permute-start.13 = (f32[136,256]{1,0:T(8,128)S(1)}, f32[136,256]{1,0:T(8,128)S(1)}, u32[]{:S(2)}, u32[]{:S(2)}) collective-permute-start(f32[136,256]{1,0:T(8,128)S(1)} %shard_map.65._), channel_id=1, source_target_pairs={{16,24},{20,28},{17,25},{21,29},{18,26},{22,30},{19,27},{23,31}} | collective-permute-start | bytes 417800 | tf_op jit(solution)/shard_map/ppermute | solution.py:298
  20.8 1.3 %collective-permute-start.14 = (f32[128,256]{1,0:T(8,128)S(1)}, f32[128,256]{1,0:T(8,128)S(1)}, u32[]{:S(2)}, u32[]{:S(2)}) collective-permute-start(f32[128,256]{1,0:T(8,128)S(1)} %shard_map.66._), channel_id=1, source_target_pairs={{8,16},{12,20},{9,17},{13,21},{10,18},{14,22},{11,19},{15,23}} | collective-permute-start | bytes 393224 | tf_op jit(solution)/shard_map/ppermute | solution.py:298
  22.3 1.3 %collective-permute-start.15 = (f32[136,256]{1,0:T(8,128)S(1)}, f32[136,256]{1,0:T(8,128)S(1)}, u32[]{:S(2)}, u32[]{:S(2)}) collective-permute-start(f32[136,256]{1,0:T(8,128)S(1)} %shard_map.67._), channel_id=1, source_target_pairs={{16,24},{20,28},{17,25},{21,29},{18,26},{22,30},{19,27},{23,31}} | collective-permute-start | bytes 417800 | tf_op jit(solution)/shard_map/ppermute | solution.py:298
  23.6 0.9 %collective-permute-start.18 = (f32[136,256]{1,0:T(8,128)S(1)}, f32[136,256]{1,0:T(8,128)S(1)}, u32[]{:S(2)}, u32[]{:S(2)}) collective-permute-start(f32[136,256]{1,0:T(8,128)S(1)} %get-tuple-element.68._), channel_id=1, source_target_pairs={{0,4},{4,0},{8,12},{12,8},{16,20},{20,16},{24,28},{28,24},{1,5},{5... | collective-permute-start | bytes 417800 | tf_op jit(solution)/shard_map/ppermute | solution.py:314
  24.6 0.8 %collective-permute-done.12.refs_0_.refs_1_ = f32[128,256]{1,0:T(8,128)S(1)} collective-permute-done((f32[128,256]{1,0:T(8,128)S(1)}, f32[128,256]{1,0:T(8,128)S(1)}, u32[]{:S(2)}, u32[]{:S(2)}) %collective-permute-start.12) | collective-permute-done | bytes 131104 | tf_op jit(solution)/shard_map/ppermute | solution.py:298
  25.4 1.3 %collective-permute-start.16 = (f32[128,256]{1,0:T(8,128)S(1)}, f32[128,256]{1,0:T(8,128)S(1)}, u32[]{:S(2)}, u32[]{:S(2)}) collective-permute-start(f32[128,256]{1,0:T(8,128)S(1)} %shard_map.69._), channel_id=1, source_target_pairs={{16,24},{20,28},{17,25},{21,29},{18,26},{22,30},{19,27},{23,31}} | collective-permute-start | bytes 393224 | tf_op jit(solution)/shard_map/ppermute | solution.py:298
  27.2 1.1 %collective-permute-done.14.refs_0_.refs_1_ = f32[128,256]{1,0:T(8,128)S(1)} collective-permute-done((f32[128,256]{1,0:T(8,128)S(1)}, f32[128,256]{1,0:T(8,128)S(1)}, u32[]{:S(2)}, u32[]{:S(2)}) %collective-permute-start.14) | collective-permute-done | bytes 131104 | tf_op jit(solution)/shard_map/ppermute | solution.py:298
  28.3 1.4 %collective-permute-start.17 = (f32[128,256]{1,0:T(8,128)S(1)}, f32[128,256]{1,0:T(8,128)S(1)}, u32[]{:S(2)}, u32[]{:S(2)}) collective-permute-start(f32[128,256]{1,0:T(8,128)S(1)} %shard_map.71._), channel_id=1, source_target_pairs={{16,24},{20,28},{17,25},{21,29},{18,26},{22,30},{19,27},{23,31}} | collective-permute-start | bytes 393224 | tf_op jit(solution)/shard_map/ppermute | solution.py:298
  30.2 0.7 %shard_map.73 = (f32[256,128]{1,0:T(8,128)S(1)}, f32[256,128]{1,0:T(8,128)S(1)}, bf16[256,256]{1,0:T(8,128)(2,1)S(1)}, f32[256,128]{1,0:T(8,128)S(1)}, f32[256,1...) custom-call(s32[1]{0:T(128)} %bitcast.places_ref._, f32[136,256]{1,0:T(8,128)S(1)} %get-tuple-element.70._, ...), custom_call_target="tpu_custom_call" | custom-call | flops 167772160 | bytes 2502660 | tf_op jit(solution)/shard_map/pallas_call | solution.py:225
  31.0 1.2 %collective-permute-start.21 = (f32[128,256]{1,0:T(8,128)S(1)}, f32[128,256]{1,0:T(8,128)S(1)}, u32[]{:S(2)}, u32[]{:S(2)}) collective-permute-start(f32[128,256]{1,0:T(8,128)S(1)} %get-tuple-element.72._), channel_id=1, source_target_pairs={{0,4},{4,0},{8,12},{12,8},{16,20},{20,16},{24,28},{28,24},{1,5},{5... | collective-permute-start | bytes 393224 | tf_op jit(solution)/shard_map/ppermute | solution.py:314
  32.3 1.2 %collective-permute-start.22 = (f32[128,256]{1,0:T(8,128)S(1)}, f32[128,256]{1,0:T(8,128)S(1)}, u32[]{:S(2)}, u32[]{:S(2)}) collective-permute-start(f32[128,256]{1,0:T(8,128)S(1)} %get-tuple-element.73._), channel_id=1, source_target_pairs={{0,4},{4,0},{8,12},{12,8},{16,20},{20,16},{24,28},{28,24},{1,5},{5... | collective-permute-start | bytes 393224 | tf_op jit(solution)/shard_map/ppermute | solution.py:314
  33.5 0.7 %shard_map.76 = (f32[256,128]{1,0:T(8,128)S(1)}, f32[256,128]{1,0:T(8,128)S(1)}, bf16[256,256]{1,0:T(8,128)(2,1)S(1)}, f32[256,128]{1,0:T(8,128)S(1)}, f32[256,1...) custom-call(s32[1]{0:T(128)} %bitcast.places_ref._, f32[128,256]{1,0:T(8,128)S(1)} %get-tuple-element.73._, ...), custom_call_target="tpu_custom_call" | custom-call | flops 167772160 | bytes 2494468 | tf_op jit(solution)/shard_map/pallas_call | solution.py:225
  34.6 0.7 %shard_map.78 = (f32[256,128]{1,0:T(8,128)S(1)}, f32[256,128]{1,0:T(8,128)S(1)}, bf16[256,256]{1,0:T(8,128)(2,1)S(1)}, f32[256,128]{1,0:T(8,128)S(1)}, f32[256,1...) custom-call(s32[1]{0:T(128)} %bitcast.places_ref._, f32[256,128]{1,0:T(8,128)S(1)} %get-tuple-element.85._.refs_15_, ...), custom_call_target="tpu_custom_call" | custom-call | flops 167772160 | bytes 2494468 | tf_op jit(solution)/shard_map/pallas_call | solution.py:225
  35.3 0.7 %shard_map.79 = (f32[256,128]{1,0:T(8,128)S(1)}, f32[256,128]{1,0:T(8,128)S(1)}, bf16[256,256]{1,0:T(8,128)(2,1)S(1)}, f32[256,128]{1,0:T(8,128)S(1)}, f32[256,1...) custom-call(s32[1]{0:T(128)} %bitcast.places_ref._, f32[256,128]{1,0:T(8,128)S(1)} %get-tuple-element.86._.refs_4_, ...), custom_call_target="tpu_custom_call" | custom-call | flops 167772160 | bytes 2494468 | tf_op jit(solution)/shard_map/pallas_call | solution.py:225
  37.4 2.3 %collective-permute-done.22.refs_5_ = f32[128,256]{1,0:T(8,128)S(1)} collective-permute-done((f32[128,256]{1,0:T(8,128)S(1)}, f32[128,256]{1,0:T(8,128)S(1)}, u32[]{:S(2)}, u32[]{:S(2)}) %collective-permute-start.22) | collective-permute-done | bytes 131104 | tf_op jit(solution)/shard_map/ppermute | solution.py:314
  40.0 4.7 %collective-permute-start.25 = (f32[8,256]{1,0:T(8,128)S(1)}, f32[8,256]{1,0:T(8,128)S(1)}, u32[]{:S(2)}, u32[]{:S(2)}) collective-permute-start(f32[8,256]{1,0:T(8,128)S(1)} %get-tuple-element.114.refs_8_), channel_id=1, source_target_pairs={{0,3},{1,2},{2,1},{3,0},{4,7},{5,6},{6,5},{7,4},{8,11},{9,10},{10,... | collective-permute-start | bytes 24584 | tf_op jit(solution)/shard_map/ppermute | solution.py:382
  45.1 1.1 %collective-permute-done.25.refs_11_ = f32[8,256]{1,0:T(8,128)S(1)} collective-permute-done((f32[8,256]{1,0:T(8,128)S(1)}, f32[8,256]{1,0:T(8,128)S(1)}, u32[]{:S(2)}, u32[]{:S(2)}) %collective-permute-start.25) | collective-permute-done | bytes 8224 | tf_op jit(solution)/shard_map/ppermute | solution.py:382
  46.2 0.9 %collective-permute-done.24.refs_10_ = f32[8,256]{1,0:T(8,128)S(1)} collective-permute-done((f32[8,256]{1,0:T(8,128)S(1)}, f32[8,256]{1,0:T(8,128)S(1)}, u32[]{:S(2)}, u32[]{:S(2)}) %collective-permute-start.24) | collective-permute-done | bytes 8224 | tf_op jit(solution)/shard_map/ppermute | solution.py:382
  47.2 1.0 %shard_map.83 = bf16[256,1024]{1,0:T(8,128)(2,1)} custom-call(s32[1]{0:T(128)} %bitcast.places_ref._, f32[256,128]{1,0:T(8,128)S(1)} %get-tuple-element.83.refs_0_, f32[256,128]{1,0:T(8,128)S(1)} %get-tuple-element.84.refs_1_, f32[256,128]{1,0:T(8,128)S(1)} %get-tuple-element.97.refs_2_, f32[256,128]{1,0:T(8,128)S(1)} %get-tuple-element.98.refs_3_, ...), custom_call_target="tpu_custom_call" | custom-call | flops 786432 | bytes 1605636 | tf_op jit(solution)/shard_map/pallas_call | solution.py:225
  (63 shorter events, 6.3 us)
Async XLA Ops:
  0.0 7.0 %copy-start = (bf16[256,1024]{1,0:T(8,128)(2,1)S(1)}, bf16[256,1024]{1,0:T(8,128)(2,1)}, u32[]{:S(2)}) copy-start(bf16[256,1024]{1,0:T(8,128)(2,1)} %k_ref.7) | copy-start | bytes 1572868
  0.0 7.0 %copy-start.1 = (bf16[256,1024]{1,0:T(8,128)(2,1)S(1)}, bf16[256,1024]{1,0:T(8,128)(2,1)}, u32[]{:S(2)}) copy-start(bf16[256,1024]{1,0:T(8,128)(2,1)} %v_ref.7) | copy-start | bytes 1572868
  2.8 5.1 %collective-permute-start = (f32[136,256]{1,0:T(8,128)}, f32[136,256]{1,0:T(8,128)S(1)}, u32[]{:S(2)}, u32[]{:S(2)}) collective-permute-start(f32[136,256]{1,0:T(8,128)} %get-tuple-element.61), channel_id=1, source_target_pairs={{0,4},{4,0},{8,12},{12,8},{16,20},{20,16},{24,28},{28,24},{1,5},{5... | collective-permute-start | bytes 417800 | tf_op jit(solution)/shard_map/ppermute | solution.py:274
  4.0 3.0 %copy-start.4 = (f32[1024]{0:T(1024)S(1)}, f32[1024]{0:T(1024)}, u32[]{:S(2)}) copy-start(f32[1024]{0:T(1024)} %param.9) | copy-start | bytes 12292
  4.0 3.0 %copy-start.3 = (bf16[8,256]{1,0:T(8,128)(2,1)S(1)}, bf16[8,256]{1,0:T(8,128)(2,1)}, u32[]{:S(2)}) copy-start(bf16[8,256]{1,0:T(8,128)(2,1)} %seeds_ref.7) | copy-start | bytes 12292
  4.0 4.6 %collective-permute-start.1 = (f32[136,256]{1,0:T(8,128)}, f32[136,256]{1,0:T(8,128)S(1)}, u32[]{:S(2)}, u32[]{:S(2)}) collective-permute-start(f32[136,256]{1,0:T(8,128)} %get-tuple-element.62.refs_1_.refs_3_), channel_id=1, source_target_pairs={{0,8},{4,12},{1,9},{5,13},{2,10},{6,14},{3,11},{7,15}} | collective-permute-start | bytes 417800 | tf_op jit(solution)/shard_map/ppermute | solution.py:298
  4.8 5.8 %collective-permute-start.2 = (f32[128,256]{1,0:T(8,128)}, f32[128,256]{1,0:T(8,128)S(1)}, u32[]{:S(2)}, u32[]{:S(2)}) collective-permute-start(f32[128,256]{1,0:T(8,128)} %get-tuple-element.64), channel_id=1, source_target_pairs={{0,4},{4,0},{8,12},{12,8},{16,20},{20,16},{24,28},{28,24},{1,5},{5... | collective-permute-start | bytes 393224 | tf_op jit(solution)/shard_map/ppermute | solution.py:274
  5.2 8.3 %collective-permute-start.4 = (f32[128,256]{1,0:T(8,128)}, f32[128,256]{1,0:T(8,128)S(1)}, u32[]{:S(2)}, u32[]{:S(2)}) collective-permute-start(f32[128,256]{1,0:T(8,128)} %get-tuple-element.67), channel_id=1, source_target_pairs={{0,4},{4,0},{8,12},{12,8},{16,20},{20,16},{24,28},{28,24},{1,5},{5... | collective-permute-start | bytes 393224 | tf_op jit(solution)/shard_map/ppermute | solution.py:274
  6.4 5.1 %collective-permute-start.3 = (f32[136,256]{1,0:T(8,128)}, f32[136,256]{1,0:T(8,128)S(1)}, u32[]{:S(2)}, u32[]{:S(2)}) collective-permute-start(f32[136,256]{1,0:T(8,128)} %get-tuple-element.65.refs_1_.refs_3_), channel_id=1, source_target_pairs={{0,8},{4,12},{1,9},{5,13},{2,10},{6,14},{3,11},{7,15}} | collective-permute-start | bytes 417800 | tf_op jit(solution)/shard_map/ppermute | solution.py:298
  7.8 0.9 %copy-start.6 = (f32[136,256]{1,0:T(8,128)S(1)}, f32[136,256]{1,0:T(8,128)}, u32[]{:S(2)}) copy-start(f32[136,256]{1,0:T(8,128)} %get-tuple-element.62.refs_1_.refs_3_) | copy-start | bytes 417796
  7.9 6.3 %collective-permute-start.5 = (f32[136,256]{1,0:T(8,128)S(1)}, f32[136,256]{1,0:T(8,128)S(1)}, u32[]{:S(2)}, u32[]{:S(2)}) collective-permute-start(f32[136,256]{1,0:T(8,128)S(1)} %shard_map.57._), channel_id=1, source_target_pairs={{0,8},{4,12},{1,9},{5,13},{2,10},{6,14},{3,11},{7,15}} | collective-permute-start | bytes 417800 | tf_op jit(solution)/shard_map/ppermute | solution.py:298
  8.8 6.7 %collective-permute-start.6 = (f32[136,256]{1,0:T(8,128)S(1)}, f32[136,256]{1,0:T(8,128)S(1)}, u32[]{:S(2)}, u32[]{:S(2)}) collective-permute-start(f32[136,256]{1,0:T(8,128)S(1)} %shard_map.58._), channel_id=1, source_target_pairs={{8,16},{12,20},{9,17},{13,21},{10,18},{14,22},{11,19},{15,23}} | collective-permute-start | bytes 417800 | tf_op jit(solution)/shard_map/ppermute | solution.py:298
  10.6 7.5 %collective-permute-start.7 = (f32[128,256]{1,0:T(8,128)S(1)}, f32[128,256]{1,0:T(8,128)S(1)}, u32[]{:S(2)}, u32[]{:S(2)}) collective-permute-start(f32[128,256]{1,0:T(8,128)S(1)} %shard_map.59._), channel_id=1, source_target_pairs={{0,8},{4,12},{1,9},{5,13},{2,10},{6,14},{3,11},{7,15}} | collective-permute-start | bytes 393224 | tf_op jit(solution)/shard_map/ppermute | solution.py:298
  11.5 7.9 %collective-permute-start.8 = (f32[136,256]{1,0:T(8,128)S(1)}, f32[136,256]{1,0:T(8,128)S(1)}, u32[]{:S(2)}, u32[]{:S(2)}) collective-permute-start(f32[136,256]{1,0:T(8,128)S(1)} %shard_map.60._), channel_id=1, source_target_pairs={{8,16},{12,20},{9,17},{13,21},{10,18},{14,22},{11,19},{15,23}} | collective-permute-start | bytes 417800 | tf_op jit(solution)/shard_map/ppermute | solution.py:298
  13.4 7.3 %collective-permute-start.9 = (f32[128,256]{1,0:T(8,128)S(1)}, f32[128,256]{1,0:T(8,128)S(1)}, u32[]{:S(2)}, u32[]{:S(2)}) collective-permute-start(f32[128,256]{1,0:T(8,128)S(1)} %shard_map.61._), channel_id=1, source_target_pairs={{0,8},{4,12},{1,9},{5,13},{2,10},{6,14},{3,11},{7,15}} | collective-permute-start | bytes 393224 | tf_op jit(solution)/shard_map/ppermute | solution.py:298
  14.2 8.1 %collective-permute-start.10 = (f32[136,256]{1,0:T(8,128)S(1)}, f32[136,256]{1,0:T(8,128)S(1)}, u32[]{:S(2)}, u32[]{:S(2)}) collective-permute-start(f32[136,256]{1,0:T(8,128)S(1)} %shard_map.62._), channel_id=1, source_target_pairs={{8,16},{12,20},{9,17},{13,21},{10,18},{14,22},{11,19},{15,23}} | collective-permute-start | bytes 417800 | tf_op jit(solution)/shard_map/ppermute | solution.py:298
  15.5 8.1 %collective-permute-start.11 = (f32[136,256]{1,0:T(8,128)S(1)}, f32[136,256]{1,0:T(8,128)S(1)}, u32[]{:S(2)}, u32[]{:S(2)}) collective-permute-start(f32[136,256]{1,0:T(8,128)S(1)} %shard_map.63._), channel_id=1, source_target_pairs={{16,24},{20,28},{17,25},{21,29},{18,26},{22,30},{19,27},{23,31}} | collective-permute-start | bytes 417800 | tf_op jit(solution)/shard_map/ppermute | solution.py:298
  18.1 7.2 %collective-permute-start.12 = (f32[128,256]{1,0:T(8,128)S(1)}, f32[128,256]{1,0:T(8,128)S(1)}, u32[]{:S(2)}, u32[]{:S(2)}) collective-permute-start(f32[128,256]{1,0:T(8,128)S(1)} %shard_map.64._), channel_id=1, source_target_pairs={{8,16},{12,20},{9,17},{13,21},{10,18},{14,22},{11,19},{15,23}} | collective-permute-start | bytes 393224 | tf_op jit(solution)/shard_map/ppermute | solution.py:298
  19.5 7.2 %collective-permute-start.13 = (f32[136,256]{1,0:T(8,128)S(1)}, f32[136,256]{1,0:T(8,128)S(1)}, u32[]{:S(2)}, u32[]{:S(2)}) collective-permute-start(f32[136,256]{1,0:T(8,128)S(1)} %shard_map.65._), channel_id=1, source_target_pairs={{16,24},{20,28},{17,25},{21,29},{18,26},{22,30},{19,27},{23,31}} | collective-permute-start | bytes 417800 | tf_op jit(solution)/shard_map/ppermute | solution.py:298
  20.8 7.5 %collective-permute-start.14 = (f32[128,256]{1,0:T(8,128)S(1)}, f32[128,256]{1,0:T(8,128)S(1)}, u32[]{:S(2)}, u32[]{:S(2)}) collective-permute-start(f32[128,256]{1,0:T(8,128)S(1)} %shard_map.66._), channel_id=1, source_target_pairs={{8,16},{12,20},{9,17},{13,21},{10,18},{14,22},{11,19},{15,23}} | collective-permute-start | bytes 393224 | tf_op jit(solution)/shard_map/ppermute | solution.py:298
  22.3 7.5 %collective-permute-start.15 = (f32[136,256]{1,0:T(8,128)S(1)}, f32[136,256]{1,0:T(8,128)S(1)}, u32[]{:S(2)}, u32[]{:S(2)}) collective-permute-start(f32[136,256]{1,0:T(8,128)S(1)} %shard_map.67._), channel_id=1, source_target_pairs={{16,24},{20,28},{17,25},{21,29},{18,26},{22,30},{19,27},{23,31}} | collective-permute-start | bytes 417800 | tf_op jit(solution)/shard_map/ppermute | solution.py:298
  23.6 10.6 %collective-permute-start.18 = (f32[136,256]{1,0:T(8,128)S(1)}, f32[136,256]{1,0:T(8,128)S(1)}, u32[]{:S(2)}, u32[]{:S(2)}) collective-permute-start(f32[136,256]{1,0:T(8,128)S(1)} %get-tuple-element.68._), channel_id=1, source_target_pairs={{0,4},{4,0},{8,12},{12,8},{16,20},{20,16},{24,28},{28,24},{1,5},{5... | collective-permute-start | bytes 417800 | tf_op jit(solution)/shard_map/ppermute | solution.py:314
  25.4 5.6 %collective-permute-start.16 = (f32[128,256]{1,0:T(8,128)S(1)}, f32[128,256]{1,0:T(8,128)S(1)}, u32[]{:S(2)}, u32[]{:S(2)}) collective-permute-start(f32[128,256]{1,0:T(8,128)S(1)} %shard_map.69._), channel_id=1, source_target_pairs={{16,24},{20,28},{17,25},{21,29},{18,26},{22,30},{19,27},{23,31}} | collective-permute-start | bytes 393224 | tf_op jit(solution)/shard_map/ppermute | solution.py:298
  26.7 7.5 %collective-permute-start.19 = (f32[136,256]{1,0:T(8,128)S(1)}, f32[136,256]{1,0:T(8,128)S(1)}, u32[]{:S(2)}, u32[]{:S(2)}) collective-permute-start(f32[136,256]{1,0:T(8,128)S(1)} %get-tuple-element.69._), channel_id=1, source_target_pairs={{0,4},{4,0},{8,12},{12,8},{16,20},{20,16},{24,28},{28,24},{1,5},{5... | collective-permute-start | bytes 417800 | tf_op jit(solution)/shard_map/ppermute | solution.py:314
  28.3 1.9 %copy-start.2 = (bf16[256,1024]{1,0:T(8,128)(2,1)S(1)}, bf16[256,1024]{1,0:T(8,128)(2,1)}, u32[]{:S(2)}) copy-start(bf16[256,1024]{1,0:T(8,128)(2,1)} %q_ref.7) | copy-start | bytes 1572868
  28.3 3.9 %collective-permute-start.17 = (f32[128,256]{1,0:T(8,128)S(1)}, f32[128,256]{1,0:T(8,128)S(1)}, u32[]{:S(2)}, u32[]{:S(2)}) collective-permute-start(f32[128,256]{1,0:T(8,128)S(1)} %shard_map.71._), channel_id=1, source_target_pairs={{16,24},{20,28},{17,25},{21,29},{18,26},{22,30},{19,27},{23,31}} | collective-permute-start | bytes 393224 | tf_op jit(solution)/shard_map/ppermute | solution.py:298
  29.8 7.1 %collective-permute-start.20 = (f32[136,256]{1,0:T(8,128)S(1)}, f32[136,256]{1,0:T(8,128)S(1)}, u32[]{:S(2)}, u32[]{:S(2)}) collective-permute-start(f32[136,256]{1,0:T(8,128)S(1)} %get-tuple-element.70._), channel_id=1, source_target_pairs={{0,4},{4,0},{8,12},{12,8},{16,20},{20,16},{24,28},{28,24},{1,5},{5... | collective-permute-start | bytes 417800 | tf_op jit(solution)/shard_map/ppermute | solution.py:314
  31.0 6.0 %collective-permute-start.21 = (f32[128,256]{1,0:T(8,128)S(1)}, f32[128,256]{1,0:T(8,128)S(1)}, u32[]{:S(2)}, u32[]{:S(2)}) collective-permute-start(f32[128,256]{1,0:T(8,128)S(1)} %get-tuple-element.72._), channel_id=1, source_target_pairs={{0,4},{4,0},{8,12},{12,8},{16,20},{20,16},{24,28},{28,24},{1,5},{5... | collective-permute-start | bytes 393224 | tf_op jit(solution)/shard_map/ppermute | solution.py:314
  32.3 7.3 %collective-permute-start.22 = (f32[128,256]{1,0:T(8,128)S(1)}, f32[128,256]{1,0:T(8,128)S(1)}, u32[]{:S(2)}, u32[]{:S(2)}) collective-permute-start(f32[128,256]{1,0:T(8,128)S(1)} %get-tuple-element.73._), channel_id=1, source_target_pairs={{0,4},{4,0},{8,12},{12,8},{16,20},{20,16},{24,28},{28,24},{1,5},{5... | collective-permute-start | bytes 393224 | tf_op jit(solution)/shard_map/ppermute | solution.py:314
  40.0 6.2 %collective-permute-start.25 = (f32[8,256]{1,0:T(8,128)S(1)}, f32[8,256]{1,0:T(8,128)S(1)}, u32[]{:S(2)}, u32[]{:S(2)}) collective-permute-start(f32[8,256]{1,0:T(8,128)S(1)} %get-tuple-element.114.refs_8_), channel_id=1, source_target_pairs={{0,3},{1,2},{2,1},{3,0},{4,7},{5,6},{6,5},{7,4},{8,11},{9,10},{10,... | collective-permute-start | bytes 24584 | tf_op jit(solution)/shard_map/ppermute | solution.py:382
  44.7 2.5 %collective-permute-start.24 = (f32[8,256]{1,0:T(8,128)S(1)}, f32[8,256]{1,0:T(8,128)S(1)}, u32[]{:S(2)}, u32[]{:S(2)}) collective-permute-start(f32[8,256]{1,0:T(8,128)S(1)} %get-tuple-element.114.refs_8_), channel_id=1, source_target_pairs={{0,2},{1,3},{2,0},{3,1},{4,6},{5,7},{6,4},{7,5},{8,10},{9,11},{10,... | collective-permute-start | bytes 24584 | tf_op jit(solution)/shard_map/ppermute | solution.py:382
  44.9 2.3 %collective-permute-start.23 = (f32[8,256]{1,0:T(8,128)S(1)}, f32[8,256]{1,0:T(8,128)S(1)}, u32[]{:S(2)}, u32[]{:S(2)}) collective-permute-start(f32[8,256]{1,0:T(8,128)S(1)} %get-tuple-element.114.refs_8_), channel_id=1, source_target_pairs={{0,1},{1,0},{2,3},{3,2},{4,5},{5,4},{6,7},{7,6},{8,9},{9,8},{10,11... | collective-permute-start | bytes 24584 | tf_op jit(solution)/shard_map/ppermute | solution.py:382
  (1 other events, 0.9 us)

commit v7 on v6

--- a/solution.py
+++ b/solution.py
@@ -14,7 +14,7 @@
 PARTS = 3
 GLUE_COST = 10**9
 GAP = 2.1
-ORDER = [(1, 0), (1, 1), (1, 2), (2, 0), (1, 3), (2, 1), (1, 4), (2, 2), (3, 0), (2, 3), (3, 1), (2, 4), (3, 2), ('X', 0), (3, 3), ('X', 1), (3, 4), ('X', 2), ('L', 0), ('X', 3), ('X', 4), ('L', 1), ('J', [(2, 0), (2, 1)]), ('L', 2), ('L', 3), ('J', [(0, 0), (0, 1), (0, 2)]), ('J', [(1, 0), (1, 1)]), ('J', [(1, 2)])]
+ORDER = [(1, 0), (1, 1), ('L', 0), (1, 2), (2, 0), (1, 3), (2, 1), (1, 4), (2, 2), (3, 0), (2, 3), (3, 1), (2, 4), (3, 2), ('X', 0), (3, 3), ('X', 1), (3, 4), ('X', 2), ('X', 3), ('X', 4), ('L', 1), ('J', [(2, 0), (2, 1)]), ('L', 2), ('L', 3), ('J', [(0, 0), (0, 1), (0, 2)]), ('J', [(1, 0), (1, 1)]), ('J', [(1, 2)])]
 
 
 NT = (((1,), (1,)), ((), ()))
@@ -180,27 +180,36 @@
 def join_kernel(half, work, final, places_ref, _, gain_ref, *refs):
     count = len(work)
     heads_refs, squares_ref = refs[-count - 1 : -1], refs[-1]
-    squares = jnp.zeros(heads_refs[0].shape, jnp.float32)
-    for (group, i, cuts, n, copies), out_ref in zip(work, heads_refs):
-        num_ref, den_ref, fq_ref = refs[:3]
+    wides, locals_ = [], []
+    for _, _, cuts, n, copies in work:
+        locals_.append(refs[:3])
         state, total = 0.0, 0.0
+        refs = refs[3:]
         for _ in range(copies):
-            parts = refs[3 : 3 + len(cuts)]
-            refs = refs[:3] + refs[3 + len(cuts) :]
+            parts, refs = refs[: len(cuts)], refs[len(cuts) :]
             rows = [parts[m][at, :] for m, at, _ in overlaps(cuts, n)]
             state = state + (rows[0] if len(rows) == 1 else jnp.concatenate(rows, axis=0))
             total = total + parts[0][cuts[0][1] + n : cuts[0][1] + n + 1, :]
-        refs = refs[3:]
-        wide = jnp.concatenate([state, jnp.broadcast_to(total, state.shape)], axis=0)
-        upper = wide.astype(jnp.bfloat16)
-        lower = (wide - upper.astype(jnp.float32)).astype(jnp.bfloat16)
-        fq = fq_ref[...]
-        both = lax.dot_general(fq, upper, NT, preferred_element_type=jnp.float32)
-        both = both + lax.dot_general(fq, lower, NT, preferred_element_type=jnp.float32)
-        head = (num_ref[...] + both[:, :WIDTH]) / (den_ref[...] + both[:, WIDTH:])
+        wides.append(jnp.concatenate([state, jnp.broadcast_to(total, state.shape)], axis=0))
+    uppers = [wide.astype(jnp.bfloat16) for wide in wides]
+    lowers = [
+        (wide - upper.astype(jnp.float32)).astype(jnp.bfloat16)
+        for wide, upper in zip(wides, uppers)
+    ]
+    fqs = [local[2][...] for local in locals_]
+    boths = [
+        lax.dot_general(fq, upper, NT, preferred_element_type=jnp.float32)
+        + lax.dot_general(fq, lower, NT, preferred_element_type=jnp.float32)
+        for fq, upper, lower in zip(fqs, uppers, lowers)
+    ]
+    heads = [
+        (num_ref[...] + both[:, :WIDTH]) / (den_ref[...] + both[:, WIDTH:])
+        for (num_ref, den_ref, _), both in zip(locals_, boths)
+    ]
+    squares = functools.reduce(lambda a, b: a + b, [head * head for head in heads])
+    for (group, i, *_), out_ref, head in zip(work, heads_refs, heads):
         place = 2 * half + i if group == 2 else first_of(group, half, places_ref) + i
         out_ref[...] = head * gain_ref[:, columns(place)]
-        squares = squares + head * head
     if len(refs) > count + 1:
         squares = squares + refs[0][...]
     if final:

time: 48.5 us -> 48.4 us (level)
  waiting for transfers between devices: 7.92 us -> 6.3 us
  starting transfers between devices: 30.2 us -> 31.4 us
    ppermute x5, starting transfers between devices: 4.16 us -> 5.51 us  [hand(): passed[i] = lax.ppermute(last, 'seq', swap)]
    ppermute x3, waiting for transfers between devices: 1.14 us -> 0.1 us  [per_device(): incoming = [lax.ppermute(part, 'seq', swap) for part in [*theirs, *cross]]]
  transfers between devices with their start and end apart: 26 -> 26, of which waited for: 9 -> 10; matrix products, arithmetic and copies ran while one was open for 0% -> 0% of each run, Pallas kernels for 11% -> 11%
where the time goes in v7:
time: 48.4 us; the launch traced here: 48 us
  starting transfers between devices  31.4 us (65%)
  Pallas kernels  9.5 us (20%)
  waiting for transfers between devices  6.3 us (13%)
    ppermute x15, starting transfers between devices, hop(): arrivals[stage, i] = lax.ppermute(sent, 'seq', pairs)  17.8 us
    pallas_call x29, Pallas kernels, call(): pl.pallas_call(kernel, out_shape=outs, in_specs=[SMEM, *specs] + [place]...  9.5 us
    ppermute x5, starting transfers between devices, hand(): passed[i] = lax.ppermute(last, 'seq', swap)  5.51 us
    ppermute x3, starting transfers between devices, per_device(): lax.ppermute(squares, 'tp', [(i, i ^ k if across == 4 else (i + k) % acro...  5.2 us
    ppermute x3, starting transfers between devices, per_device(): incoming = [lax.ppermute(part, 'seq', swap) for part in [*theirs, *cross]]  2.81 us
    ppermute x5, waiting for transfers between devices, hand(): passed[i] = lax.ppermute(last, 'seq', swap)  2.46 us
    ppermute x3, waiting for transfers between devices, per_device(): lax.ppermute(squares, 'tp', [(i, i ^ k if across == 4 else (i + k) % acro...  2.03 us
    ppermute x15, waiting for transfers between devices, hop(): arrivals[stage, i] = lax.ppermute(sent, 'seq', pairs)  1.71 us
  transfers between devices with their start and end apart: 26, of which 10 were waited for; matrix products, arithmetic and copies ran while one was open for 0% of the time, Pallas kernels for 11%

profile of v7, /device:TPU:17, one launch (start us, length us, event | category | flops | bytes accessed | tf_op | source)
XLA Modules:
  0.0 48.0 jit_solution(13905736727712865851)
XLA Ops:
  0.0 2.7 %shard_map.57 = (f32[136,256]{1,0:T(8,128)}, f32[136,256]{1,0:T(8,128)}, f32[136,256]{1,0:T(8,128)}, f32[128,256]{1,0:T(8,128)}, f32[128,256]{1,0:T(8,128)}) custom-call(s32[1]{0:T(128)} %bitcast.places_ref._, bf16[8,256]{1,0:T(8,128)(2,1)} %seeds_ref.7, bf16[256,1024]{1,0:T(8,128)(2,1)} %k_ref.7, bf16[256,1024]{1,0:T(8,128)(2,1)} %v_ref.7), custom_call_target="tpu_custom_call" | custom-call | flops 167772160 | bytes 1732612 | tf_op jit(solution)/shard_map/pallas_call | solution.py:234
  2.8 1.3 %collective-permute-start = (f32[136,256]{1,0:T(8,128)}, f32[136,256]{1,0:T(8,128)S(1)}, u32[]{:S(2)}, u32[]{:S(2)}) collective-permute-start(f32[136,256]{1,0:T(8,128)} %get-tuple-element.62), channel_id=1, source_target_pairs={{0,4},{4,0},{8,12},{12,8},{16,20},{20,16},{24,28},{28,24},{1,5},{5... | collective-permute-start | bytes 417800 | tf_op jit(solution)/shard_map/ppermute | solution.py:283
  4.0 0.8 %collective-permute-start.1 = (f32[136,256]{1,0:T(8,128)}, f32[136,256]{1,0:T(8,128)S(1)}, u32[]{:S(2)}, u32[]{:S(2)}) collective-permute-start(f32[136,256]{1,0:T(8,128)} %get-tuple-element.63.refs_1_.refs_3_), channel_id=1, source_target_pairs={{0,8},{4,12},{1,9},{5,13},{2,10},{6,14},{3,11},{7,15}} | collective-permute-start | bytes 417800 | tf_op jit(solution)/shard_map/ppermute | solution.py:307
  5.2 1.2 %collective-permute-start.4 = (f32[128,256]{1,0:T(8,128)}, f32[128,256]{1,0:T(8,128)S(1)}, u32[]{:S(2)}, u32[]{:S(2)}) collective-permute-start(f32[128,256]{1,0:T(8,128)} %get-tuple-element.68), channel_id=1, source_target_pairs={{0,4},{4,0},{8,12},{12,8},{16,20},{20,16},{24,28},{28,24},{1,5},{5... | collective-permute-start | bytes 393224 | tf_op jit(solution)/shard_map/ppermute | solution.py:283
  7.1 0.7 %shard_map.56 = (f32[136,256]{1,0:T(8,128)S(1)}, f32[128,256]{1,0:T(8,128)S(1)}, f32[128,256]{1,0:T(8,128)S(1)}, f32[1,1024]{1,0:T(1,128)S(1)}) custom-call(s32[1]{0:T(128)} %bitcast.places_ref._, bf16[8,256]{1,0:T(8,128)(2,1)S(1)} %copy-done.3, bf16[256,1024]{1,0:T(8,128)(2,1)S(1)} %copy-done, bf16[256,1024]{1,0:T(8,128)(2,1)S(1)} %copy-done.1, ...), custom_call_target="tpu_custom_call" | custom-call | flops 100663296 | bytes 1462276 | tf_op jit(solution)/shard_map/pallas_call | solution.py:234
  8.1 0.7 %shard_map.55 = (f32[256,128]{1,0:T(8,128)S(1)}, f32[256,128]{1,0:T(8,128)S(1)}, bf16[256,256]{1,0:T(8,128)(2,1)S(1)}, f32[256,128]{1,0:T(8,128)S(1)}, f32[256,1...) custom-call(s32[1]{0:T(128)} %bitcast.places_ref._, s32[1]{0:T(128)} %bitcast.places_ref._, bf16[8,256]{1,0:T(8,128)(2,1)S(1)} %copy-done.3, ...), custom_call_target="tpu_custom_call" | custom-call | flops 167772160 | bytes 2363400 | tf_op jit(solution)/shard_map/pallas_call | solution.py:234
  8.9 0.8 %collective-permute-start.5 = (f32[136,256]{1,0:T(8,128)S(1)}, f32[136,256]{1,0:T(8,128)S(1)}, u32[]{:S(2)}, u32[]{:S(2)}) collective-permute-start(f32[136,256]{1,0:T(8,128)S(1)} %shard_map.58._), channel_id=1, source_target_pairs={{0,8},{4,12},{1,9},{5,13},{2,10},{6,14},{3,11},{7,15}} | collective-permute-start | bytes 417800 | tf_op jit(solution)/shard_map/ppermute | solution.py:307
  9.8 1.3 %collective-permute-start.6 = (f32[136,256]{1,0:T(8,128)S(1)}, f32[136,256]{1,0:T(8,128)S(1)}, u32[]{:S(2)}, u32[]{:S(2)}) collective-permute-start(f32[136,256]{1,0:T(8,128)S(1)} %shard_map.59._), channel_id=1, source_target_pairs={{8,16},{12,20},{9,17},{13,21},{10,18},{14,22},{11,19},{15,23}} | collective-permute-start | bytes 417800 | tf_op jit(solution)/shard_map/ppermute | solution.py:307
  11.1 0.8 %collective-permute-start.7 = (f32[128,256]{1,0:T(8,128)S(1)}, f32[128,256]{1,0:T(8,128)S(1)}, u32[]{:S(2)}, u32[]{:S(2)}) collective-permute-start(f32[128,256]{1,0:T(8,128)S(1)} %shard_map.60._), channel_id=1, source_target_pairs={{0,8},{4,12},{1,9},{5,13},{2,10},{6,14},{3,11},{7,15}} | collective-permute-start | bytes 393224 | tf_op jit(solution)/shard_map/ppermute | solution.py:307
  12.0 1.3 %collective-permute-start.8 = (f32[136,256]{1,0:T(8,128)S(1)}, f32[136,256]{1,0:T(8,128)S(1)}, u32[]{:S(2)}, u32[]{:S(2)}) collective-permute-start(f32[136,256]{1,0:T(8,128)S(1)} %shard_map.61._), channel_id=1, source_target_pairs={{8,16},{12,20},{9,17},{13,21},{10,18},{14,22},{11,19},{15,23}} | collective-permute-start | bytes 417800 | tf_op jit(solution)/shard_map/ppermute | solution.py:307
  13.4 0.7 %collective-permute-start.9 = (f32[128,256]{1,0:T(8,128)S(1)}, f32[128,256]{1,0:T(8,128)S(1)}, u32[]{:S(2)}, u32[]{:S(2)}) collective-permute-start(f32[128,256]{1,0:T(8,128)S(1)} %shard_map.62._), channel_id=1, source_target_pairs={{0,8},{4,12},{1,9},{5,13},{2,10},{6,14},{3,11},{7,15}} | collective-permute-start | bytes 393224 | tf_op jit(solution)/shard_map/ppermute | solution.py:307
  14.2 1.3 %collective-permute-start.10 = (f32[136,256]{1,0:T(8,128)S(1)}, f32[136,256]{1,0:T(8,128)S(1)}, u32[]{:S(2)}, u32[]{:S(2)}) collective-permute-start(f32[136,256]{1,0:T(8,128)S(1)} %shard_map.63._), channel_id=1, source_target_pairs={{8,16},{12,20},{9,17},{13,21},{10,18},{14,22},{11,19},{15,23}} | collective-permute-start | bytes 417800 | tf_op jit(solution)/shard_map/ppermute | solution.py:307
  15.6 2.5 %collective-permute-start.11 = (f32[136,256]{1,0:T(8,128)S(1)}, f32[136,256]{1,0:T(8,128)S(1)}, u32[]{:S(2)}, u32[]{:S(2)}) collective-permute-start(f32[136,256]{1,0:T(8,128)S(1)} %shard_map.64._), channel_id=1, source_target_pairs={{16,24},{20,28},{17,25},{21,29},{18,26},{22,30},{19,27},{23,31}} | collective-permute-start | bytes 417800 | tf_op jit(solution)/shard_map/ppermute | solution.py:307
  18.1 1.3 %collective-permute-start.12 = (f32[128,256]{1,0:T(8,128)S(1)}, f32[128,256]{1,0:T(8,128)S(1)}, u32[]{:S(2)}, u32[]{:S(2)}) collective-permute-start(f32[128,256]{1,0:T(8,128)S(1)} %shard_map.65._), channel_id=1, source_target_pairs={{8,16},{12,20},{9,17},{13,21},{10,18},{14,22},{11,19},{15,23}} | collective-permute-start | bytes 393224 | tf_op jit(solution)/shard_map/ppermute | solution.py:307
  19.5 1.3 %collective-permute-start.13 = (f32[136,256]{1,0:T(8,128)S(1)}, f32[136,256]{1,0:T(8,128)S(1)}, u32[]{:S(2)}, u32[]{:S(2)}) collective-permute-start(f32[136,256]{1,0:T(8,128)S(1)} %shard_map.66._), channel_id=1, source_target_pairs={{16,24},{20,28},{17,25},{21,29},{18,26},{22,30},{19,27},{23,31}} | collective-permute-start | bytes 417800 | tf_op jit(solution)/shard_map/ppermute | solution.py:307
  20.8 1.3 %collective-permute-start.14 = (f32[128,256]{1,0:T(8,128)S(1)}, f32[128,256]{1,0:T(8,128)S(1)}, u32[]{:S(2)}, u32[]{:S(2)}) collective-permute-start(f32[128,256]{1,0:T(8,128)S(1)} %shard_map.67._), channel_id=1, source_target_pairs={{8,16},{12,20},{9,17},{13,21},{10,18},{14,22},{11,19},{15,23}} | collective-permute-start | bytes 393224 | tf_op jit(solution)/shard_map/ppermute | solution.py:307
  22.4 1.3 %collective-permute-start.15 = (f32[136,256]{1,0:T(8,128)S(1)}, f32[136,256]{1,0:T(8,128)S(1)}, u32[]{:S(2)}, u32[]{:S(2)}) collective-permute-start(f32[136,256]{1,0:T(8,128)S(1)} %shard_map.68._), channel_id=1, source_target_pairs={{16,24},{20,28},{17,25},{21,29},{18,26},{22,30},{19,27},{23,31}} | collective-permute-start | bytes 417800 | tf_op jit(solution)/shard_map/ppermute | solution.py:307
  23.8 1.1 %collective-permute-start.18 = (f32[136,256]{1,0:T(8,128)S(1)}, f32[136,256]{1,0:T(8,128)S(1)}, u32[]{:S(2)}, u32[]{:S(2)}) collective-permute-start(f32[136,256]{1,0:T(8,128)S(1)} %get-tuple-element.69._), channel_id=1, source_target_pairs={{0,4},{4,0},{8,12},{12,8},{16,20},{20,16},{24,28},{28,24},{1,5},{5... | collective-permute-start | bytes 417800 | tf_op jit(solution)/shard_map/ppermute | solution.py:323
  25.0 1.3 %collective-permute-start.16 = (f32[128,256]{1,0:T(8,128)S(1)}, f32[128,256]{1,0:T(8,128)S(1)}, u32[]{:S(2)}, u32[]{:S(2)}) collective-permute-start(f32[128,256]{1,0:T(8,128)S(1)} %shard_map.70._), channel_id=1, source_target_pairs={{16,24},{20,28},{17,25},{21,29},{18,26},{22,30},{19,27},{23,31}} | collective-permute-start | bytes 393224 | tf_op jit(solution)/shard_map/ppermute | solution.py:307
  26.4 1.2 %collective-permute-start.19 = (f32[136,256]{1,0:T(8,128)S(1)}, f32[136,256]{1,0:T(8,128)S(1)}, u32[]{:S(2)}, u32[]{:S(2)}) collective-permute-start(f32[136,256]{1,0:T(8,128)S(1)} %get-tuple-element.70._), channel_id=1, source_target_pairs={{0,4},{4,0},{8,12},{12,8},{16,20},{20,16},{24,28},{28,24},{1,5},{5... | collective-permute-start | bytes 417800 | tf_op jit(solution)/shard_map/ppermute | solution.py:323
  27.5 0.7 %collective-permute-done.14.refs_0_.refs_1_ = f32[128,256]{1,0:T(8,128)S(1)} collective-permute-done((f32[128,256]{1,0:T(8,128)S(1)}, f32[128,256]{1,0:T(8,128)S(1)}, u32[]{:S(2)}, u32[]{:S(2)}) %collective-permute-start.14) | collective-permute-done | bytes 131104 | tf_op jit(solution)/shard_map/ppermute | solution.py:307
  28.3 1.3 %collective-permute-start.17 = (f32[128,256]{1,0:T(8,128)S(1)}, f32[128,256]{1,0:T(8,128)S(1)}, u32[]{:S(2)}, u32[]{:S(2)}) collective-permute-start(f32[128,256]{1,0:T(8,128)S(1)} %shard_map.72._), channel_id=1, source_target_pairs={{16,24},{20,28},{17,25},{21,29},{18,26},{22,30},{19,27},{23,31}} | collective-permute-start | bytes 393224 | tf_op jit(solution)/shard_map/ppermute | solution.py:307
  29.9 1.4 %collective-permute-start.21 = (f32[128,256]{1,0:T(8,128)S(1)}, f32[128,256]{1,0:T(8,128)S(1)}, u32[]{:S(2)}, u32[]{:S(2)}) collective-permute-start(f32[128,256]{1,0:T(8,128)S(1)} %get-tuple-element.72._), channel_id=1, source_target_pairs={{0,4},{4,0},{8,12},{12,8},{16,20},{20,16},{24,28},{28,24},{1,5},{5... | collective-permute-start | bytes 393224 | tf_op jit(solution)/shard_map/ppermute | solution.py:323
  31.9 1.6 %collective-permute-start.22 = (f32[128,256]{1,0:T(8,128)S(1)}, f32[128,256]{1,0:T(8,128)S(1)}, u32[]{:S(2)}, u32[]{:S(2)}) collective-permute-start(f32[128,256]{1,0:T(8,128)S(1)} %get-tuple-element.73._), channel_id=1, source_target_pairs={{0,4},{4,0},{8,12},{12,8},{16,20},{20,16},{24,28},{28,24},{1,5},{5... | collective-permute-start | bytes 393224 | tf_op jit(solution)/shard_map/ppermute | solution.py:323
  33.5 0.7 %shard_map.76 = (f32[256,128]{1,0:T(8,128)S(1)}, f32[256,128]{1,0:T(8,128)S(1)}, bf16[256,256]{1,0:T(8,128)(2,1)S(1)}, f32[256,128]{1,0:T(8,128)S(1)}, f32[256,1...) custom-call(s32[1]{0:T(128)} %bitcast.places_ref._, f32[128,256]{1,0:T(8,128)S(1)} %get-tuple-element.73._, ...), custom_call_target="tpu_custom_call" | custom-call | flops 167772160 | bytes 2494468 | tf_op jit(solution)/shard_map/pallas_call | solution.py:234
  34.6 0.7 %shard_map.78 = (f32[256,128]{1,0:T(8,128)S(1)}, f32[256,128]{1,0:T(8,128)S(1)}, bf16[256,256]{1,0:T(8,128)(2,1)S(1)}, f32[256,128]{1,0:T(8,128)S(1)}, f32[256,1...) custom-call(s32[1]{0:T(128)} %bitcast.places_ref._, f32[256,128]{1,0:T(8,128)S(1)} %get-tuple-element.85._.refs_15_, ...), custom_call_target="tpu_custom_call" | custom-call | flops 167772160 | bytes 2494468 | tf_op jit(solution)/shard_map/pallas_call | solution.py:234
  35.4 0.7 %shard_map.79 = (f32[256,128]{1,0:T(8,128)S(1)}, f32[256,128]{1,0:T(8,128)S(1)}, bf16[256,256]{1,0:T(8,128)(2,1)S(1)}, f32[256,128]{1,0:T(8,128)S(1)}, f32[256,1...) custom-call(s32[1]{0:T(128)} %bitcast.places_ref._, f32[256,128]{1,0:T(8,128)S(1)} %get-tuple-element.86._.refs_4_, ...), custom_call_target="tpu_custom_call" | custom-call | flops 167772160 | bytes 2494468 | tf_op jit(solution)/shard_map/pallas_call | solution.py:234
  37.1 2.2 %collective-permute-done.22.refs_5_ = f32[128,256]{1,0:T(8,128)S(1)} collective-permute-done((f32[128,256]{1,0:T(8,128)S(1)}, f32[128,256]{1,0:T(8,128)S(1)}, u32[]{:S(2)}, u32[]{:S(2)}) %collective-permute-start.22) | collective-permute-done | bytes 131104 | tf_op jit(solution)/shard_map/ppermute | solution.py:323
  39.8 4.7 %collective-permute-start.25 = (f32[8,256]{1,0:T(8,128)S(1)}, f32[8,256]{1,0:T(8,128)S(1)}, u32[]{:S(2)}, u32[]{:S(2)}) collective-permute-start(f32[8,256]{1,0:T(8,128)S(1)} %get-tuple-element.114.refs_8_), channel_id=1, source_target_pairs={{0,3},{1,2},{2,1},{3,0},{4,7},{5,6},{6,5},{7,4},{8,11},{9,10},{10,... | collective-permute-start | bytes 24584 | tf_op jit(solution)/shard_map/ppermute | solution.py:391
  45.0 1.1 %collective-permute-done.25.refs_11_ = f32[8,256]{1,0:T(8,128)S(1)} collective-permute-done((f32[8,256]{1,0:T(8,128)S(1)}, f32[8,256]{1,0:T(8,128)S(1)}, u32[]{:S(2)}, u32[]{:S(2)}) %collective-permute-start.25) | collective-permute-done | bytes 8224 | tf_op jit(solution)/shard_map/ppermute | solution.py:391
  46.1 0.9 %collective-permute-done.24.refs_10_ = f32[8,256]{1,0:T(8,128)S(1)} collective-permute-done((f32[8,256]{1,0:T(8,128)S(1)}, f32[8,256]{1,0:T(8,128)S(1)}, u32[]{:S(2)}, u32[]{:S(2)}) %collective-permute-start.24) | collective-permute-done | bytes 8224 | tf_op jit(solution)/shard_map/ppermute | solution.py:391
  47.0 1.0 %shard_map.83 = bf16[256,1024]{1,0:T(8,128)(2,1)} custom-call(s32[1]{0:T(128)} %bitcast.places_ref._, f32[256,128]{1,0:T(8,128)S(1)} %get-tuple-element.83.refs_0_, f32[256,128]{1,0:T(8,128)S(1)} %get-tuple-element.84.refs_1_, f32[256,128]{1,0:T(8,128)S(1)} %get-tuple-element.97.refs_2_, f32[256,128]{1,0:T(8,128)S(1)} %get-tuple-element.98.refs_3_, ...), custom_call_target="tpu_custom_call" | custom-call | flops 786432 | bytes 1605636 | tf_op jit(solution)/shard_map/pallas_call | solution.py:234
  (63 shorter events, 5.5 us)
Async XLA Ops:
  0.0 7.0 %copy-start = (bf16[256,1024]{1,0:T(8,128)(2,1)S(1)}, bf16[256,1024]{1,0:T(8,128)(2,1)}, u32[]{:S(2)}) copy-start(bf16[256,1024]{1,0:T(8,128)(2,1)} %k_ref.7) | copy-start | bytes 1572868
  0.0 7.0 %copy-start.1 = (bf16[256,1024]{1,0:T(8,128)(2,1)S(1)}, bf16[256,1024]{1,0:T(8,128)(2,1)}, u32[]{:S(2)}) copy-start(bf16[256,1024]{1,0:T(8,128)(2,1)} %v_ref.7) | copy-start | bytes 1572868
  2.8 6.1 %collective-permute-start = (f32[136,256]{1,0:T(8,128)}, f32[136,256]{1,0:T(8,128)S(1)}, u32[]{:S(2)}, u32[]{:S(2)}) collective-permute-start(f32[136,256]{1,0:T(8,128)} %get-tuple-element.62), channel_id=1, source_target_pairs={{0,4},{4,0},{8,12},{12,8},{16,20},{20,16},{24,28},{28,24},{1,5},{5... | collective-permute-start | bytes 417800 | tf_op jit(solution)/shard_map/ppermute | solution.py:283
  4.0 3.0 %copy-start.4 = (f32[1024]{0:T(1024)S(1)}, f32[1024]{0:T(1024)}, u32[]{:S(2)}) copy-start(f32[1024]{0:T(1024)} %param.9) | copy-start | bytes 12292
  4.0 3.0 %copy-start.3 = (bf16[8,256]{1,0:T(8,128)(2,1)S(1)}, bf16[8,256]{1,0:T(8,128)(2,1)}, u32[]{:S(2)}) copy-start(bf16[8,256]{1,0:T(8,128)(2,1)} %seeds_ref.7) | copy-start | bytes 12292
  4.0 5.7 %collective-permute-start.1 = (f32[136,256]{1,0:T(8,128)}, f32[136,256]{1,0:T(8,128)S(1)}, u32[]{:S(2)}, u32[]{:S(2)}) collective-permute-start(f32[136,256]{1,0:T(8,128)} %get-tuple-element.63.refs_1_.refs_3_), channel_id=1, source_target_pairs={{0,8},{4,12},{1,9},{5,13},{2,10},{6,14},{3,11},{7,15}} | collective-permute-start | bytes 417800 | tf_op jit(solution)/shard_map/ppermute | solution.py:307
  4.8 6.3 %collective-permute-start.2 = (f32[128,256]{1,0:T(8,128)}, f32[128,256]{1,0:T(8,128)S(1)}, u32[]{:S(2)}, u32[]{:S(2)}) collective-permute-start(f32[128,256]{1,0:T(8,128)} %get-tuple-element.65), channel_id=1, source_target_pairs={{0,4},{4,0},{8,12},{12,8},{16,20},{20,16},{24,28},{28,24},{1,5},{5... | collective-permute-start | bytes 393224 | tf_op jit(solution)/shard_map/ppermute | solution.py:283
  5.2 8.3 %collective-permute-start.4 = (f32[128,256]{1,0:T(8,128)}, f32[128,256]{1,0:T(8,128)S(1)}, u32[]{:S(2)}, u32[]{:S(2)}) collective-permute-start(f32[128,256]{1,0:T(8,128)} %get-tuple-element.68), channel_id=1, source_target_pairs={{0,4},{4,0},{8,12},{12,8},{16,20},{20,16},{24,28},{28,24},{1,5},{5... | collective-permute-start | bytes 393224 | tf_op jit(solution)/shard_map/ppermute | solution.py:283
  6.4 5.6 %collective-permute-start.3 = (f32[136,256]{1,0:T(8,128)}, f32[136,256]{1,0:T(8,128)S(1)}, u32[]{:S(2)}, u32[]{:S(2)}) collective-permute-start(f32[136,256]{1,0:T(8,128)} %get-tuple-element.66.refs_1_.refs_3_), channel_id=1, source_target_pairs={{0,8},{4,12},{1,9},{5,13},{2,10},{6,14},{3,11},{7,15}} | collective-permute-start | bytes 417800 | tf_op jit(solution)/shard_map/ppermute | solution.py:307
  7.1 1.0 %copy-start.2 = (bf16[256,1024]{1,0:T(8,128)(2,1)S(1)}, bf16[256,1024]{1,0:T(8,128)(2,1)}, u32[]{:S(2)}) copy-start(bf16[256,1024]{1,0:T(8,128)(2,1)} %q_ref.7) | copy-start | bytes 1572868
  8.9 0.9 %copy-start.6 = (f32[136,256]{1,0:T(8,128)S(1)}, f32[136,256]{1,0:T(8,128)}, u32[]{:S(2)}) copy-start(f32[136,256]{1,0:T(8,128)} %get-tuple-element.63.refs_1_.refs_3_) | copy-start | bytes 417796
  8.9 5.2 %collective-permute-start.5 = (f32[136,256]{1,0:T(8,128)S(1)}, f32[136,256]{1,0:T(8,128)S(1)}, u32[]{:S(2)}, u32[]{:S(2)}) collective-permute-start(f32[136,256]{1,0:T(8,128)S(1)} %shard_map.58._), channel_id=1, source_target_pairs={{0,8},{4,12},{1,9},{5,13},{2,10},{6,14},{3,11},{7,15}} | collective-permute-start | bytes 417800 | tf_op jit(solution)/shard_map/ppermute | solution.py:307
  9.8 5.8 %collective-permute-start.6 = (f32[136,256]{1,0:T(8,128)S(1)}, f32[136,256]{1,0:T(8,128)S(1)}, u32[]{:S(2)}, u32[]{:S(2)}) collective-permute-start(f32[136,256]{1,0:T(8,128)S(1)} %shard_map.59._), channel_id=1, source_target_pairs={{8,16},{12,20},{9,17},{13,21},{10,18},{14,22},{11,19},{15,23}} | collective-permute-start | bytes 417800 | tf_op jit(solution)/shard_map/ppermute | solution.py:307
  11.1 7.0 %collective-permute-start.7 = (f32[128,256]{1,0:T(8,128)S(1)}, f32[128,256]{1,0:T(8,128)S(1)}, u32[]{:S(2)}, u32[]{:S(2)}) collective-permute-start(f32[128,256]{1,0:T(8,128)S(1)} %shard_map.60._), channel_id=1, source_target_pairs={{0,8},{4,12},{1,9},{5,13},{2,10},{6,14},{3,11},{7,15}} | collective-permute-start | bytes 393224 | tf_op jit(solution)/shard_map/ppermute | solution.py:307
  12.0 7.4 %collective-permute-start.8 = (f32[136,256]{1,0:T(8,128)S(1)}, f32[136,256]{1,0:T(8,128)S(1)}, u32[]{:S(2)}, u32[]{:S(2)}) collective-permute-start(f32[136,256]{1,0:T(8,128)S(1)} %shard_map.61._), channel_id=1, source_target_pairs={{8,16},{12,20},{9,17},{13,21},{10,18},{14,22},{11,19},{15,23}} | collective-permute-start | bytes 417800 | tf_op jit(solution)/shard_map/ppermute | solution.py:307
  13.4 7.3 %collective-permute-start.9 = (f32[128,256]{1,0:T(8,128)S(1)}, f32[128,256]{1,0:T(8,128)S(1)}, u32[]{:S(2)}, u32[]{:S(2)}) collective-permute-start(f32[128,256]{1,0:T(8,128)S(1)} %shard_map.62._), channel_id=1, source_target_pairs={{0,8},{4,12},{1,9},{5,13},{2,10},{6,14},{3,11},{7,15}} | collective-permute-start | bytes 393224 | tf_op jit(solution)/shard_map/ppermute | solution.py:307
  14.2 8.2 %collective-permute-start.10 = (f32[136,256]{1,0:T(8,128)S(1)}, f32[136,256]{1,0:T(8,128)S(1)}, u32[]{:S(2)}, u32[]{:S(2)}) collective-permute-start(f32[136,256]{1,0:T(8,128)S(1)} %shard_map.63._), channel_id=1, source_target_pairs={{8,16},{12,20},{9,17},{13,21},{10,18},{14,22},{11,19},{15,23}} | collective-permute-start | bytes 417800 | tf_op jit(solution)/shard_map/ppermute | solution.py:307
  15.6 8.1 %collective-permute-start.11 = (f32[136,256]{1,0:T(8,128)S(1)}, f32[136,256]{1,0:T(8,128)S(1)}, u32[]{:S(2)}, u32[]{:S(2)}) collective-permute-start(f32[136,256]{1,0:T(8,128)S(1)} %shard_map.64._), channel_id=1, source_target_pairs={{16,24},{20,28},{17,25},{21,29},{18,26},{22,30},{19,27},{23,31}} | collective-permute-start | bytes 417800 | tf_op jit(solution)/shard_map/ppermute | solution.py:307
  18.1 6.8 %collective-permute-start.12 = (f32[128,256]{1,0:T(8,128)S(1)}, f32[128,256]{1,0:T(8,128)S(1)}, u32[]{:S(2)}, u32[]{:S(2)}) collective-permute-start(f32[128,256]{1,0:T(8,128)S(1)} %shard_map.65._), channel_id=1, source_target_pairs={{8,16},{12,20},{9,17},{13,21},{10,18},{14,22},{11,19},{15,23}} | collective-permute-start | bytes 393224 | tf_op jit(solution)/shard_map/ppermute | solution.py:307
  19.5 6.8 %collective-permute-start.13 = (f32[136,256]{1,0:T(8,128)S(1)}, f32[136,256]{1,0:T(8,128)S(1)}, u32[]{:S(2)}, u32[]{:S(2)}) collective-permute-start(f32[136,256]{1,0:T(8,128)S(1)} %shard_map.66._), channel_id=1, source_target_pairs={{16,24},{20,28},{17,25},{21,29},{18,26},{22,30},{19,27},{23,31}} | collective-permute-start | bytes 417800 | tf_op jit(solution)/shard_map/ppermute | solution.py:307
  20.8 7.4 %collective-permute-start.14 = (f32[128,256]{1,0:T(8,128)S(1)}, f32[128,256]{1,0:T(8,128)S(1)}, u32[]{:S(2)}, u32[]{:S(2)}) collective-permute-start(f32[128,256]{1,0:T(8,128)S(1)} %shard_map.67._), channel_id=1, source_target_pairs={{8,16},{12,20},{9,17},{13,21},{10,18},{14,22},{11,19},{15,23}} | collective-permute-start | bytes 393224 | tf_op jit(solution)/shard_map/ppermute | solution.py:307
  22.4 7.2 %collective-permute-start.15 = (f32[136,256]{1,0:T(8,128)S(1)}, f32[136,256]{1,0:T(8,128)S(1)}, u32[]{:S(2)}, u32[]{:S(2)}) collective-permute-start(f32[136,256]{1,0:T(8,128)S(1)} %shard_map.68._), channel_id=1, source_target_pairs={{16,24},{20,28},{17,25},{21,29},{18,26},{22,30},{19,27},{23,31}} | collective-permute-start | bytes 417800 | tf_op jit(solution)/shard_map/ppermute | solution.py:307
  23.8 10.5 %collective-permute-start.18 = (f32[136,256]{1,0:T(8,128)S(1)}, f32[136,256]{1,0:T(8,128)S(1)}, u32[]{:S(2)}, u32[]{:S(2)}) collective-permute-start(f32[136,256]{1,0:T(8,128)S(1)} %get-tuple-element.69._), channel_id=1, source_target_pairs={{0,4},{4,0},{8,12},{12,8},{16,20},{20,16},{24,28},{28,24},{1,5},{5... | collective-permute-start | bytes 417800 | tf_op jit(solution)/shard_map/ppermute | solution.py:323
  25.0 4.9 %collective-permute-start.16 = (f32[128,256]{1,0:T(8,128)S(1)}, f32[128,256]{1,0:T(8,128)S(1)}, u32[]{:S(2)}, u32[]{:S(2)}) collective-permute-start(f32[128,256]{1,0:T(8,128)S(1)} %shard_map.70._), channel_id=1, source_target_pairs={{16,24},{20,28},{17,25},{21,29},{18,26},{22,30},{19,27},{23,31}} | collective-permute-start | bytes 393224 | tf_op jit(solution)/shard_map/ppermute | solution.py:307
  26.4 7.9 %collective-permute-start.19 = (f32[136,256]{1,0:T(8,128)S(1)}, f32[136,256]{1,0:T(8,128)S(1)}, u32[]{:S(2)}, u32[]{:S(2)}) collective-permute-start(f32[136,256]{1,0:T(8,128)S(1)} %get-tuple-element.70._), channel_id=1, source_target_pairs={{0,4},{4,0},{8,12},{12,8},{16,20},{20,16},{24,28},{28,24},{1,5},{5... | collective-permute-start | bytes 417800 | tf_op jit(solution)/shard_map/ppermute | solution.py:323
  28.3 3.5 %collective-permute-start.17 = (f32[128,256]{1,0:T(8,128)S(1)}, f32[128,256]{1,0:T(8,128)S(1)}, u32[]{:S(2)}, u32[]{:S(2)}) collective-permute-start(f32[128,256]{1,0:T(8,128)S(1)} %shard_map.72._), channel_id=1, source_target_pairs={{16,24},{20,28},{17,25},{21,29},{18,26},{22,30},{19,27},{23,31}} | collective-permute-start | bytes 393224 | tf_op jit(solution)/shard_map/ppermute | solution.py:307
  29.7 7.1 %collective-permute-start.20 = (f32[136,256]{1,0:T(8,128)S(1)}, f32[136,256]{1,0:T(8,128)S(1)}, u32[]{:S(2)}, u32[]{:S(2)}) collective-permute-start(f32[136,256]{1,0:T(8,128)S(1)} %get-tuple-element.71._), channel_id=1, source_target_pairs={{0,4},{4,0},{8,12},{12,8},{16,20},{20,16},{24,28},{28,24},{1,5},{5... | collective-permute-start | bytes 417800 | tf_op jit(solution)/shard_map/ppermute | solution.py:323
  29.9 6.9 %collective-permute-start.21 = (f32[128,256]{1,0:T(8,128)S(1)}, f32[128,256]{1,0:T(8,128)S(1)}, u32[]{:S(2)}, u32[]{:S(2)}) collective-permute-start(f32[128,256]{1,0:T(8,128)S(1)} %get-tuple-element.72._), channel_id=1, source_target_pairs={{0,4},{4,0},{8,12},{12,8},{16,20},{20,16},{24,28},{28,24},{1,5},{5... | collective-permute-start | bytes 393224 | tf_op jit(solution)/shard_map/ppermute | solution.py:323
  31.9 7.5 %collective-permute-start.22 = (f32[128,256]{1,0:T(8,128)S(1)}, f32[128,256]{1,0:T(8,128)S(1)}, u32[]{:S(2)}, u32[]{:S(2)}) collective-permute-start(f32[128,256]{1,0:T(8,128)S(1)} %get-tuple-element.73._), channel_id=1, source_target_pairs={{0,4},{4,0},{8,12},{12,8},{16,20},{20,16},{24,28},{28,24},{1,5},{5... | collective-permute-start | bytes 393224 | tf_op jit(solution)/shard_map/ppermute | solution.py:323
  39.8 6.3 %collective-permute-start.25 = (f32[8,256]{1,0:T(8,128)S(1)}, f32[8,256]{1,0:T(8,128)S(1)}, u32[]{:S(2)}, u32[]{:S(2)}) collective-permute-start(f32[8,256]{1,0:T(8,128)S(1)} %get-tuple-element.114.refs_8_), channel_id=1, source_target_pairs={{0,3},{1,2},{2,1},{3,0},{4,7},{5,6},{6,5},{7,4},{8,11},{9,10},{10,... | collective-permute-start | bytes 24584 | tf_op jit(solution)/shard_map/ppermute | solution.py:391
  44.5 2.5 %collective-permute-start.24 = (f32[8,256]{1,0:T(8,128)S(1)}, f32[8,256]{1,0:T(8,128)S(1)}, u32[]{:S(2)}, u32[]{:S(2)}) collective-permute-start(f32[8,256]{1,0:T(8,128)S(1)} %get-tuple-element.114.refs_8_), channel_id=1, source_target_pairs={{0,2},{1,3},{2,0},{3,1},{4,6},{5,7},{6,4},{7,5},{8,10},{9,11},{10,... | collective-permute-start | bytes 24584 | tf_op jit(solution)/shard_map/ppermute | solution.py:391
  44.7 2.3 %collective-permute-start.23 = (f32[8,256]{1,0:T(8,128)S(1)}, f32[8,256]{1,0:T(8,128)S(1)}, u32[]{:S(2)}, u32[]{:S(2)}) collective-permute-start(f32[8,256]{1,0:T(8,128)S(1)} %get-tuple-element.114.refs_8_), channel_id=1, source_target_pairs={{0,1},{1,0},{2,3},{3,2},{4,5},{5,4},{6,7},{7,6},{8,9},{9,8},{10,11... | collective-permute-start | bytes 24584 | tf_op jit(solution)/shard_map/ppermute | solution.py:391
  (1 other events, 0.9 us)

commit v8 on v7

--- a/solution.py
+++ b/solution.py
@@ -389,7 +389,7 @@
             hop(kind, i)
     gathered = [squares] + [
         lax.ppermute(squares, "tp", [(i, (i ^ k) if across == 4 else (i + k) % across) for i in range(across)])
-        for k in range(1, across)
+        for k in range(across - 1, 0, -1)
     ]
     return call(
         functools.partial(norm_kernel, half, heads * WIDTH * across, list(results)),

time: 48.4 us -> 49.1 us (1.014)
  waiting for transfers between devices: 6.3 us -> 6.89 us
    ppermute x3, waiting for transfers between devices: 2.03 us -> 2.62 us  [per_device(): lax.ppermute(squares, 'tp', [(i, i ^ k if across == 4 else (i + k) % acro...]
where the time goes in v8:
time: 49.1 us; the launch traced here: 48.7 us
  starting transfers between devices  31.5 us (64%)
  Pallas kernels  9.5 us (19%)
  waiting for transfers between devices  6.89 us (14%)
    ppermute x15, starting transfers between devices, hop(): arrivals[stage, i] = lax.ppermute(sent, 'seq', pairs)  17.8 us
    pallas_call x29, Pallas kernels, call(): pl.pallas_call(kernel, out_shape=outs, in_specs=[SMEM, *specs] + [place]...  9.5 us
    ppermute x5, starting transfers between devices, hand(): passed[i] = lax.ppermute(last, 'seq', swap)  5.51 us
    ppermute x3, starting transfers between devices, per_device(): lax.ppermute(squares, 'tp', [(i, i ^ k if across == 4 else (i + k) % acro...  5.31 us
    ppermute x3, starting transfers between devices, per_device(): incoming = [lax.ppermute(part, 'seq', swap) for part in [*theirs, *cross]]  2.81 us
    ppermute x3, waiting for transfers between devices, per_device(): lax.ppermute(squares, 'tp', [(i, i ^ k if across == 4 else (i + k) % acro...  2.62 us
    ppermute x5, waiting for transfers between devices, hand(): passed[i] = lax.ppermute(last, 'seq', swap)  2.46 us
    ppermute x15, waiting for transfers between devices, hop(): arrivals[stage, i] = lax.ppermute(sent, 'seq', pairs)  1.71 us
  transfers between devices with their start and end apart: 26, of which 10 were waited for; matrix products, arithmetic and copies ran while one was open for 0% of the time, Pallas kernels for 11%

profile of v8, /device:TPU:17, one launch (start us, length us, event | category | flops | bytes accessed | tf_op | source)
XLA Modules:
  0.0 48.7 jit_solution(18375918163785082600)
XLA Ops:
  0.0 2.7 %shard_map.57 = (f32[136,256]{1,0:T(8,128)}, f32[136,256]{1,0:T(8,128)}, f32[136,256]{1,0:T(8,128)}, f32[128,256]{1,0:T(8,128)}, f32[128,256]{1,0:T(8,128)}) custom-call(s32[1]{0:T(128)} %bitcast.places_ref._, bf16[8,256]{1,0:T(8,128)(2,1)} %seeds_ref.7, bf16[256,1024]{1,0:T(8,128)(2,1)} %k_ref.7, bf16[256,1024]{1,0:T(8,128)(2,1)} %v_ref.7), custom_call_target="tpu_custom_call" | custom-call | flops 167772160 | bytes 1732612 | tf_op jit(solution)/shard_map/pallas_call | solution.py:234
  2.8 1.3 %collective-permute-start = (f32[136,256]{1,0:T(8,128)}, f32[136,256]{1,0:T(8,128)S(1)}, u32[]{:S(2)}, u32[]{:S(2)}) collective-permute-start(f32[136,256]{1,0:T(8,128)} %get-tuple-element.62), channel_id=1, source_target_pairs={{0,4},{4,0},{8,12},{12,8},{16,20},{20,16},{24,28},{28,24},{1,5},{5... | collective-permute-start | bytes 417800 | tf_op jit(solution)/shard_map/ppermute | solution.py:283
  4.0 0.8 %collective-permute-start.1 = (f32[136,256]{1,0:T(8,128)}, f32[136,256]{1,0:T(8,128)S(1)}, u32[]{:S(2)}, u32[]{:S(2)}) collective-permute-start(f32[136,256]{1,0:T(8,128)} %get-tuple-element.63.refs_1_.refs_3_), channel_id=1, source_target_pairs={{0,8},{4,12},{1,9},{5,13},{2,10},{6,14},{3,11},{7,15}} | collective-permute-start | bytes 417800 | tf_op jit(solution)/shard_map/ppermute | solution.py:307
  5.2 1.2 %collective-permute-start.4 = (f32[128,256]{1,0:T(8,128)}, f32[128,256]{1,0:T(8,128)S(1)}, u32[]{:S(2)}, u32[]{:S(2)}) collective-permute-start(f32[128,256]{1,0:T(8,128)} %get-tuple-element.68), channel_id=1, source_target_pairs={{0,4},{4,0},{8,12},{12,8},{16,20},{20,16},{24,28},{28,24},{1,5},{5... | collective-permute-start | bytes 393224 | tf_op jit(solution)/shard_map/ppermute | solution.py:283
  7.1 0.7 %shard_map.56 = (f32[136,256]{1,0:T(8,128)S(1)}, f32[128,256]{1,0:T(8,128)S(1)}, f32[128,256]{1,0:T(8,128)S(1)}, f32[1,1024]{1,0:T(1,128)S(1)}) custom-call(s32[1]{0:T(128)} %bitcast.places_ref._, bf16[8,256]{1,0:T(8,128)(2,1)S(1)} %copy-done.3, bf16[256,1024]{1,0:T(8,128)(2,1)S(1)} %copy-done, bf16[256,1024]{1,0:T(8,128)(2,1)S(1)} %copy-done.1, ...), custom_call_target="tpu_custom_call" | custom-call | flops 100663296 | bytes 1462276 | tf_op jit(solution)/shard_map/pallas_call | solution.py:234
  8.1 0.7 %shard_map.55 = (f32[256,128]{1,0:T(8,128)S(1)}, f32[256,128]{1,0:T(8,128)S(1)}, bf16[256,256]{1,0:T(8,128)(2,1)S(1)}, f32[256,128]{1,0:T(8,128)S(1)}, f32[256,1...) custom-call(s32[1]{0:T(128)} %bitcast.places_ref._, s32[1]{0:T(128)} %bitcast.places_ref._, bf16[8,256]{1,0:T(8,128)(2,1)S(1)} %copy-done.3, ...), custom_call_target="tpu_custom_call" | custom-call | flops 167772160 | bytes 2363400 | tf_op jit(solution)/shard_map/pallas_call | solution.py:234
  8.9 0.8 %collective-permute-start.5 = (f32[136,256]{1,0:T(8,128)S(1)}, f32[136,256]{1,0:T(8,128)S(1)}, u32[]{:S(2)}, u32[]{:S(2)}) collective-permute-start(f32[136,256]{1,0:T(8,128)S(1)} %shard_map.58._), channel_id=1, source_target_pairs={{0,8},{4,12},{1,9},{5,13},{2,10},{6,14},{3,11},{7,15}} | collective-permute-start | bytes 417800 | tf_op jit(solution)/shard_map/ppermute | solution.py:307
  9.8 1.3 %collective-permute-start.6 = (f32[136,256]{1,0:T(8,128)S(1)}, f32[136,256]{1,0:T(8,128)S(1)}, u32[]{:S(2)}, u32[]{:S(2)}) collective-permute-start(f32[136,256]{1,0:T(8,128)S(1)} %shard_map.59._), channel_id=1, source_target_pairs={{8,16},{12,20},{9,17},{13,21},{10,18},{14,22},{11,19},{15,23}} | collective-permute-start | bytes 417800 | tf_op jit(solution)/shard_map/ppermute | solution.py:307
  11.1 0.8 %collective-permute-start.7 = (f32[128,256]{1,0:T(8,128)S(1)}, f32[128,256]{1,0:T(8,128)S(1)}, u32[]{:S(2)}, u32[]{:S(2)}) collective-permute-start(f32[128,256]{1,0:T(8,128)S(1)} %shard_map.60._), channel_id=1, source_target_pairs={{0,8},{4,12},{1,9},{5,13},{2,10},{6,14},{3,11},{7,15}} | collective-permute-start | bytes 393224 | tf_op jit(solution)/shard_map/ppermute | solution.py:307
  12.0 1.3 %collective-permute-start.8 = (f32[136,256]{1,0:T(8,128)S(1)}, f32[136,256]{1,0:T(8,128)S(1)}, u32[]{:S(2)}, u32[]{:S(2)}) collective-permute-start(f32[136,256]{1,0:T(8,128)S(1)} %shard_map.61._), channel_id=1, source_target_pairs={{8,16},{12,20},{9,17},{13,21},{10,18},{14,22},{11,19},{15,23}} | collective-permute-start | bytes 417800 | tf_op jit(solution)/shard_map/ppermute | solution.py:307
  14.2 1.3 %collective-permute-start.10 = (f32[136,256]{1,0:T(8,128)S(1)}, f32[136,256]{1,0:T(8,128)S(1)}, u32[]{:S(2)}, u32[]{:S(2)}) collective-permute-start(f32[136,256]{1,0:T(8,128)S(1)} %shard_map.63._), channel_id=1, source_target_pairs={{8,16},{12,20},{9,17},{13,21},{10,18},{14,22},{11,19},{15,23}} | collective-permute-start | bytes 417800 | tf_op jit(solution)/shard_map/ppermute | solution.py:307
  15.6 2.5 %collective-permute-start.11 = (f32[136,256]{1,0:T(8,128)S(1)}, f32[136,256]{1,0:T(8,128)S(1)}, u32[]{:S(2)}, u32[]{:S(2)}) collective-permute-start(f32[136,256]{1,0:T(8,128)S(1)} %shard_map.64._), channel_id=1, source_target_pairs={{16,24},{20,28},{17,25},{21,29},{18,26},{22,30},{19,27},{23,31}} | collective-permute-start | bytes 417800 | tf_op jit(solution)/shard_map/ppermute | solution.py:307
  18.1 1.3 %collective-permute-start.12 = (f32[128,256]{1,0:T(8,128)S(1)}, f32[128,256]{1,0:T(8,128)S(1)}, u32[]{:S(2)}, u32[]{:S(2)}) collective-permute-start(f32[128,256]{1,0:T(8,128)S(1)} %shard_map.65._), channel_id=1, source_target_pairs={{8,16},{12,20},{9,17},{13,21},{10,18},{14,22},{11,19},{15,23}} | collective-permute-start | bytes 393224 | tf_op jit(solution)/shard_map/ppermute | solution.py:307
  19.5 1.3 %collective-permute-start.13 = (f32[136,256]{1,0:T(8,128)S(1)}, f32[136,256]{1,0:T(8,128)S(1)}, u32[]{:S(2)}, u32[]{:S(2)}) collective-permute-start(f32[136,256]{1,0:T(8,128)S(1)} %shard_map.66._), channel_id=1, source_target_pairs={{16,24},{20,28},{17,25},{21,29},{18,26},{22,30},{19,27},{23,31}} | collective-permute-start | bytes 417800 | tf_op jit(solution)/shard_map/ppermute | solution.py:307
  20.8 1.3 %collective-permute-start.14 = (f32[128,256]{1,0:T(8,128)S(1)}, f32[128,256]{1,0:T(8,128)S(1)}, u32[]{:S(2)}, u32[]{:S(2)}) collective-permute-start(f32[128,256]{1,0:T(8,128)S(1)} %shard_map.67._), channel_id=1, source_target_pairs={{8,16},{12,20},{9,17},{13,21},{10,18},{14,22},{11,19},{15,23}} | collective-permute-start | bytes 393224 | tf_op jit(solution)/shard_map/ppermute | solution.py:307
  22.4 1.3 %collective-permute-start.15 = (f32[136,256]{1,0:T(8,128)S(1)}, f32[136,256]{1,0:T(8,128)S(1)}, u32[]{:S(2)}, u32[]{:S(2)}) collective-permute-start(f32[136,256]{1,0:T(8,128)S(1)} %shard_map.68._), channel_id=1, source_target_pairs={{16,24},{20,28},{17,25},{21,29},{18,26},{22,30},{19,27},{23,31}} | collective-permute-start | bytes 417800 | tf_op jit(solution)/shard_map/ppermute | solution.py:307
  23.8 1.1 %collective-permute-start.18 = (f32[136,256]{1,0:T(8,128)S(1)}, f32[136,256]{1,0:T(8,128)S(1)}, u32[]{:S(2)}, u32[]{:S(2)}) collective-permute-start(f32[136,256]{1,0:T(8,128)S(1)} %get-tuple-element.69._), channel_id=1, source_target_pairs={{0,4},{4,0},{8,12},{12,8},{16,20},{20,16},{24,28},{28,24},{1,5},{5... | collective-permute-start | bytes 417800 | tf_op jit(solution)/shard_map/ppermute | solution.py:323
  25.0 1.3 %collective-permute-start.16 = (f32[128,256]{1,0:T(8,128)S(1)}, f32[128,256]{1,0:T(8,128)S(1)}, u32[]{:S(2)}, u32[]{:S(2)}) collective-permute-start(f32[128,256]{1,0:T(8,128)S(1)} %shard_map.70._), channel_id=1, source_target_pairs={{16,24},{20,28},{17,25},{21,29},{18,26},{22,30},{19,27},{23,31}} | collective-permute-start | bytes 393224 | tf_op jit(solution)/shard_map/ppermute | solution.py:307
  26.4 1.2 %collective-permute-start.19 = (f32[136,256]{1,0:T(8,128)S(1)}, f32[136,256]{1,0:T(8,128)S(1)}, u32[]{:S(2)}, u32[]{:S(2)}) collective-permute-start(f32[136,256]{1,0:T(8,128)S(1)} %get-tuple-element.70._), channel_id=1, source_target_pairs={{0,4},{4,0},{8,12},{12,8},{16,20},{20,16},{24,28},{28,24},{1,5},{5... | collective-permute-start | bytes 417800 | tf_op jit(solution)/shard_map/ppermute | solution.py:323
  27.5 0.7 %collective-permute-done.14.refs_0_.refs_1_ = f32[128,256]{1,0:T(8,128)S(1)} collective-permute-done((f32[128,256]{1,0:T(8,128)S(1)}, f32[128,256]{1,0:T(8,128)S(1)}, u32[]{:S(2)}, u32[]{:S(2)}) %collective-permute-start.14) | collective-permute-done | bytes 131104 | tf_op jit(solution)/shard_map/ppermute | solution.py:307
  28.3 1.3 %collective-permute-start.17 = (f32[128,256]{1,0:T(8,128)S(1)}, f32[128,256]{1,0:T(8,128)S(1)}, u32[]{:S(2)}, u32[]{:S(2)}) collective-permute-start(f32[128,256]{1,0:T(8,128)S(1)} %shard_map.72._), channel_id=1, source_target_pairs={{16,24},{20,28},{17,25},{21,29},{18,26},{22,30},{19,27},{23,31}} | collective-permute-start | bytes 393224 | tf_op jit(solution)/shard_map/ppermute | solution.py:307
  29.9 1.4 %collective-permute-start.21 = (f32[128,256]{1,0:T(8,128)S(1)}, f32[128,256]{1,0:T(8,128)S(1)}, u32[]{:S(2)}, u32[]{:S(2)}) collective-permute-start(f32[128,256]{1,0:T(8,128)S(1)} %get-tuple-element.72._), channel_id=1, source_target_pairs={{0,4},{4,0},{8,12},{12,8},{16,20},{20,16},{24,28},{28,24},{1,5},{5... | collective-permute-start | bytes 393224 | tf_op jit(solution)/shard_map/ppermute | solution.py:323
  31.9 1.6 %collective-permute-start.22 = (f32[128,256]{1,0:T(8,128)S(1)}, f32[128,256]{1,0:T(8,128)S(1)}, u32[]{:S(2)}, u32[]{:S(2)}) collective-permute-start(f32[128,256]{1,0:T(8,128)S(1)} %get-tuple-element.73._), channel_id=1, source_target_pairs={{0,4},{4,0},{8,12},{12,8},{16,20},{20,16},{24,28},{28,24},{1,5},{5... | collective-permute-start | bytes 393224 | tf_op jit(solution)/shard_map/ppermute | solution.py:323
  33.5 0.7 %shard_map.76 = (f32[256,128]{1,0:T(8,128)S(1)}, f32[256,128]{1,0:T(8,128)S(1)}, bf16[256,256]{1,0:T(8,128)(2,1)S(1)}, f32[256,128]{1,0:T(8,128)S(1)}, f32[256,1...) custom-call(s32[1]{0:T(128)} %bitcast.places_ref._, f32[128,256]{1,0:T(8,128)S(1)} %get-tuple-element.73._, ...), custom_call_target="tpu_custom_call" | custom-call | flops 167772160 | bytes 2494468 | tf_op jit(solution)/shard_map/pallas_call | solution.py:234
  34.6 0.7 %shard_map.78 = (f32[256,128]{1,0:T(8,128)S(1)}, f32[256,128]{1,0:T(8,128)S(1)}, bf16[256,256]{1,0:T(8,128)(2,1)S(1)}, f32[256,128]{1,0:T(8,128)S(1)}, f32[256,1...) custom-call(s32[1]{0:T(128)} %bitcast.places_ref._, f32[256,128]{1,0:T(8,128)S(1)} %get-tuple-element.85._.refs_15_, ...), custom_call_target="tpu_custom_call" | custom-call | flops 167772160 | bytes 2494468 | tf_op jit(solution)/shard_map/pallas_call | solution.py:234
  35.4 0.7 %shard_map.79 = (f32[256,128]{1,0:T(8,128)S(1)}, f32[256,128]{1,0:T(8,128)S(1)}, bf16[256,256]{1,0:T(8,128)(2,1)S(1)}, f32[256,128]{1,0:T(8,128)S(1)}, f32[256,1...) custom-call(s32[1]{0:T(128)} %bitcast.places_ref._, f32[256,128]{1,0:T(8,128)S(1)} %get-tuple-element.86._.refs_4_, ...), custom_call_target="tpu_custom_call" | custom-call | flops 167772160 | bytes 2494468 | tf_op jit(solution)/shard_map/pallas_call | solution.py:234
  37.1 2.2 %collective-permute-done.22.refs_5_ = f32[128,256]{1,0:T(8,128)S(1)} collective-permute-done((f32[128,256]{1,0:T(8,128)S(1)}, f32[128,256]{1,0:T(8,128)S(1)}, u32[]{:S(2)}, u32[]{:S(2)}) %collective-permute-start.22) | collective-permute-done | bytes 131104 | tf_op jit(solution)/shard_map/ppermute | solution.py:323
  39.8 3.6 %collective-permute-start.25 = (f32[8,256]{1,0:T(8,128)S(1)}, f32[8,256]{1,0:T(8,128)S(1)}, u32[]{:S(2)}, u32[]{:S(2)}) collective-permute-start(f32[8,256]{1,0:T(8,128)S(1)} %get-tuple-element.114.refs_8_), channel_id=1, source_target_pairs={{0,1},{1,0},{2,3},{3,2},{4,5},{5,4},{6,7},{7,6},{8,9},{9,8},{10,11... | collective-permute-start | bytes 24584 | tf_op jit(solution)/shard_map/ppermute | solution.py:391
  43.4 1.3 %collective-permute-start.24 = (f32[8,256]{1,0:T(8,128)S(1)}, f32[8,256]{1,0:T(8,128)S(1)}, u32[]{:S(2)}, u32[]{:S(2)}) collective-permute-start(f32[8,256]{1,0:T(8,128)S(1)} %get-tuple-element.114.refs_8_), channel_id=1, source_target_pairs={{0,2},{1,3},{2,0},{3,1},{4,6},{5,7},{6,4},{7,5},{8,10},{9,11},{10,... | collective-permute-start | bytes 24584 | tf_op jit(solution)/shard_map/ppermute | solution.py:391
  45.1 0.8 %collective-permute-done.24.refs_10_ = f32[8,256]{1,0:T(8,128)S(1)} collective-permute-done((f32[8,256]{1,0:T(8,128)S(1)}, f32[8,256]{1,0:T(8,128)S(1)}, u32[]{:S(2)}, u32[]{:S(2)}) %collective-permute-start.24) | collective-permute-done | bytes 8224 | tf_op jit(solution)/shard_map/ppermute | solution.py:391
  45.9 1.8 %collective-permute-done.23.refs_9_ = f32[8,256]{1,0:T(8,128)S(1)} collective-permute-done((f32[8,256]{1,0:T(8,128)S(1)}, f32[8,256]{1,0:T(8,128)S(1)}, u32[]{:S(2)}, u32[]{:S(2)}) %collective-permute-start.23) | collective-permute-done | bytes 8224 | tf_op jit(solution)/shard_map/ppermute | solution.py:391
  47.7 1.0 %shard_map.83 = bf16[256,1024]{1,0:T(8,128)(2,1)} custom-call(s32[1]{0:T(128)} %bitcast.places_ref._, f32[256,128]{1,0:T(8,128)S(1)} %get-tuple-element.83.refs_0_, f32[256,128]{1,0:T(8,128)S(1)} %get-tuple-element.84.refs_1_, f32[256,128]{1,0:T(8,128)S(1)} %get-tuple-element.97.refs_2_, f32[256,128]{1,0:T(8,128)S(1)} %get-tuple-element.98.refs_3_, ...), custom_call_target="tpu_custom_call" | custom-call | flops 786432 | bytes 1605636 | tf_op jit(solution)/shard_map/pallas_call | solution.py:234
  (63 shorter events, 6.1 us)
Async XLA Ops:
  0.0 7.0 %copy-start = (bf16[256,1024]{1,0:T(8,128)(2,1)S(1)}, bf16[256,1024]{1,0:T(8,128)(2,1)}, u32[]{:S(2)}) copy-start(bf16[256,1024]{1,0:T(8,128)(2,1)} %k_ref.7) | copy-start | bytes 1572868
  0.0 7.0 %copy-start.1 = (bf16[256,1024]{1,0:T(8,128)(2,1)S(1)}, bf16[256,1024]{1,0:T(8,128)(2,1)}, u32[]{:S(2)}) copy-start(bf16[256,1024]{1,0:T(8,128)(2,1)} %v_ref.7) | copy-start | bytes 1572868
  2.8 6.1 %collective-permute-start = (f32[136,256]{1,0:T(8,128)}, f32[136,256]{1,0:T(8,128)S(1)}, u32[]{:S(2)}, u32[]{:S(2)}) collective-permute-start(f32[136,256]{1,0:T(8,128)} %get-tuple-element.62), channel_id=1, source_target_pairs={{0,4},{4,0},{8,12},{12,8},{16,20},{20,16},{24,28},{28,24},{1,5},{5... | collective-permute-start | bytes 417800 | tf_op jit(solution)/shard_map/ppermute | solution.py:283
  4.0 3.0 %copy-start.4 = (f32[1024]{0:T(1024)S(1)}, f32[1024]{0:T(1024)}, u32[]{:S(2)}) copy-start(f32[1024]{0:T(1024)} %param.9) | copy-start | bytes 12292
  4.0 3.0 %copy-start.3 = (bf16[8,256]{1,0:T(8,128)(2,1)S(1)}, bf16[8,256]{1,0:T(8,128)(2,1)}, u32[]{:S(2)}) copy-start(bf16[8,256]{1,0:T(8,128)(2,1)} %seeds_ref.7) | copy-start | bytes 12292
  4.0 5.7 %collective-permute-start.1 = (f32[136,256]{1,0:T(8,128)}, f32[136,256]{1,0:T(8,128)S(1)}, u32[]{:S(2)}, u32[]{:S(2)}) collective-permute-start(f32[136,256]{1,0:T(8,128)} %get-tuple-element.63.refs_1_.refs_3_), channel_id=1, source_target_pairs={{0,8},{4,12},{1,9},{5,13},{2,10},{6,14},{3,11},{7,15}} | collective-permute-start | bytes 417800 | tf_op jit(solution)/shard_map/ppermute | solution.py:307
  4.8 6.3 %collective-permute-start.2 = (f32[128,256]{1,0:T(8,128)}, f32[128,256]{1,0:T(8,128)S(1)}, u32[]{:S(2)}, u32[]{:S(2)}) collective-permute-start(f32[128,256]{1,0:T(8,128)} %get-tuple-element.65), channel_id=1, source_target_pairs={{0,4},{4,0},{8,12},{12,8},{16,20},{20,16},{24,28},{28,24},{1,5},{5... | collective-permute-start | bytes 393224 | tf_op jit(solution)/shard_map/ppermute | solution.py:283
  5.2 8.3 %collective-permute-start.4 = (f32[128,256]{1,0:T(8,128)}, f32[128,256]{1,0:T(8,128)S(1)}, u32[]{:S(2)}, u32[]{:S(2)}) collective-permute-start(f32[128,256]{1,0:T(8,128)} %get-tuple-element.68), channel_id=1, source_target_pairs={{0,4},{4,0},{8,12},{12,8},{16,20},{20,16},{24,28},{28,24},{1,5},{5... | collective-permute-start | bytes 393224 | tf_op jit(solution)/shard_map/ppermute | solution.py:283
  6.4 5.6 %collective-permute-start.3 = (f32[136,256]{1,0:T(8,128)}, f32[136,256]{1,0:T(8,128)S(1)}, u32[]{:S(2)}, u32[]{:S(2)}) collective-permute-start(f32[136,256]{1,0:T(8,128)} %get-tuple-element.66.refs_1_.refs_3_), channel_id=1, source_target_pairs={{0,8},{4,12},{1,9},{5,13},{2,10},{6,14},{3,11},{7,15}} | collective-permute-start | bytes 417800 | tf_op jit(solution)/shard_map/ppermute | solution.py:307
  7.1 1.0 %copy-start.2 = (bf16[256,1024]{1,0:T(8,128)(2,1)S(1)}, bf16[256,1024]{1,0:T(8,128)(2,1)}, u32[]{:S(2)}) copy-start(bf16[256,1024]{1,0:T(8,128)(2,1)} %q_ref.7) | copy-start | bytes 1572868
  8.9 0.9 %copy-start.6 = (f32[136,256]{1,0:T(8,128)S(1)}, f32[136,256]{1,0:T(8,128)}, u32[]{:S(2)}) copy-start(f32[136,256]{1,0:T(8,128)} %get-tuple-element.63.refs_1_.refs_3_) | copy-start | bytes 417796
  8.9 5.2 %collective-permute-start.5 = (f32[136,256]{1,0:T(8,128)S(1)}, f32[136,256]{1,0:T(8,128)S(1)}, u32[]{:S(2)}, u32[]{:S(2)}) collective-permute-start(f32[136,256]{1,0:T(8,128)S(1)} %shard_map.58._), channel_id=1, source_target_pairs={{0,8},{4,12},{1,9},{5,13},{2,10},{6,14},{3,11},{7,15}} | collective-permute-start | bytes 417800 | tf_op jit(solution)/shard_map/ppermute | solution.py:307
  9.8 5.8 %collective-permute-start.6 = (f32[136,256]{1,0:T(8,128)S(1)}, f32[136,256]{1,0:T(8,128)S(1)}, u32[]{:S(2)}, u32[]{:S(2)}) collective-permute-start(f32[136,256]{1,0:T(8,128)S(1)} %shard_map.59._), channel_id=1, source_target_pairs={{8,16},{12,20},{9,17},{13,21},{10,18},{14,22},{11,19},{15,23}} | collective-permute-start | bytes 417800 | tf_op jit(solution)/shard_map/ppermute | solution.py:307
  11.1 7.0 %collective-permute-start.7 = (f32[128,256]{1,0:T(8,128)S(1)}, f32[128,256]{1,0:T(8,128)S(1)}, u32[]{:S(2)}, u32[]{:S(2)}) collective-permute-start(f32[128,256]{1,0:T(8,128)S(1)} %shard_map.60._), channel_id=1, source_target_pairs={{0,8},{4,12},{1,9},{5,13},{2,10},{6,14},{3,11},{7,15}} | collective-permute-start | bytes 393224 | tf_op jit(solution)/shard_map/ppermute | solution.py:307
  12.0 7.4 %collective-permute-start.8 = (f32[136,256]{1,0:T(8,128)S(1)}, f32[136,256]{1,0:T(8,128)S(1)}, u32[]{:S(2)}, u32[]{:S(2)}) collective-permute-start(f32[136,256]{1,0:T(8,128)S(1)} %shard_map.61._), channel_id=1, source_target_pairs={{8,16},{12,20},{9,17},{13,21},{10,18},{14,22},{11,19},{15,23}} | collective-permute-start | bytes 417800 | tf_op jit(solution)/shard_map/ppermute | solution.py:307
  13.4 7.3 %collective-permute-start.9 = (f32[128,256]{1,0:T(8,128)S(1)}, f32[128,256]{1,0:T(8,128)S(1)}, u32[]{:S(2)}, u32[]{:S(2)}) collective-permute-start(f32[128,256]{1,0:T(8,128)S(1)} %shard_map.62._), channel_id=1, source_target_pairs={{0,8},{4,12},{1,9},{5,13},{2,10},{6,14},{3,11},{7,15}} | collective-permute-start | bytes 393224 | tf_op jit(solution)/shard_map/ppermute | solution.py:307
  14.2 8.2 %collective-permute-start.10 = (f32[136,256]{1,0:T(8,128)S(1)}, f32[136,256]{1,0:T(8,128)S(1)}, u32[]{:S(2)}, u32[]{:S(2)}) collective-permute-start(f32[136,256]{1,0:T(8,128)S(1)} %shard_map.63._), channel_id=1, source_target_pairs={{8,16},{12,20},{9,17},{13,21},{10,18},{14,22},{11,19},{15,23}} | collective-permute-start | bytes 417800 | tf_op jit(solution)/shard_map/ppermute | solution.py:307
  15.6 8.1 %collective-permute-start.11 = (f32[136,256]{1,0:T(8,128)S(1)}, f32[136,256]{1,0:T(8,128)S(1)}, u32[]{:S(2)}, u32[]{:S(2)}) collective-permute-start(f32[136,256]{1,0:T(8,128)S(1)} %shard_map.64._), channel_id=1, source_target_pairs={{16,24},{20,28},{17,25},{21,29},{18,26},{22,30},{19,27},{23,31}} | collective-permute-start | bytes 417800 | tf_op jit(solution)/shard_map/ppermute | solution.py:307
  18.1 6.8 %collective-permute-start.12 = (f32[128,256]{1,0:T(8,128)S(1)}, f32[128,256]{1,0:T(8,128)S(1)}, u32[]{:S(2)}, u32[]{:S(2)}) collective-permute-start(f32[128,256]{1,0:T(8,128)S(1)} %shard_map.65._), channel_id=1, source_target_pairs={{8,16},{12,20},{9,17},{13,21},{10,18},{14,22},{11,19},{15,23}} | collective-permute-start | bytes 393224 | tf_op jit(solution)/shard_map/ppermute | solution.py:307
  19.5 6.8 %collective-permute-start.13 = (f32[136,256]{1,0:T(8,128)S(1)}, f32[136,256]{1,0:T(8,128)S(1)}, u32[]{:S(2)}, u32[]{:S(2)}) collective-permute-start(f32[136,256]{1,0:T(8,128)S(1)} %shard_map.66._), channel_id=1, source_target_pairs={{16,24},{20,28},{17,25},{21,29},{18,26},{22,30},{19,27},{23,31}} | collective-permute-start | bytes 417800 | tf_op jit(solution)/shard_map/ppermute | solution.py:307
  20.8 7.4 %collective-permute-start.14 = (f32[128,256]{1,0:T(8,128)S(1)}, f32[128,256]{1,0:T(8,128)S(1)}, u32[]{:S(2)}, u32[]{:S(2)}) collective-permute-start(f32[128,256]{1,0:T(8,128)S(1)} %shard_map.67._), channel_id=1, source_target_pairs={{8,16},{12,20},{9,17},{13,21},{10,18},{14,22},{11,19},{15,23}} | collective-permute-start | bytes 393224 | tf_op jit(solution)/shard_map/ppermute | solution.py:307
  22.4 7.2 %collective-permute-start.15 = (f32[136,256]{1,0:T(8,128)S(1)}, f32[136,256]{1,0:T(8,128)S(1)}, u32[]{:S(2)}, u32[]{:S(2)}) collective-permute-start(f32[136,256]{1,0:T(8,128)S(1)} %shard_map.68._), channel_id=1, source_target_pairs={{16,24},{20,28},{17,25},{21,29},{18,26},{22,30},{19,27},{23,31}} | collective-permute-start | bytes 417800 | tf_op jit(solution)/shard_map/ppermute | solution.py:307
  23.8 10.5 %collective-permute-start.18 = (f32[136,256]{1,0:T(8,128)S(1)}, f32[136,256]{1,0:T(8,128)S(1)}, u32[]{:S(2)}, u32[]{:S(2)}) collective-permute-start(f32[136,256]{1,0:T(8,128)S(1)} %get-tuple-element.69._), channel_id=1, source_target_pairs={{0,4},{4,0},{8,12},{12,8},{16,20},{20,16},{24,28},{28,24},{1,5},{5... | collective-permute-start | bytes 417800 | tf_op jit(solution)/shard_map/ppermute | solution.py:323
  25.0 4.9 %collective-permute-start.16 = (f32[128,256]{1,0:T(8,128)S(1)}, f32[128,256]{1,0:T(8,128)S(1)}, u32[]{:S(2)}, u32[]{:S(2)}) collective-permute-start(f32[128,256]{1,0:T(8,128)S(1)} %shard_map.70._), channel_id=1, source_target_pairs={{16,24},{20,28},{17,25},{21,29},{18,26},{22,30},{19,27},{23,31}} | collective-permute-start | bytes 393224 | tf_op jit(solution)/shard_map/ppermute | solution.py:307
  26.4 7.9 %collective-permute-start.19 = (f32[136,256]{1,0:T(8,128)S(1)}, f32[136,256]{1,0:T(8,128)S(1)}, u32[]{:S(2)}, u32[]{:S(2)}) collective-permute-start(f32[136,256]{1,0:T(8,128)S(1)} %get-tuple-element.70._), channel_id=1, source_target_pairs={{0,4},{4,0},{8,12},{12,8},{16,20},{20,16},{24,28},{28,24},{1,5},{5... | collective-permute-start | bytes 417800 | tf_op jit(solution)/shard_map/ppermute | solution.py:323
  28.3 3.5 %collective-permute-start.17 = (f32[128,256]{1,0:T(8,128)S(1)}, f32[128,256]{1,0:T(8,128)S(1)}, u32[]{:S(2)}, u32[]{:S(2)}) collective-permute-start(f32[128,256]{1,0:T(8,128)S(1)} %shard_map.72._), channel_id=1, source_target_pairs={{16,24},{20,28},{17,25},{21,29},{18,26},{22,30},{19,27},{23,31}} | collective-permute-start | bytes 393224 | tf_op jit(solution)/shard_map/ppermute | solution.py:307
  29.7 7.1 %collective-permute-start.20 = (f32[136,256]{1,0:T(8,128)S(1)}, f32[136,256]{1,0:T(8,128)S(1)}, u32[]{:S(2)}, u32[]{:S(2)}) collective-permute-start(f32[136,256]{1,0:T(8,128)S(1)} %get-tuple-element.71._), channel_id=1, source_target_pairs={{0,4},{4,0},{8,12},{12,8},{16,20},{20,16},{24,28},{28,24},{1,5},{5... | collective-permute-start | bytes 417800 | tf_op jit(solution)/shard_map/ppermute | solution.py:323
  29.9 6.9 %collective-permute-start.21 = (f32[128,256]{1,0:T(8,128)S(1)}, f32[128,256]{1,0:T(8,128)S(1)}, u32[]{:S(2)}, u32[]{:S(2)}) collective-permute-start(f32[128,256]{1,0:T(8,128)S(1)} %get-tuple-element.72._), channel_id=1, source_target_pairs={{0,4},{4,0},{8,12},{12,8},{16,20},{20,16},{24,28},{28,24},{1,5},{5... | collective-permute-start | bytes 393224 | tf_op jit(solution)/shard_map/ppermute | solution.py:323
  31.9 7.5 %collective-permute-start.22 = (f32[128,256]{1,0:T(8,128)S(1)}, f32[128,256]{1,0:T(8,128)S(1)}, u32[]{:S(2)}, u32[]{:S(2)}) collective-permute-start(f32[128,256]{1,0:T(8,128)S(1)} %get-tuple-element.73._), channel_id=1, source_target_pairs={{0,4},{4,0},{8,12},{12,8},{16,20},{20,16},{24,28},{28,24},{1,5},{5... | collective-permute-start | bytes 393224 | tf_op jit(solution)/shard_map/ppermute | solution.py:323
  39.8 5.3 %collective-permute-start.25 = (f32[8,256]{1,0:T(8,128)S(1)}, f32[8,256]{1,0:T(8,128)S(1)}, u32[]{:S(2)}, u32[]{:S(2)}) collective-permute-start(f32[8,256]{1,0:T(8,128)S(1)} %get-tuple-element.114.refs_8_), channel_id=1, source_target_pairs={{0,1},{1,0},{2,3},{3,2},{4,5},{5,4},{6,7},{7,6},{8,9},{9,8},{10,11... | collective-permute-start | bytes 24584 | tf_op jit(solution)/shard_map/ppermute | solution.py:391
  43.4 2.5 %collective-permute-start.24 = (f32[8,256]{1,0:T(8,128)S(1)}, f32[8,256]{1,0:T(8,128)S(1)}, u32[]{:S(2)}, u32[]{:S(2)}) collective-permute-start(f32[8,256]{1,0:T(8,128)S(1)} %get-tuple-element.114.refs_8_), channel_id=1, source_target_pairs={{0,2},{1,3},{2,0},{3,1},{4,6},{5,7},{6,4},{7,5},{8,10},{9,11},{10,... | collective-permute-start | bytes 24584 | tf_op jit(solution)/shard_map/ppermute | solution.py:391
  44.6 3.1 %collective-permute-start.23 = (f32[8,256]{1,0:T(8,128)S(1)}, f32[8,256]{1,0:T(8,128)S(1)}, u32[]{:S(2)}, u32[]{:S(2)}) collective-permute-start(f32[8,256]{1,0:T(8,128)S(1)} %get-tuple-element.114.refs_8_), channel_id=1, source_target_pairs={{0,3},{1,2},{2,1},{3,0},{4,7},{5,6},{6,5},{7,4},{8,11},{9,10},{10,... | collective-permute-start | bytes 24584 | tf_op jit(solution)/shard_map/ppermute | solution.py:391
  (1 other events, 0.9 us)
